TPU v7x, 1024 devices: a whole 4x4x32 slice. The times are simulated.
1024 devices in a mesh: dp: 64 (over y, z_lo), replica: 16 (over z_hi, x, core).
Axes of the slice: x: 4, y: 4, z: 32 (z_hi: 2, z_lo: 16; z = z_hi * 16 + z_lo), core: 2. Of those that a mesh axis runs over, the one named last changes fastest.
Arguments:
- tokens: bfloat16 [16384, 8, 1152], P(('dp', 'replica')), may hold values from -6 to 6
- token_count: int32 [16384], P(('dp', 'replica')), may hold values from 1 to 8
- image_embed: bfloat16 [16384, 1152], P(('dp', 'replica')), may hold values from -6 to 6
- norm_gain: float32 [1152], replicated, may hold values from 0.25 to 1.75
- head_weight: bfloat16 [1152, 1152], replicated, may hold values from -0.1875 to 0.1875
- head_bias: float32 [1152], replicated, may hold values from -3 to 3
- logit_scale: float32 [1], replicated, may hold values from 1.6 to 2.4
- logit_bias: float32 [1], replicated, may hold values from -8 to -4
Outputs:
- grad_weight: float32 [64, 1152, 1152], P('dp', 'replica')
All inputs are finite; a program needn't handle non-finite values.
Results may differ from a plain program's by a relative error of at most 0.019.
Values may be sent and summed in bfloat16 or wider, within the bound.
No kernel may reach another device: no remote copies, remote signals or barrier semaphores. Data moves between devices by JAX's collectives and lax.ppermute only.
A program may use at most 32 MiB of HBM per device.

v0:
```python
import jax
import jax.numpy as jnp
from jax import lax
from jax.sharding import PartitionSpec as P


def gelu_parts(pre):
    coeff = 0.7978845608
    inner = coeff * (pre + 0.044715 * pre * pre * pre)
    hyper = jnp.tanh(inner)
    act = 0.5 * pre * (1.0 + hyper)
    slope = 0.5 * (1.0 + hyper) + 0.5 * pre * (1.0 - hyper * hyper) * coeff * (
        1.0 + 3.0 * 0.044715 * pre * pre
    )
    return (act, slope)


def layer_front(tokens, norm_gain, head_weight, head_bias):
    values = tokens.astype(jnp.float32)
    center = jnp.mean(values, axis=-1, keepdims=True)
    spread = jnp.mean((values - center) ** 2, axis=-1, keepdims=True)
    normed = ((values - center) * lax.rsqrt(spread + 1e-06) * norm_gain).astype(jnp.bfloat16)
    pre = (
        jnp.einsum("abtd,de->abte", normed, head_weight, preferred_element_type=jnp.float32)
        + head_bias
    )
    return (normed, pre)


def live_scale(counts, length):
    keep = (jnp.arange(length, dtype=jnp.int32) < counts[..., None]).astype(jnp.float32)
    return keep / jnp.maximum(counts, 1).astype(jnp.float32)[..., None]


def on_device(
    tokens, token_count, image_embed, norm_gain, head_weight, head_bias, logit_scale, logit_bias
):
    rows, length, width = tokens.shape
    helpers = lax.axis_size("replica")
    cap = max(2, (2 * rows + helpers - 1) // helpers)
    pair_index = jnp.arange(rows, dtype=jnp.int32)
    target = (pair_index + lax.axis_index("replica")) % helpers
    position = target * cap + pair_index // helpers
    outgoing = jnp.zeros((helpers * cap, length, width), jnp.bfloat16).at[position].set(tokens)
    outgoing = outgoing.reshape(helpers, cap, length, width)
    counts_out = (
        jnp.zeros((helpers * cap,), jnp.int32).at[position].set(token_count).reshape(helpers, cap)
    )
    received = lax.all_to_all(outgoing, "replica", split_axis=0, concat_axis=0, tiled=True)
    counts = lax.all_to_all(counts_out, "replica", split_axis=0, concat_axis=0, tiled=True)
    normed, pre = layer_front(received, norm_gain, head_weight, head_bias)
    act, slope = gelu_parts(pre)
    summed = jnp.sum(act * live_scale(counts, length)[..., None], axis=2)
    returned = lax.all_to_all(
        summed.astype(jnp.bfloat16), "replica", split_axis=0, concat_axis=0, tiled=True
    ).astype(summed.dtype)
    results = (returned, received, counts)
    pooled = results[0].reshape(helpers * cap, width)[position]
    size = jnp.sqrt(jnp.sum(pooled * pooled, axis=-1, keepdims=True) + 1e-06)
    unit32 = pooled / size
    unit = unit32.astype(jnp.bfloat16)
    images = image_embed.astype(jnp.float32)
    image = (images / jnp.sqrt(jnp.sum(images * images, axis=-1, keepdims=True) + 1e-06)).astype(
        jnp.bfloat16
    )
    temper = jnp.exp(logit_scale[0])
    group = rows * lax.axis_size("dp")
    my_rows = lax.axis_index("dp") * rows + jnp.arange(rows, dtype=jnp.int32)
    piece = lax.all_gather(image, "dp", axis=0, tiled=True)
    cosine = jnp.dot(unit, piece.T, preferred_element_type=jnp.float32)
    logit = temper * cosine + logit_bias[0]
    column = jnp.arange(piece.shape[0], dtype=jnp.int32)
    label = jnp.where(my_rows[:, None] == column[None, :], 1.0, -1.0)
    dlogit = (-label / (1.0 + jnp.exp(label * logit)) / group).astype(jnp.bfloat16)
    dunit = temper * jnp.dot(dlogit, piece, preferred_element_type=jnp.float32)
    dpooled = (dunit - unit32 * jnp.sum(unit32 * dunit, axis=-1, keepdims=True)) / size
    back = (
        jnp.zeros((helpers * cap, width), jnp.float32)
        .at[position]
        .set(dpooled)
        .reshape(helpers, cap, width)
    )
    arriving = lax.all_to_all(back, "replica", split_axis=0, concat_axis=0, tiled=True)
    counts = results[2]
    normed, pre = layer_front(results[1], norm_gain, head_weight, head_bias)
    act, slope = gelu_parts(pre)
    dpre = (arriving[:, :, None, :] * live_scale(counts, length)[..., None] * slope).astype(
        jnp.bfloat16
    )
    normed_flat = normed.reshape(-1, width)
    dpre_flat = dpre.reshape(-1, width)
    part = lax.dot_general(
        normed_flat, dpre_flat, (((0,), (0,)), ((), ())), preferred_element_type=jnp.float32
    )
    grad = lax.psum_scatter(
        part.astype(jnp.bfloat16), "replica", scatter_dimension=0, tiled=True
    ).astype(jnp.float32)
    return grad[None]


def solution(mesh):
    in_specs = (
        P(("dp", "replica"), None, None),
        P(("dp", "replica")),
        P(("dp", "replica"), None),
        P(),
        P(),
        P(),
        P(),
        P(),
    )
    out_specs = P("dp", "replica", None)
    return jax.shard_map(
        on_device, mesh=mesh, in_specs=in_specs, out_specs=out_specs, check_vma=False
    )
```

profile of v0, /device:TPU:1, one launch (start us, length us, event | category | flops | bytes accessed | tf_op | source)
XLA Modules:
  0.0 1057.3 jit_solution(17933422291580806873)
XLA Ops:
  6.6 0.9 scatter_custom_fusion.1
  7.5 0.7 all_to_all.16
  8.1 32.3 %all-to-all-start.1 = ((s32[16,1,2]{2,1,0:T(1,128)}), s32[16,1,2]{2,1,0:T(1,128)S(1)}, u32[]{:S(2)}, u32[]{:S(2)}) async-start(s32[16,1,2]{2,1,0:T(1,128)} %bitcast.5), calls=%async_computation.1 | async-start | bytes 16384 | tf_op jit(solution)/shard_map/all_to_all | solution.py:50
  40.5 2.0 scatter_fusion
  42.5 21.7 %all-to-all-done.1 = s32[16,1,2]{2,1,0:T(1,128)S(1)} async-done(((s32[16,1,2]{2,1,0:T(1,128)}), s32[16,1,2]{2,1,0:T(1,128)S(1)}, u32[]{:S(2)}, u32[]{:S(2)}) %all-to-all-start.1) | async-done | bytes 160 | tf_op jit(solution)/shard_map/all_to_all | solution.py:50
  64.2 4.2 all-to-all-start
  68.4 0.1 fusion.32
  68.6 0.7 fusion.33
  69.5 0.1 fusion.49
  69.7 29.2 %all-to-all-done = bf16[16,2,8,1152]{3,2,1,0:T(8,128)(2,1)S(1)} async-done(((bf16[16,2,8,1152]{3,2,1,0:T(8,128)(2,1)}), bf16[16,2,8,1152]{3,2,1,0:T(8,128)(2,1)S(1)}, u32[]{:S(2)}, u32[]{:S(2)}) %all-to-all-start) | async-done | bytes 589856 | tf_op jit(solution)/shard_map/all_to_all | solution.py:49
  98.8 0.2 convert_reduce_fusion
  99.0 0.3 fusion.4
  99.4 3.0 multiply_reduce_fusion
  102.4 4.0 all-to-all-start.2
  107.9 26.4 %all-to-all-done.2 = bf16[16,2,1152]{2,1,0:T(2,128)(2,1)S(1)} async-done(((bf16[16,2,1152]{2,1,0:T(2,128)(2,1)}), bf16[16,2,1152]{2,1,0:T(2,128)(2,1)S(1)}, u32[]{:S(2)}, u32[]{:S(2)}) %all-to-all-start.2) | async-done | bytes 73760 | tf_op jit(solution)/shard_map/all_to_all | solution.py:54
  134.3 0.6 gather_fusion
  134.9 0.1 multiply_reduce_fusion.2
  135.1 633.3 %all-gather.2.cloned.1.call-done = bf16[1024,1152]{1,0:T(8,128)(2,1)} async-done(((bf16[16,1152]{1,0:T(8,128)(2,1)}), bf16[1024,1152]{1,0:T(8,128)(2,1)}) %all-gather.2.cloned.1.call-update) | async-done | bytes 2359312 | tf_op jit(solution)/shard_map/all_gather | solution.py:69
  768.3 4.1 multiply_reduce_fusion.1
  772.4 1.0 scatter_custom_fusion.2
  773.5 74.2 %all_to_all.24 = f32[16,2,1152]{2,1,0:T(2,128)S(1)} all-to-all(f32[16,2,1152]{2,1,0:T(2,128)S(1)} %reshape.155), channel_id=1, replica_groups=mesh['dp'=64,'replica'=16] {'replica'}, dimensions={0} | all-to-all | bytes 294912 | tf_op jit(solution)/shard_map/all_to_all | solution.py:83
  847.8 4.4 fusion
  852.2 196.6 %reduce-scatter.4.cloned.1.call-done = bf16[72,1152]{1,0:T(8,128)(2,1)} async-done(((bf16[1152,1152]{1,0:T(8,128)(2,1)}), bf16[72,1152]{1,0:T(8,128)(2,1)}) %reduce-scatter.4.cloned.1.call-update) | async-done | bytes 165904
  1048.8 1.7 bitcast_convert_fusion
  (36 shorter events, 0.6 us)
Async XLA Ops:
  6.5 92.8 %copy-start = (bf16[1152,1152]{1,0:T(8,128)(2,1)S(1)}, bf16[1152,1152]{1,0:T(8,128)(2,1)}, u32[]{:S(2)}) copy-start(bf16[1152,1152]{1,0:T(8,128)(2,1)} %param.12) | copy-start | bytes 7962628
  6.6 101.3 %copy-start.6 = (s32[16]{0:T(128)}, s32[16]{0:T(128)S(1)}, u32[]{:S(2)}) copy-start(s32[16]{0:T(128)S(1)} %fusion.53) | copy-start | bytes 196
  8.1 56.1 %all-to-all-start.1 = ((s32[16,1,2]{2,1,0:T(1,128)}), s32[16,1,2]{2,1,0:T(1,128)S(1)}, u32[]{:S(2)}, u32[]{:S(2)}) async-start(s32[16,1,2]{2,1,0:T(1,128)} %bitcast.5), calls=%async_computation.1 | async-start | bytes 16384 | tf_op jit(solution)/shard_map/all_to_all | solution.py:50
  40.5 27.9 %copy-start.2 = (bf16[16,1152]{1,0:T(8,128)(2,1)S(1)}, bf16[16,1152]{1,0:T(8,128)(2,1)}, u32[]{:S(2)}) copy-start(bf16[16,1152]{1,0:T(8,128)(2,1)} %param.10) | copy-start | bytes 110596
  42.5 21.7 %copy-start.1 = (bf16[32,8,1152]{2,1,0:T(8,128)(2,1)}, bf16[32,8,1152]{2,1,0:T(8,128)(2,1)S(1)}, u32[]{:S(2)}) copy-start(bf16[32,8,1152]{2,1,0:T(8,128)(2,1)S(1)} %scatter_fusion) | copy-start | bytes 1769476
  64.2 35.2 %copy-start.7 = (f32[1152]{0:T(1024)S(1)}, f32[1152]{0:T(1024)}, u32[]{:S(2)}) copy-start(f32[1152]{0:T(1024)} %param.13) | copy-start | bytes 13828
  64.2 35.2 %copy-start.8 = (f32[1152]{0:T(1024)S(1)}, f32[1152]{0:T(1024)}, u32[]{:S(2)}) copy-start(f32[1152]{0:T(1024)} %param.11) | copy-start | bytes 13828
  64.2 34.6 %all-to-all-start = ((bf16[16,2,8,1152]{3,2,1,0:T(8,128)(2,1)}), bf16[16,2,8,1152]{3,2,1,0:T(8,128)(2,1)S(1)}, u32[]{:S(2)}, u32[]{:S(2)}) async-start(bf16[16,2,8,1152]{3,2,1,0:T(8,128)(2,1)} %bitcast.31), calls=%async_computation | async-start | bytes 1179648 | tf_op jit(solution)/shard_map/all_to_all | solution.py:49
  68.4 700.0 %all-gather.2.cloned.1.call-start = ((), (), s32[]{:S(2)}) async-start(), calls=%async_computation.5 | async-start | bytes 2396160 | tf_op jit(solution)/shard_map/all_gather | solution.py:69
  69.7 32.8 %copy-start.3 = (f32[16,2,8]{2,1,0:T(2,128)}, f32[16,2,8]{2,1,0:T(2,128)S(1)}, u32[]{:S(2)}) copy-start(f32[16,2,8]{2,1,0:T(2,128)S(1)} %fusion.49) | copy-start | bytes 3076
  99.4 3.0 copy-start.4
  102.4 31.9 %all-to-all-start.2 = ((bf16[16,2,1152]{2,1,0:T(2,128)(2,1)}), bf16[16,2,1152]{2,1,0:T(2,128)(2,1)S(1)}, u32[]{:S(2)}, u32[]{:S(2)}) async-start(bf16[16,2,1152]{2,1,0:T(2,128)(2,1)} %get-tuple-element.5), calls=%async_computation.2 | async-start | bytes 147456 | tf_op jit(solution)/shard_map/all_to_all | solution.py:54
  106.5 942.3 %reduce-scatter.4.cloned.1.call-start = ((), (), s32[]{:S(2)}) async-start(), calls=%async_computation.6 | async-start | bytes 2820096
  135.1 637.4 %copy-start.5 = (f32[16]{0:T(128)}, f32[16]{0:T(128)S(1)}, u32[]{:S(2)}) copy-start(f32[16]{0:T(128)S(1)} %add_sqrt_fusion.1) | copy-start | bytes 196
Sparse Core Ops, SparseCore 0:
  71.9 696.4 all-gather.1
  852.3 196.4 reduce-scatter.3
where the time goes:
time: 1060 us
  waiting for transfers between devices  907 us (86%)
  blocking collectives  74.2 us (7%)
  starting transfers between devices  40.6 us (4%)
  between operations  14.9 us (1%)
  matrix products  11.5 us (1%)
    all_gather x1, waiting for transfers between devices, on_device(): piece = lax.all_gather(image, 'dp', axis=0, tiled=True)  633 us
    unnamed x3, waiting for transfers between devices  197 us
    all_to_all x1, blocking collectives, on_device(): lax.all_to_all(back, 'replica', split_axis=0, concat_axis=0, tiled=True)  74.2 us
    all_to_all x1, starting transfers between devices, on_device(): lax.all_to_all(counts_out, 'replica', split_axis=0, concat_axis=0, tiled=...  32.3 us
    all_to_all x1, waiting for transfers between devices, on_device(): lax.all_to_all(outgoing, 'replica', split_axis=0, concat_axis=0, tiled=True)  29.2 us
    all_to_all x1, waiting for transfers between devices, on_device(): lax.all_to_all(summed.astype(jnp.bfloat16), 'replica', split_axis=0, conc...  26.4 us
    all_to_all x1, waiting for transfers between devices, on_device(): lax.all_to_all(counts_out, 'replica', split_axis=0, concat_axis=0, tiled=...  21.7 us
  transfers between devices with their start and end apart: 5, of which 5 were waited for; matrix products, arithmetic and copies ran while one was open for 1% of the time, Pallas kernels for 0%

commit v1 on v0

v1 whole, which is shorter than its diff:
```python
import jax
import jax.numpy as jnp
from jax import lax
from jax.sharding import Mesh, PartitionSpec as P

AXES = ("y", "za", "zb", "zh", "x", "c")
SIZES = (4, 4, 4, 2, 4, 2)


def gelu_terms(pre):
    coeff = 0.7978845608
    inner = coeff * (pre + 0.044715 * pre * pre * pre)
    return coeff, jnp.tanh(inner)


def gelu(pre):
    _, hyper = gelu_terms(pre)
    return 0.5 * pre * (1.0 + hyper)


def gelu_slope(pre):
    coeff, hyper = gelu_terms(pre)
    return 0.5 * (1.0 + hyper) + 0.5 * pre * (1.0 - hyper * hyper) * coeff * (
        1.0 + 3.0 * 0.044715 * pre * pre
    )


def spread_to(value, axes, count):
    copies = jnp.broadcast_to(value[None], (count,) + value.shape)
    return lax.all_to_all(copies, axes, split_axis=0, concat_axis=0, tiled=True)


def on_device(
    tokens, token_count, image_embed, norm_gain, head_weight, head_bias, logit_scale, logit_bias
):
    rows, length, width = tokens.shape
    part = width // 16
    group = 64 * rows
    my = {name: lax.axis_index(name) for name in AXES}

    images = image_embed.astype(jnp.float32)
    image = (images / jnp.sqrt(jnp.sum(images * images, axis=-1, keepdims=True) + 1e-06)).astype(
        jnp.bfloat16
    )
    some_images = spread_to(image, "za", 4).reshape(4 * rows, width)

    values = tokens.reshape(rows * length, width).astype(jnp.float32)
    center = jnp.mean(values, axis=-1, keepdims=True)
    spread = jnp.mean((values - center) ** 2, axis=-1, keepdims=True)
    normed = ((values - center) * lax.rsqrt(spread + 1e-06) * norm_gain).astype(jnp.bfloat16)
    live = jnp.arange(length, dtype=jnp.int32) < token_count[:, None]
    live_flat = live.reshape(rows * length, 1)
    masked = jnp.where(live_flat, normed, 0)

    by_x = spread_to(masked, "x", 4)
    other = lax.ppermute(by_x, "c", [(0, 1), (1, 0)])

    pre = jnp.dot(normed, head_weight, preferred_element_type=jnp.float32) + head_bias
    per_count = 1.0 / token_count.astype(jnp.float32)[:, None]
    scale = live.astype(jnp.float32) * per_count
    pooled = jnp.sum(gelu(pre).reshape(rows, length, width) * scale[:, :, None], axis=1)
    size = jnp.sqrt(jnp.sum(pooled * pooled, axis=-1, keepdims=True) + 1e-06)
    unit32 = pooled / size
    unit = unit32.astype(jnp.bfloat16)
    units = spread_to(unit, ("y", "zb"), 16).reshape(16 * rows, width)

    temper = jnp.exp(logit_scale[0])
    cosine = jnp.dot(units, some_images.T, preferred_element_type=jnp.float32)
    logit = temper * cosine + logit_bias[0]
    unit_at = lax.broadcasted_iota(jnp.int32, cosine.shape, 0)
    image_at = lax.broadcasted_iota(jnp.int32, cosine.shape, 1)
    same = (unit_at - (my["y"] * 4 + my["zb"]) * rows) == (image_at - my["za"] * rows)
    mine = (unit_at // rows) == (my["y"] * 4 + my["zb"])
    label = jnp.where(same & mine, 1.0, -1.0)
    dlogit = (-label / (1.0 + jnp.exp(label * logit)) / group).astype(jnp.bfloat16)
    terms = jnp.dot(dlogit, some_images, preferred_element_type=jnp.float32).astype(jnp.bfloat16)
    terms = lax.all_to_all(
        terms.reshape(16, rows, width), ("y", "zb"), split_axis=0, concat_axis=0, tiled=True
    )
    dunit = temper * jnp.sum(terms.astype(jnp.float32), axis=0)
    dpooled = (dunit - unit32 * jnp.sum(unit32 * dunit, axis=-1, keepdims=True)) / size
    share = (dpooled * per_count).astype(jnp.bfloat16)
    shares = spread_to(share, ("x", "c"), 8)

    first = my["c"] == 0
    halves = jnp.stack(
        [jnp.where(first, by_x, other), jnp.where(first, other, by_x)], axis=1
    ).reshape(8 * rows * length, width)
    slope = gelu_slope(
        jnp.dot(halves, head_weight, preferred_element_type=jnp.float32) + head_bias
    ).astype(jnp.bfloat16)
    here = my["x"] * 2 + my["c"]
    wanted = lax.broadcasted_iota(jnp.int32, (width, 2 * part), 1)
    source = lax.broadcasted_iota(jnp.int32, (width, 2 * part), 0)
    half_of = wanted // part
    zh_of = jnp.where(half_of == 0, my["zh"], 1 - my["zh"])
    pick = (source == (zh_of * 8 + here) * part + wanted % part).astype(jnp.bfloat16)
    columns = jnp.dot(halves, pick, preferred_element_type=jnp.float32).astype(jnp.bfloat16)
    slope, columns = lax.optimization_barrier((slope, columns))

    dpre = (
        shares.reshape(8 * rows, 1, width).astype(jnp.float32)
        * slope.reshape(8 * rows, length, width).astype(jnp.float32)
    ).astype(jnp.bfloat16)
    both = lax.dot_general(
        columns,
        dpre.reshape(8 * rows * length, width),
        (((0,), (0,)), ((), ())),
        preferred_element_type=jnp.float32,
    )
    away = lax.ppermute(both[part:].astype(jnp.bfloat16), "zh", [(0, 1), (1, 0)])
    return (both[:part] + away.astype(jnp.float32))[None]


def solution(mesh):
    fine = Mesh(mesh.devices.reshape(SIZES), AXES)
    everyone = AXES
    in_specs = (
        P(everyone, None, None),
        P(everyone),
        P(everyone, None),
        P(),
        P(),
        P(),
        P(),
        P(),
    )
    out_specs = P(("y", "za", "zb"), ("zh", "x", "c"), None)
    return jax.shard_map(
        on_device, mesh=fine, in_specs=in_specs, out_specs=out_specs, check_vma=False
    )
```

time: 1060 us -> 165 us (0.16)
  the two profiles are of different devices: /device:TPU:1 before, /device:TPU:961 now
where the time goes in v1:
time: 165 us; the launch traced here: 164 us
  waiting for transfers between devices  78.2 us (47%)
  starting transfers between devices  53.9 us (33%)
  matrix products  15.5 us (9%)
  other arithmetic  9.47 us (6%)
  local copies, waits for them, and re-layouts  5.13 us (3%)
    ppermute x1, waiting for transfers between devices, on_device(): lax.ppermute(both[part:].astype(jnp.bfloat16), 'zh', [(0, 1), (1, 0)])  38.3 us
    all_to_all x4, waiting for transfers between devices, spread_to(): return lax.all_to_all(copies, axes, split_axis=0, concat_axis=0, tiled=True)  37.1 us
    all_to_all x4, starting transfers between devices, spread_to(): return lax.all_to_all(copies, axes, split_axis=0, concat_axis=0, tiled=True)  32.3 us
    ppermute x1, starting transfers between devices, on_device(): lax.ppermute(both[part:].astype(jnp.bfloat16), 'zh', [(0, 1), (1, 0)])  11.1 us
    all_to_all x1, starting transfers between devices, on_device(): lax.all_to_all(terms.reshape(16, rows, width), ('y', 'zb'), split_axis=0,...  6.41 us
    dot_general x1, matrix products, on_device(): jnp.dot(halves, head_weight, preferred_element_type=jnp.float32) + head_bias  6.01 us
    ppermute x1, starting transfers between devices, on_device(): other = lax.ppermute(by_x, 'c', [(0, 1), (1, 0)])  4.05 us
    broadcast_in_dim x4, local copies, waits for them, and re-layouts, spread_to(): copies = jnp.broadcast_to(value[None], (count,) + value.shape)  3.41 us
  transfers between devices with their start and end apart: 7, of which 6 were waited for; matrix products, arithmetic and copies ran while one was open for 12% of the time, Pallas kernels for 0%

profile of v1, /device:TPU:961, one launch (start us, length us, event | category | flops | bytes accessed | tf_op | source)
XLA Modules:
  0.0 163.7 jit_solution(3519578480590527692)
XLA Ops:
  0.0 1.0 fusion.47
  2.6 16.3 %all-to-all-start.2 = ((bf16[4,16,1152]{2,1,0:T(8,128)(2,1)}), bf16[4,16,1152]{2,1,0:T(8,128)(2,1)S(1)}, u32[]{:S(2)}, u32[]{:S(2)}) async-start(bf16[4,16,1152]{2,1,0:T(8,128)(2,1)} %broadcast_in_dim.75), calls=%async_computation.2 | async-start | bytes 294912 | tf_op jit(solution)/shard_map/all_to_all | solution.py:30
  18.8 1.1 convert_reduce_fusion.1
  19.9 1.2 fusion.29
  22.7 1.8 %fusion.23 = f32[16,1152]{1,0:T(8,128)S(1)} fusion(bf16[1152,1152]{1,0:T(8,128)(2,1)S(1)} %copy-done, f32[16,8]{1,0:T(8,128)S(1)} %broadcast_select_fusion.1, f32[1152]{0:T(1024)} %param.13, bf16[16,8,1152]{2,1,0:T(8,128)(2,1)} %param.8, f32[1152]{0:T(1024)} %param.11, f32[128]{0:T(128)S(1)} %rsqrt.12, f32[128]{0:T(128)S(1)} %div.71), kind=kOutput, calls=%fused_computation.39 | convolution fusion | flops 342079488 | bytes 3033600 | tf_op jit(solution)/shard_map/dot_general | solution.py:58
  24.8 6.8 %all-to-all-done.2 = bf16[4,16,1152]{2,1,0:T(8,128)(2,1)S(1)} async-done(((bf16[4,16,1152]{2,1,0:T(8,128)(2,1)}), bf16[4,16,1152]{2,1,0:T(8,128)(2,1)S(1)}, u32[]{:S(2)}, u32[]{:S(2)}) %all-to-all-start.2) | async-done | bytes 147488 | tf_op jit(solution)/shard_map/all_to_all | solution.py:30
  32.4 8.1 %all-to-all-start.1 = ((bf16[16,16,1152]{2,1,0:T(8,128)(2,1)}), bf16[16,16,1152]{2,1,0:T(8,128)(2,1)}, u32[]{:S(2)}, u32[]{:S(2)}) async-start(bf16[16,16,1152]{2,1,0:T(8,128)(2,1)} %broadcast_in_dim.74), calls=%async_computation.1 | async-start | bytes 1179648 | tf_op jit(solution)/shard_map/all_to_all | solution.py:30
  41.0 14.6 %all-to-all-done.1 = bf16[16,16,1152]{2,1,0:T(8,128)(2,1)} async-done(((bf16[16,16,1152]{2,1,0:T(8,128)(2,1)}), bf16[16,16,1152]{2,1,0:T(8,128)(2,1)}, u32[]{:S(2)}, u32[]{:S(2)}) %all-to-all-start.1) | async-done | bytes 589856 | tf_op jit(solution)/shard_map/all_to_all | solution.py:30
  55.6 1.1 broadcast_in_dim.38
  56.7 4.3 %all-to-all-start = ((bf16[4,128,1152]{2,1,0:T(8,128)(2,1)}), bf16[4,128,1152]{2,1,0:T(8,128)(2,1)}, u32[]{:S(2)}, u32[]{:S(2)}) async-start(bf16[4,128,1152]{2,1,0:T(8,128)(2,1)} %broadcast_in_dim.38), calls=%async_computation | async-start | bytes 2359296 | tf_op jit(solution)/shard_map/all_to_all | solution.py:30
  62.4 2.7 %convolution_convert_fusion = bf16[256,1152]{1,0:T(8,128)(2,1)} fusion(bf16[64,1152]{1,0:T(8,128)(2,1)S(1)} %bitcast.53, bf16[256,1152]{1,0:T(8,128)(2,1)} %bitcast.7, f32[]{:T(128)} %bitcast.49, f32[]{:T(128)} %bitcast.5, s32[]{:T(128)S(6)} %add.118, s32[256]{0:T(256)S(1)} %get-tuple-element.17, s32[256]{0:T(256)S(1)} %broadcast_add_fusion, ...), kind=kOutput, calls=%fused_computation.10 | convolution fusion | flops 76005376 | bytes 1330700 | tf_op jit(solution)/shard_map/dot_general | solution.py:76
  65.0 11.6 %all-to-all-done = bf16[4,128,1152]{2,1,0:T(8,128)(2,1)} async-done(((bf16[4,128,1152]{2,1,0:T(8,128)(2,1)}), bf16[4,128,1152]{2,1,0:T(8,128)(2,1)}, u32[]{:S(2)}, u32[]{:S(2)}) %all-to-all-start) | async-done | bytes 1179680 | tf_op jit(solution)/shard_map/all_to_all | solution.py:30
  76.6 6.4 %all-to-all-start.3 = ((bf16[16,16,1152]{2,1,0:T(8,128)(2,1)}), bf16[16,16,1152]{2,1,0:T(8,128)(2,1)S(1)}, u32[]{:S(2)}, u32[]{:S(2)}) async-start(bf16[16,16,1152]{2,1,0:T(8,128)(2,1)} %bitcast.52), calls=%async_computation.3 | async-start | bytes 1179648 | tf_op jit(solution)/shard_map/all_to_all | solution.py:77
  83.0 4.1 %collective-permute-start = (bf16[4,128,1152]{2,1,0:T(8,128)(2,1)}, bf16[4,128,1152]{2,1,0:T(8,128)(2,1)}, u32[]{:S(2)}, u32[]{:S(2)}) collective-permute-start(bf16[4,128,1152]{2,1,0:T(8,128)(2,1)} %all-to-all-done), channel_id=1, source_target_pairs={{0,1},{1,0},{2,3},{3,2},{4,5},{5,4},{6,7},{7,6},{8,9},{9,8},{10,11... | collective-permute-start | bytes 3538952 | tf_op jit(solution)/shard_map/ppermute | solution.py:56
  87.1 2.7 %collective-permute-done = bf16[4,128,1152]{2,1,0:T(8,128)(2,1)} collective-permute-done((bf16[4,128,1152]{2,1,0:T(8,128)(2,1)}, bf16[4,128,1152]{2,1,0:T(8,128)(2,1)}, u32[]{:S(2)}, u32[]{:S(2)}) %collective-permute-start) | collective-permute-done | bytes 1179680 | tf_op jit(solution)/shard_map/ppermute | solution.py:56
  89.9 1.8 %select_bitcast_fusion.1 = (bf16[4,1,128,1152]{3,2,1,0:T(8,128)(2,1)S(1)}, bf16[4,1,128,1152]{3,2,1,0:T(8,128)(2,1)S(1)}) fusion(bf16[4,128,1152]{2,1,0:T(8,128)(2,1)} %all-to-all-done, bf16[4,128,1152]{2,1,0:T(8,128)(2,1)} %collective-permute-done, pred[]{:T(512)S(6)} %eq.21), kind=kLoop, calls=%fused_computation.20 | loop fusion | flops 1179648 | bytes 4718593 | tf_op jit(solution)/shard_map/stack | solution.py:86
  92.0 1.4 copy-done.2
  93.4 6.0 %fusion.5 = bf16[1024,1152]{1,0:T(8,128)(2,1)} fusion(bf16[1024,1152]{1,0:T(8,128)(2,1)S(1)} %bitcast.50, bf16[1152,1152]{1,0:T(8,128)(2,1)S(1)} %copy-done, f32[1152]{0:T(1024)S(1)} %copy-done.5), kind=kOutput, calls=%fused_computation.7 | convolution fusion | flops 2740322304 | bytes 7377408 | tf_op jit(solution)/shard_map/dot_general | solution.py:90
  100.5 3.7 %all-to-all-start.4 = ((bf16[8,16,1152]{2,1,0:T(8,128)(2,1)}), bf16[8,16,1152]{2,1,0:T(8,128)(2,1)S(1)}, u32[]{:S(2)}, u32[]{:S(2)}) async-start(bf16[8,16,1152]{2,1,0:T(8,128)(2,1)} %broadcast_in_dim.76), calls=%async_computation.4 | async-start | bytes 589824 | tf_op jit(solution)/shard_map/all_to_all | solution.py:30
  104.2 2.6 %convolution_convert_fusion.1 = bf16[1024,144]{0,1:T(8,128)(2,1)S(1)} fusion(bf16[1024,1152]{1,0:T(8,128)(2,1)} %bitcast.51, s32[144]{0:T(256)S(1)} %get-tuple-element.12, s32[144]{0:T(256)S(1)} %get-tuple-element.15, s32[]{:T(128)S(6)} %add.113, s32[]{:T(128)S(6)} %sub.68, s32[]{:T(128)S(6)} %axis_index.65, s32[144]{0:T(256)S(1)} %get-tuple-element.11, ...), kind=kOutput, calls=%fused_computation.15 | convolution fusion | flops 341379072 | bytes 2656812 | tf_op jit(solution)/shard_map/dot_general | solution.py:98
  106.8 4.2 %all-to-all-done.4 = bf16[8,16,1152]{2,1,0:T(8,128)(2,1)S(1)} async-done(((bf16[8,16,1152]{2,1,0:T(8,128)(2,1)}), bf16[8,16,1152]{2,1,0:T(8,128)(2,1)S(1)}, u32[]{:S(2)}, u32[]{:S(2)}) %all-to-all-start.4) | async-done | bytes 294944 | tf_op jit(solution)/shard_map/all_to_all | solution.py:30
  111.1 2.4 %fusion.7 = f32[144,1152]{1,0:T(8,128)S(1)} fusion(bf16[1024,144]{0,1:T(8,128)(2,1)S(1)} %convolution_convert_fusion.1, bf16[1024,1152]{1,0:T(8,128)(2,1)} %fusion.5, f32[128,1152]{1,0:T(8,128)S(1)} %bitcast_convert_fusion), kind=kOutput, calls=%fused_computation.12 | convolution fusion | flops 343277568 | bytes 3907584 | tf_op jit(solution)/shard_map/dot_general | solution.py:105
  113.5 11.1 %collective-permute-start.1 = (bf16[72,1152]{1,0:T(8,128)(2,1)S(1)}, bf16[72,1152]{1,0:T(8,128)(2,1)S(1)}, u32[]{:S(2)}, u32[]{:S(2)}) collective-permute-start(bf16[72,1152]{1,0:T(8,128)(2,1)S(1)} %slice.15), channel_id=1, source_target_pairs={{0,8},{8,0},{1,9},{9,1},{2,10},{10,2},{3,11},{11,3},{4,12},{12,4},... | collective-permute-start | bytes 497672 | tf_op jit(solution)/shard_map/ppermute | solution.py:111
  124.7 38.3 %collective-permute-done.1 = bf16[72,1152]{1,0:T(8,128)(2,1)S(1)} collective-permute-done((bf16[72,1152]{1,0:T(8,128)(2,1)S(1)}, bf16[72,1152]{1,0:T(8,128)(2,1)S(1)}, u32[]{:S(2)}, u32[]{:S(2)}) %collective-permute-start.1) | collective-permute-done | bytes 165920 | tf_op jit(solution)/shard_map/ppermute | solution.py:111
  (43 shorter events, 6.9 us)
Async XLA Ops:
  0.0 22.7 %copy-start = (bf16[1152,1152]{1,0:T(8,128)(2,1)S(1)}, bf16[1152,1152]{1,0:T(8,128)(2,1)}, u32[]{:S(2)}) copy-start(bf16[1152,1152]{1,0:T(8,128)(2,1)} %param.12) | copy-start | bytes 7962628
  2.6 29.0 %all-to-all-start.2 = ((bf16[4,16,1152]{2,1,0:T(8,128)(2,1)}), bf16[4,16,1152]{2,1,0:T(8,128)(2,1)S(1)}, u32[]{:S(2)}, u32[]{:S(2)}) async-start(bf16[4,16,1152]{2,1,0:T(8,128)(2,1)} %broadcast_in_dim.75), calls=%async_computation.2 | async-start | bytes 294912 | tf_op jit(solution)/shard_map/all_to_all | solution.py:30
  22.7 17.8 %copy-start.4 = (s32[16]{0:T(128)S(1)}, s32[16]{0:T(128)}, u32[]{:S(2)}) copy-start(s32[16]{0:T(128)} %param.9) | copy-start | bytes 196
  22.7 18.0 %copy-start.1 = (bf16[16,8,1152]{2,1,0:T(8,128)(2,1)S(1)}, bf16[16,8,1152]{2,1,0:T(8,128)(2,1)}, u32[]{:S(2)}) copy-start(bf16[16,8,1152]{2,1,0:T(8,128)(2,1)} %param.8) | copy-start | bytes 884740
  22.7 18.0 %copy-start.3 = (f32[1152]{0:T(1024)S(1)}, f32[1152]{0:T(1024)}, u32[]{:S(2)}) copy-start(f32[1152]{0:T(1024)} %param.11) | copy-start | bytes 13828
  32.4 23.1 %all-to-all-start.1 = ((bf16[16,16,1152]{2,1,0:T(8,128)(2,1)}), bf16[16,16,1152]{2,1,0:T(8,128)(2,1)}, u32[]{:S(2)}, u32[]{:S(2)}) async-start(bf16[16,16,1152]{2,1,0:T(8,128)(2,1)} %broadcast_in_dim.74), calls=%async_computation.1 | async-start | bytes 1179648 | tf_op jit(solution)/shard_map/all_to_all | solution.py:30
  56.7 19.9 %all-to-all-start = ((bf16[4,128,1152]{2,1,0:T(8,128)(2,1)}), bf16[4,128,1152]{2,1,0:T(8,128)(2,1)}, u32[]{:S(2)}, u32[]{:S(2)}) async-start(bf16[4,128,1152]{2,1,0:T(8,128)(2,1)} %broadcast_in_dim.38), calls=%async_computation | async-start | bytes 2359296 | tf_op jit(solution)/shard_map/all_to_all | solution.py:30
  76.6 22.8 %all-to-all-start.3 = ((bf16[16,16,1152]{2,1,0:T(8,128)(2,1)}), bf16[16,16,1152]{2,1,0:T(8,128)(2,1)S(1)}, u32[]{:S(2)}, u32[]{:S(2)}) async-start(bf16[16,16,1152]{2,1,0:T(8,128)(2,1)} %bitcast.52), calls=%async_computation.3 | async-start | bytes 1179648 | tf_op jit(solution)/shard_map/all_to_all | solution.py:77
  83.0 6.9 %collective-permute-start = (bf16[4,128,1152]{2,1,0:T(8,128)(2,1)}, bf16[4,128,1152]{2,1,0:T(8,128)(2,1)}, u32[]{:S(2)}, u32[]{:S(2)}) collective-permute-start(bf16[4,128,1152]{2,1,0:T(8,128)(2,1)} %all-to-all-done), channel_id=1, source_target_pairs={{0,1},{1,0},{2,3},{3,2},{4,5},{5,4},{6,7},{7,6},{8,9},{9,8},{10,11... | collective-permute-start | bytes 3538952 | tf_op jit(solution)/shard_map/ppermute | solution.py:56
  91.7 1.7 %copy-start.5 = (f32[1152]{0:T(1024)S(1)}, f32[1152]{0:T(1024)}, u32[]{:S(2)}) copy-start(f32[1152]{0:T(1024)} %param.13) | copy-start | bytes 13828
  92.0 1.4 copy-start.2
  100.5 10.5 %all-to-all-start.4 = ((bf16[8,16,1152]{2,1,0:T(8,128)(2,1)}), bf16[8,16,1152]{2,1,0:T(8,128)(2,1)S(1)}, u32[]{:S(2)}, u32[]{:S(2)}) async-start(bf16[8,16,1152]{2,1,0:T(8,128)(2,1)} %broadcast_in_dim.76), calls=%async_computation.4 | async-start | bytes 589824 | tf_op jit(solution)/shard_map/all_to_all | solution.py:30
  113.5 49.4 %collective-permute-start.1 = (bf16[72,1152]{1,0:T(8,128)(2,1)S(1)}, bf16[72,1152]{1,0:T(8,128)(2,1)S(1)}, u32[]{:S(2)}, u32[]{:S(2)}) collective-permute-start(bf16[72,1152]{1,0:T(8,128)(2,1)S(1)} %slice.15), channel_id=1, source_target_pairs={{0,8},{8,0},{1,9},{9,1},{2,10},{10,2},{3,11},{11,3},{4,12},{12,4},... | collective-permute-start | bytes 497672 | tf_op jit(solution)/shard_map/ppermute | solution.py:111

commit v2 on v1

v2 whole, which is shorter than its diff:
```python
import jax
import jax.numpy as jnp
from jax import lax
from jax.sharding import Mesh, PartitionSpec as P

AXES = ("y", "za", "zb", "zh", "x", "c")
SIZES = (4, 4, 4, 2, 4, 2)


def size_of(*names):
    count = 1
    for name in names:
        count *= SIZES[AXES.index(name)]
    return count


def gelu_terms(pre):
    coeff = 0.7978845608
    inner = coeff * (pre + 0.044715 * pre * pre * pre)
    return coeff, jnp.tanh(inner)


def gelu(pre):
    _, hyper = gelu_terms(pre)
    return 0.5 * pre * (1.0 + hyper)


def gelu_slope(pre):
    coeff, hyper = gelu_terms(pre)
    return 0.5 * (1.0 + hyper) + 0.5 * pre * (1.0 - hyper * hyper) * coeff * (
        1.0 + 3.0 * 0.044715 * pre * pre
    )


def spread_to(value, *axes):
    copies = jnp.broadcast_to(value[None], (size_of(*axes),) + value.shape)
    return lax.all_to_all(copies, axes, split_axis=0, concat_axis=0, tiled=True)


def from_others(value, axis):
    count = size_of(axis)
    moved = [
        lax.ppermute(value, axis, [(i, (i + k) % count) for i in range(count)])
        for k in range(1, count)
    ]
    return [value] + moved


def on_device(
    tokens, token_count, image_embed, norm_gain, head_weight, head_bias, logit_scale, logit_bias
):
    rows, length, width = tokens.shape
    part = width // size_of("zh", "x", "c")
    group = size_of("y", "za", "zb") * rows
    my = {name: lax.axis_index(name) for name in AXES}

    images = image_embed.astype(jnp.float32)
    image = (images / jnp.sqrt(jnp.sum(images * images, axis=-1, keepdims=True) + 1e-06)).astype(
        jnp.bfloat16
    )
    tokens, image = lax.optimization_barrier((tokens, image))
    some_images = spread_to(image, "za").reshape(-1, width)

    values = tokens.reshape(rows * length, width).astype(jnp.float32)
    center = jnp.mean(values, axis=-1, keepdims=True)
    spread = jnp.mean((values - center) ** 2, axis=-1, keepdims=True)
    normed = ((values - center) * lax.rsqrt(spread + 1e-06) * norm_gain).astype(jnp.bfloat16)
    live = jnp.arange(length, dtype=jnp.int32) < token_count[:, None]
    masked = jnp.where(live.reshape(rows * length, 1), normed, 0)

    pre = jnp.dot(normed, head_weight, preferred_element_type=jnp.float32) + head_bias
    per_count = 1.0 / token_count.astype(jnp.float32)[:, None]
    scale = live.astype(jnp.float32) * per_count
    pooled = jnp.sum(gelu(pre).reshape(rows, length, width) * scale[:, :, None], axis=1)
    size = jnp.sqrt(jnp.sum(pooled * pooled, axis=-1, keepdims=True) + 1e-06)
    unit32 = pooled / size
    unit = unit32.astype(jnp.bfloat16)
    units = from_others(unit, "zb")
    masked, units = lax.optimization_barrier((masked, units))
    by_x = jnp.concatenate(from_others(masked, "x"))
    other = lax.ppermute(by_x, "c", [(0, 1), (1, 0)])

    units, some_images = lax.optimization_barrier((units, some_images))
    units = jnp.concatenate(units)
    all_images = spread_to(some_images, "y").reshape(-1, width)

    temper = jnp.exp(logit_scale[0])
    cosine = jnp.dot(units, all_images.T, preferred_element_type=jnp.float32)
    logit = temper * cosine + logit_bias[0]
    unit_at = lax.broadcasted_iota(jnp.int32, cosine.shape, 0)
    image_at = lax.broadcasted_iota(jnp.int32, cosine.shape, 1)
    same = unit_at == image_at - (my["y"] * size_of("za") + my["za"]) * rows
    label = jnp.where(same & (unit_at < rows), 1.0, -1.0)
    dlogit = (-label / (1.0 + jnp.exp(label * logit)) / group).astype(jnp.bfloat16)
    terms = jnp.dot(dlogit, all_images, preferred_element_type=jnp.float32).astype(jnp.bfloat16)
    near = size_of("zb")
    return_to = (my["zb"] - jnp.arange(near)) % near
    terms = terms.reshape(near, rows, width)[return_to]
    terms, other = lax.optimization_barrier((terms, other))
    halves = jnp.concatenate([by_x, other])
    terms = lax.all_to_all(terms, "zb", split_axis=0, concat_axis=0, tiled=True)
    dunit = temper * jnp.sum(terms.astype(jnp.float32), axis=0)
    dpooled = (dunit - unit32 * jnp.sum(unit32 * dunit, axis=-1, keepdims=True)) / size
    share = (dpooled * per_count).astype(jnp.bfloat16)
    slope = gelu_slope(
        jnp.dot(halves, head_weight, preferred_element_type=jnp.float32) + head_bias
    ).astype(jnp.bfloat16)
    here = my["x"] * 2 + my["c"]
    team = 2 * size_of("x")
    wanted = lax.broadcasted_iota(jnp.int32, (width, 2 * part), 1)
    source = lax.broadcasted_iota(jnp.int32, (width, 2 * part), 0)
    half_of = wanted // part
    zh_of = jnp.where(half_of == 0, my["zh"], 1 - my["zh"])
    pick = (source == (zh_of * team + here) * part + wanted % part).astype(jnp.bfloat16)
    columns = jnp.dot(halves, pick, preferred_element_type=jnp.float32).astype(jnp.bfloat16)
    share, slope, columns = lax.optimization_barrier((share, slope, columns))
    shares = spread_to(share, "x", "c")
    along = size_of("x")
    owners = jnp.stack(
        [((my["x"] - k) % along) * 2 + (my["c"] ^ j) for j in (0, 1) for k in range(along)]
    )
    shares = shares[owners]

    dpre = (
        shares.reshape(team * rows, 1, width).astype(jnp.float32)
        * slope.reshape(team * rows, length, width).astype(jnp.float32)
    ).astype(jnp.bfloat16)
    both = lax.dot_general(
        columns,
        dpre.reshape(team * rows * length, width),
        (((0,), (0,)), ((), ())),
        preferred_element_type=jnp.float32,
    )
    away = lax.ppermute(both[part:].astype(jnp.bfloat16), "zh", [(0, 1), (1, 0)])
    return (both[:part] + away.astype(jnp.float32))[None]


def solution(mesh):
    fine = Mesh(mesh.devices.reshape(SIZES), AXES)
    everyone = AXES
    in_specs = (
        P(everyone, None, None),
        P(everyone),
        P(everyone, None),
        P(),
        P(),
        P(),
        P(),
        P(),
    )
    out_specs = P(("y", "za", "zb"), ("zh", "x", "c"), None)
    return jax.shard_map(
        on_device, mesh=fine, in_specs=in_specs, out_specs=out_specs, check_vma=False
    )
```

time: 165 us -> 174 us (1.055)
  the two profiles are of different devices: /device:TPU:961 before, /device:TPU:288 now
where the time goes in v2:
time: 174 us; the launch traced here: 173 us
  starting transfers between devices  68.8 us (40%)
  waiting for transfers between devices  59.5 us (34%)
  matrix products  16.9 us (10%)
  other arithmetic  13.3 us (8%)
  local copies, waits for them, and re-layouts  12.3 us (7%)
    ppermute x1, waiting for transfers between devices, on_device(): lax.ppermute(both[part:].astype(jnp.bfloat16), 'zh', [(0, 1), (1, 0)])  38 us
    all_to_all x3, starting transfers between devices, spread_to(): return lax.all_to_all(copies, axes, split_axis=0, concat_axis=0, tiled=True)  27.4 us
    ppermute x6, starting transfers between devices, from_others(): lax.ppermute(value, axis, [(i, (i + k) % count) for i in range(count)])  22.4 us
    all_to_all x3, waiting for transfers between devices, spread_to(): return lax.all_to_all(copies, axes, split_axis=0, concat_axis=0, tiled=True)  17.3 us
    ppermute x1, starting transfers between devices, on_device(): lax.ppermute(both[part:].astype(jnp.bfloat16), 'zh', [(0, 1), (1, 0)])  12.8 us
    dot_general x1, matrix products, on_device(): jnp.dot(halves, head_weight, preferred_element_type=jnp.float32) + head_bias  8.21 us
    all_to_all x1, starting transfers between devices, on_device(): terms = lax.all_to_all(terms, 'zb', split_axis=0, concat_axis=0, tiled=True)  4.31 us
    ppermute x6, waiting for transfers between devices, from_others(): lax.ppermute(value, axis, [(i, (i + k) % count) for i in range(count)])  4.24 us
  transfers between devices with their start and end apart: 12, of which 5 were waited for; matrix products, arithmetic and copies ran while one was open for 17% of the time, Pallas kernels for 0%

profile of v2, /device:TPU:288, one launch (start us, length us, event | category | flops | bytes accessed | tf_op | source)
XLA Modules:
  0.0 172.6 jit_solution(17415805585384371941)
XLA Ops:
  5.8 1.8 %fusion.23 = f32[16,1152]{1,0:T(8,128)S(1)} fusion(bf16[1152,1152]{1,0:T(8,128)(2,1)S(1)} %copy-done, f32[16,8]{1,0:T(8,128)S(1)} %broadcast_select_fusion.1, f32[1152]{0:T(1024)} %param.13, bf16[16,8,1152]{2,1,0:T(8,128)(2,1)} %param.8, f32[1152]{0:T(1024)} %param.11, f32[128]{0:T(128)S(1)} %rsqrt.12, f32[128]{0:T(128)S(1)} %div.53), kind=kOutput, calls=%fused_computation.38 | convolution fusion | flops 342079488 | bytes 3033600 | tf_op jit(solution)/shard_map/dot_general | solution.py:71
  7.9 3.8 %collective-permute-start = (bf16[16,1152]{1,0:T(8,128)(2,1)S(1)}, bf16[16,1152]{1,0:T(8,128)(2,1)}, u32[]{:S(2)}, u32[]{:S(2)}) collective-permute-start(bf16[16,1152]{1,0:T(8,128)(2,1)S(1)} %fusion.82), channel_id=1, source_target_pairs={{0,16},{16,32},{32,48},{48,0},{1,17},{17,33},{33,49},{49,1},{2,18}... | collective-permute-start | bytes 110600 | tf_op jit(solution)/shard_map/ppermute | solution.py:43
  11.7 3.3 %collective-permute-start.1 = (bf16[16,1152]{1,0:T(8,128)(2,1)S(1)}, bf16[16,1152]{1,0:T(8,128)(2,1)S(1)}, u32[]{:S(2)}, u32[]{:S(2)}) collective-permute-start(bf16[16,1152]{1,0:T(8,128)(2,1)S(1)} %fusion.82), channel_id=1, source_target_pairs={{0,32},{16,48},{32,0},{48,16},{1,33},{17,49},{33,1},{49,17},{2,34}... | collective-permute-start | bytes 110600 | tf_op jit(solution)/shard_map/ppermute | solution.py:43
  15.0 3.9 %collective-permute-start.2 = (bf16[16,1152]{1,0:T(8,128)(2,1)S(1)}, bf16[16,1152]{1,0:T(8,128)(2,1)S(1)}, u32[]{:S(2)}, u32[]{:S(2)}) collective-permute-start(bf16[16,1152]{1,0:T(8,128)(2,1)S(1)} %fusion.82), channel_id=1, source_target_pairs={{0,48},{16,0},{32,16},{48,32},{1,49},{17,1},{33,17},{49,33},{2,50}... | collective-permute-start | bytes 110600 | tf_op jit(solution)/shard_map/ppermute | solution.py:43
  19.6 18.6 %all-to-all-start = ((bf16[4,16,1152]{2,1,0:T(8,128)(2,1)}), bf16[4,16,1152]{2,1,0:T(8,128)(2,1)}, u32[]{:S(2)}, u32[]{:S(2)}) async-start(bf16[4,16,1152]{2,1,0:T(8,128)(2,1)} %broadcast_in_dim.40), calls=%async_computation | async-start | bytes 294912 | tf_op jit(solution)/shard_map/all_to_all | solution.py:37
  41.0 3.4 %collective-permute-start.3 = (bf16[128,1152]{1,0:T(8,128)(2,1)S(1)}, bf16[128,1152]{1,0:T(8,128)(2,1)}, u32[]{:S(2)}, u32[]{:S(2)}) collective-permute-start(bf16[128,1152]{1,0:T(8,128)(2,1)S(1)} %broadcast_select_fusion), channel_id=1, source_target_pairs={{0,2},{2,4},{4,6},{6,0},{1,3},{3,5},{5,7},{7,1},{8,10},{10,12},{12... | collective-permute-start | bytes 884744 | tf_op jit(solution)/shard_map/ppermute | solution.py:43
  44.4 4.6 %collective-permute-start.4 = (bf16[128,1152]{1,0:T(8,128)(2,1)S(1)}, bf16[128,1152]{1,0:T(8,128)(2,1)S(1)}, u32[]{:S(2)}, u32[]{:S(2)}) collective-permute-start(bf16[128,1152]{1,0:T(8,128)(2,1)S(1)} %broadcast_select_fusion), channel_id=1, source_target_pairs={{0,4},{2,6},{4,0},{6,2},{1,5},{3,7},{5,1},{7,3},{8,12},{10,14},{12... | collective-permute-start | bytes 884744 | tf_op jit(solution)/shard_map/ppermute | solution.py:43
  49.1 3.3 %collective-permute-start.5 = (bf16[128,1152]{1,0:T(8,128)(2,1)S(1)}, bf16[128,1152]{1,0:T(8,128)(2,1)S(1)}, u32[]{:S(2)}, u32[]{:S(2)}) collective-permute-start(bf16[128,1152]{1,0:T(8,128)(2,1)S(1)} %broadcast_select_fusion), channel_id=1, source_target_pairs={{0,6},{2,0},{4,2},{6,4},{1,7},{3,1},{5,3},{7,5},{8,14},{10,8},{12,... | collective-permute-start | bytes 884744 | tf_op jit(solution)/shard_map/ppermute | solution.py:43
  56.1 2.7 %collective-permute-done.4 = bf16[128,1152]{1,0:T(8,128)(2,1)S(1)} collective-permute-done((bf16[128,1152]{1,0:T(8,128)(2,1)S(1)}, bf16[128,1152]{1,0:T(8,128)(2,1)S(1)}, u32[]{:S(2)}, u32[]{:S(2)}) %collective-permute-start.4) | collective-permute-done | bytes 294944 | tf_op jit(solution)/shard_map/ppermute | solution.py:43
  60.3 2.1 %pad_maximum_fusion = bf16[512,1152]{1,0:T(8,128)(2,1)} fusion(bf16[128,1152]{1,0:T(8,128)(2,1)S(1)} %collective-permute-done.5, bf16[128,1152]{1,0:T(8,128)(2,1)S(1)} %collective-permute-done.4, bf16[128,1152]{1,0:T(8,128)(2,1)} %collective-permute-done.3, bf16[128,1152]{1,0:T(8,128)(2,1)S(1)} %broadcast_select_fusion), kind=kLoop, calls=%fused_computation.17 | loop fusion | flops 4718592 | bytes 2359296 | tf_op jit(solution)/shard_map/concatenate | solution.py:80
  62.4 1.9 %collective-permute-start.6 = (bf16[512,1152]{1,0:T(8,128)(2,1)}, bf16[512,1152]{1,0:T(8,128)(2,1)}, u32[]{:S(2)}, u32[]{:S(2)}) collective-permute-start(bf16[512,1152]{1,0:T(8,128)(2,1)} %pad_maximum_fusion), channel_id=1, source_target_pairs={{0,1},{1,0},{2,3},{3,2},{4,5},{5,4},{6,7},{7,6},{8,9},{9,8},{10,11... | collective-permute-start | bytes 3538952 | tf_op jit(solution)/shard_map/ppermute | solution.py:81
  66.7 1.8 %broadcast_in_dim.41 = bf16[4,64,1152]{2,1,0:T(8,128)(2,1)} broadcast(bf16[64,1152]{1,0:T(8,128)(2,1)} %bitcast.3), dimensions={1,2} | broadcast | bytes 737280 | tf_op jit(solution)/shard_map/broadcast_in_dim | solution.py:36
  68.5 4.5 %all-to-all-start.1 = ((bf16[4,64,1152]{2,1,0:T(8,128)(2,1)}), bf16[4,64,1152]{2,1,0:T(8,128)(2,1)}, u32[]{:S(2)}, u32[]{:S(2)}) async-start(bf16[4,64,1152]{2,1,0:T(8,128)(2,1)} %broadcast_in_dim.41), calls=%async_computation.1 | async-start | bytes 1179648 | tf_op jit(solution)/shard_map/all_to_all | solution.py:37
  74.5 9.5 %all-to-all-done.1 = bf16[4,64,1152]{2,1,0:T(8,128)(2,1)} async-done(((bf16[4,64,1152]{2,1,0:T(8,128)(2,1)}), bf16[4,64,1152]{2,1,0:T(8,128)(2,1)}, u32[]{:S(2)}, u32[]{:S(2)}) %all-to-all-start.1) | async-done | bytes 589856 | tf_op jit(solution)/shard_map/all_to_all | solution.py:37
  84.0 2.0 %convolution_convert_fusion = bf16[64,1152]{1,0:T(8,128)(2,1)S(1)} fusion(bf16[256,1152]{1,0:T(8,128)(2,1)} %bitcast.4, bf16[16,1152]{1,0:T(8,128)(2,1)} %copy-done.12, bf16[16,1152]{1,0:T(8,128)(2,1)} %copy-done.11, bf16[16,1152]{1,0:T(8,128)(2,1)} %collective-permute-done, bf16[16,1152]{1,0:T(8,128)(2,1)} %copy-done.4, f32[]{:T(128)} %bitcast.53, ...), kind=kOutput, calls=%fused_computation.15 | convolution fusion | flops 76341248 | bytes 885832 | tf_op jit(solution)/shard_map/dot_general | solution.py:95
  87.2 4.3 %all-to-all-start.2 = ((bf16[4,16,1152]{2,1,0:T(8,128)(2,1)}), bf16[4,16,1152]{2,1,0:T(8,128)(2,1)S(1)}, u32[]{:S(2)}, u32[]{:S(2)}) async-start(bf16[4,16,1152]{2,1,0:T(8,128)(2,1)} %gather_fusion), calls=%async_computation.2 | async-start | bytes 294912 | tf_op jit(solution)/shard_map/all_to_all | solution.py:101
  91.5 2.4 %constant_dynamic-update-slice_fusion = bf16[1024,1152]{1,0:T(8,128)(2,1)} fusion(bf16[1024,1152]{1,0:T(8,128)(2,1)} %constant_dynamic-update-slice_fusion.1, bf16[512,1152]{1,0:T(8,128)(2,1)} %collective-permute-done.6), kind=kLoop, calls=%fused_computation.89 | loop fusion | bytes 2359296 | tf_op jit(solution)/shard_map/concatenate | solution.py:100
  93.9 2.6 %convolution_convert_fusion.1 = bf16[1024,144]{0,1:T(8,128)(2,1)S(1)} fusion(bf16[1024,1152]{1,0:T(8,128)(2,1)} %constant_dynamic-update-slice_fusion, s32[144]{0:T(256)S(1)} %copy-done.7, s32[144]{0:T(256)S(1)} %copy-done.8, s32[]{:T(128)S(6)} %add.200, s32[]{:T(128)S(6)} %sub.76, s32[]{:T(128)S(6)} %axis_index.72, s32[144]{0:T(256)S(1)} %get-tuple-element.39, ...), kind=kOutput, calls=%fused_computation.16 | convolution fusion | flops 341379072 | bytes 2656812 | tf_op jit(solution)/shard_map/dot_general | solution.py:115
  96.6 8.2 %fusion.5 = bf16[1024,1152]{1,0:T(8,128)(2,1)} fusion(bf16[1024,1152]{1,0:T(8,128)(2,1)} %constant_dynamic-update-slice_fusion, bf16[1152,1152]{1,0:T(8,128)(2,1)S(1)} %copy-done, f32[1152]{0:T(1024)S(1)} %copy-done.13), kind=kOutput, calls=%fused_computation.9 | convolution fusion | flops 2740322304 | bytes 7377408 | tf_op jit(solution)/shard_map/dot_general | solution.py:106
  105.9 4.3 %all-to-all-start.3 = ((bf16[8,16,1152]{2,1,0:T(8,128)(2,1)}), bf16[8,16,1152]{2,1,0:T(8,128)(2,1)S(1)}, u32[]{:S(2)}, u32[]{:S(2)}) async-start(bf16[8,16,1152]{2,1,0:T(8,128)(2,1)} %broadcast_in_dim.71), calls=%async_computation.3 | async-start | bytes 589824 | tf_op jit(solution)/shard_map/all_to_all | solution.py:37
  110.2 7.9 %all-to-all-done.3 = bf16[8,16,1152]{2,1,0:T(8,128)(2,1)S(1)} async-done(((bf16[8,16,1152]{2,1,0:T(8,128)(2,1)}), bf16[8,16,1152]{2,1,0:T(8,128)(2,1)S(1)}, u32[]{:S(2)}, u32[]{:S(2)}) %all-to-all-start.3) | async-done | bytes 294944 | tf_op jit(solution)/shard_map/all_to_all | solution.py:37
  118.8 2.3 %fusion.7 = f32[144,1152]{1,0:T(8,128)S(1)} fusion(bf16[1024,144]{0,1:T(8,128)(2,1)S(1)} %convolution_convert_fusion.1, bf16[1024,1152]{1,0:T(8,128)(2,1)} %fusion.5, f32[128,1152]{1,0:T(8,128)S(1)} %bitcast_convert_fusion), kind=kOutput, calls=%fused_computation.13 | convolution fusion | flops 343277568 | bytes 3907584 | tf_op jit(solution)/shard_map/dot_general | solution.py:128
  121.1 12.8 %collective-permute-start.7 = (bf16[72,1152]{1,0:T(8,128)(2,1)S(1)}, bf16[72,1152]{1,0:T(8,128)(2,1)S(1)}, u32[]{:S(2)}, u32[]{:S(2)}) collective-permute-start(bf16[72,1152]{1,0:T(8,128)(2,1)S(1)} %slice.19), channel_id=1, source_target_pairs={{0,8},{8,0},{1,9},{9,1},{2,10},{10,2},{3,11},{11,3},{4,12},{12,4},... | collective-permute-start | bytes 497672 | tf_op jit(solution)/shard_map/ppermute | solution.py:134
  133.8 38.0 %collective-permute-done.7 = bf16[72,1152]{1,0:T(8,128)(2,1)S(1)} collective-permute-done((bf16[72,1152]{1,0:T(8,128)(2,1)S(1)}, bf16[72,1152]{1,0:T(8,128)(2,1)S(1)}, u32[]{:S(2)}, u32[]{:S(2)}) %collective-permute-start.7) | collective-permute-done | bytes 165920 | tf_op jit(solution)/shard_map/ppermute | solution.py:134
  (81 shorter events, 20.9 us)
Async XLA Ops:
  5.8 32.5 %copy-start.6 = (s32[16]{0:T(128)S(1)}, s32[16]{0:T(128)}, u32[]{:S(2)}) copy-start(s32[16]{0:T(128)} %param.9) | copy-start | bytes 196
  5.8 34.4 %copy-start.1 = (bf16[16,8,1152]{2,1,0:T(8,128)(2,1)S(1)}, bf16[16,8,1152]{2,1,0:T(8,128)(2,1)}, u32[]{:S(2)}) copy-start(bf16[16,8,1152]{2,1,0:T(8,128)(2,1)} %param.8) | copy-start | bytes 884740
  5.8 34.4 %copy-start.5 = (f32[1152]{0:T(1024)S(1)}, f32[1152]{0:T(1024)}, u32[]{:S(2)}) copy-start(f32[1152]{0:T(1024)} %param.11) | copy-start | bytes 13828
  7.6 32.4 %copy-start.2 = (f32[16,1152]{1,0:T(8,128)}, f32[16,1152]{1,0:T(8,128)S(1)}, u32[]{:S(2)}) copy-start(f32[16,1152]{1,0:T(8,128)S(1)} %fusion.23) | copy-start | bytes 221188
  7.9 36.5 %copy-start.4 = (bf16[16,1152]{1,0:T(8,128)(2,1)}, bf16[16,1152]{1,0:T(8,128)(2,1)S(1)}, u32[]{:S(2)}) copy-start(bf16[16,1152]{1,0:T(8,128)(2,1)S(1)} %fusion.82) | copy-start | bytes 110596
  7.9 33.1 %collective-permute-start = (bf16[16,1152]{1,0:T(8,128)(2,1)S(1)}, bf16[16,1152]{1,0:T(8,128)(2,1)}, u32[]{:S(2)}, u32[]{:S(2)}) collective-permute-start(bf16[16,1152]{1,0:T(8,128)(2,1)S(1)} %fusion.82), channel_id=1, source_target_pairs={{0,16},{16,32},{32,48},{48,0},{1,17},{17,33},{33,49},{49,1},{2,18}... | collective-permute-start | bytes 110600 | tf_op jit(solution)/shard_map/ppermute | solution.py:43
  11.7 29.3 %collective-permute-start.1 = (bf16[16,1152]{1,0:T(8,128)(2,1)S(1)}, bf16[16,1152]{1,0:T(8,128)(2,1)S(1)}, u32[]{:S(2)}, u32[]{:S(2)}) collective-permute-start(bf16[16,1152]{1,0:T(8,128)(2,1)S(1)} %fusion.82), channel_id=1, source_target_pairs={{0,32},{16,48},{32,0},{48,16},{1,33},{17,49},{33,1},{49,17},{2,34}... | collective-permute-start | bytes 110600 | tf_op jit(solution)/shard_map/ppermute | solution.py:43
  15.0 26.0 %collective-permute-start.2 = (bf16[16,1152]{1,0:T(8,128)(2,1)S(1)}, bf16[16,1152]{1,0:T(8,128)(2,1)S(1)}, u32[]{:S(2)}, u32[]{:S(2)}) collective-permute-start(bf16[16,1152]{1,0:T(8,128)(2,1)S(1)} %fusion.82), channel_id=1, source_target_pairs={{0,48},{16,0},{32,16},{48,32},{1,49},{17,1},{33,17},{49,33},{2,50}... | collective-permute-start | bytes 110600 | tf_op jit(solution)/shard_map/ppermute | solution.py:43
  19.6 47.1 %all-to-all-start = ((bf16[4,16,1152]{2,1,0:T(8,128)(2,1)}), bf16[4,16,1152]{2,1,0:T(8,128)(2,1)}, u32[]{:S(2)}, u32[]{:S(2)}) async-start(bf16[4,16,1152]{2,1,0:T(8,128)(2,1)} %broadcast_in_dim.40), calls=%async_computation | async-start | bytes 294912 | tf_op jit(solution)/shard_map/all_to_all | solution.py:37
  41.0 15.1 %collective-permute-start.3 = (bf16[128,1152]{1,0:T(8,128)(2,1)S(1)}, bf16[128,1152]{1,0:T(8,128)(2,1)}, u32[]{:S(2)}, u32[]{:S(2)}) collective-permute-start(bf16[128,1152]{1,0:T(8,128)(2,1)S(1)} %broadcast_select_fusion), channel_id=1, source_target_pairs={{0,2},{2,4},{4,6},{6,0},{1,3},{3,5},{5,7},{7,1},{8,10},{10,12},{12... | collective-permute-start | bytes 884744 | tf_op jit(solution)/shard_map/ppermute | solution.py:43
  44.4 14.3 %collective-permute-start.4 = (bf16[128,1152]{1,0:T(8,128)(2,1)S(1)}, bf16[128,1152]{1,0:T(8,128)(2,1)S(1)}, u32[]{:S(2)}, u32[]{:S(2)}) collective-permute-start(bf16[128,1152]{1,0:T(8,128)(2,1)S(1)} %broadcast_select_fusion), channel_id=1, source_target_pairs={{0,4},{2,6},{4,0},{6,2},{1,5},{3,7},{5,1},{7,3},{8,12},{10,14},{12... | collective-permute-start | bytes 884744 | tf_op jit(solution)/shard_map/ppermute | solution.py:43
  49.1 11.2 %collective-permute-start.5 = (bf16[128,1152]{1,0:T(8,128)(2,1)S(1)}, bf16[128,1152]{1,0:T(8,128)(2,1)S(1)}, u32[]{:S(2)}, u32[]{:S(2)}) collective-permute-start(bf16[128,1152]{1,0:T(8,128)(2,1)S(1)} %broadcast_select_fusion), channel_id=1, source_target_pairs={{0,6},{2,0},{4,2},{6,4},{1,7},{3,1},{5,3},{7,5},{8,14},{10,8},{12,... | collective-permute-start | bytes 884744 | tf_op jit(solution)/shard_map/ppermute | solution.py:43
  62.4 24.8 %collective-permute-start.6 = (bf16[512,1152]{1,0:T(8,128)(2,1)}, bf16[512,1152]{1,0:T(8,128)(2,1)}, u32[]{:S(2)}, u32[]{:S(2)}) collective-permute-start(bf16[512,1152]{1,0:T(8,128)(2,1)} %pad_maximum_fusion), channel_id=1, source_target_pairs={{0,1},{1,0},{2,3},{3,2},{4,5},{5,4},{6,7},{7,6},{8,9},{9,8},{10,11... | collective-permute-start | bytes 3538952 | tf_op jit(solution)/shard_map/ppermute | solution.py:81
  68.5 15.4 %all-to-all-start.1 = ((bf16[4,64,1152]{2,1,0:T(8,128)(2,1)}), bf16[4,64,1152]{2,1,0:T(8,128)(2,1)}, u32[]{:S(2)}, u32[]{:S(2)}) async-start(bf16[4,64,1152]{2,1,0:T(8,128)(2,1)} %broadcast_in_dim.41), calls=%async_computation.1 | async-start | bytes 1179648 | tf_op jit(solution)/shard_map/all_to_all | solution.py:37
  74.5 19.4 %copy-start.7 = (s32[144]{0:T(256)S(1)}, s32[144]{0:T(256)}, u32[]{:S(2)}) copy-start(s32[144]{0:T(256)} %get-tuple-element.40) | copy-start | bytes 1732
  74.5 19.4 %copy-start.8 = (s32[144]{0:T(256)S(1)}, s32[144]{0:T(256)}, u32[]{:S(2)}) copy-start(s32[144]{0:T(256)} %get-tuple-element.43) | copy-start | bytes 1732
  74.5 19.4 %copy-start.9 = (s32[144]{0:T(256)S(1)}, s32[144]{0:T(256)}, u32[]{:S(2)}) copy-start(s32[144]{0:T(256)} %get-tuple-element.44) | copy-start | bytes 1732
  74.5 19.4 %copy-start.14 = (pred[144]{0:T(512)(128)(4,1)S(1)}, pred[144]{0:T(512)(128)(4,1)}, u32[]{:S(2)}) copy-start(pred[144]{0:T(512)(128)(4,1)} %get-tuple-element.41) | copy-start | bytes 436
  74.5 19.4 %copy-start.15 = (pred[144]{0:T(512)(128)(4,1)S(1)}, pred[144]{0:T(512)(128)(4,1)}, u32[]{:S(2)}) copy-start(pred[144]{0:T(512)(128)(4,1)} %get-tuple-element.42) | copy-start | bytes 436
  87.2 17.6 %all-to-all-start.2 = ((bf16[4,16,1152]{2,1,0:T(8,128)(2,1)}), bf16[4,16,1152]{2,1,0:T(8,128)(2,1)S(1)}, u32[]{:S(2)}, u32[]{:S(2)}) async-start(bf16[4,16,1152]{2,1,0:T(8,128)(2,1)} %gather_fusion), calls=%async_computation.2 | async-start | bytes 294912 | tf_op jit(solution)/shard_map/all_to_all | solution.py:101
  96.6 8.3 %copy-start.3 = (f32[16,1152]{1,0:T(8,128)S(1)}, f32[16,1152]{1,0:T(8,128)}, u32[]{:S(2)}) copy-start(f32[16,1152]{1,0:T(8,128)} %copy-done.2) | copy-start | bytes 221188
  96.6 13.6 %copy-start.10 = (s32[8,1]{0,1:T(1,128)S(1)}, s32[8,1]{0,1:T(1,128)}, u32[]{:S(2)}) copy-start(s32[8,1]{0,1:T(1,128)} %stack.35) | copy-start | bytes 100
  105.9 12.2 %all-to-all-start.3 = ((bf16[8,16,1152]{2,1,0:T(8,128)(2,1)}), bf16[8,16,1152]{2,1,0:T(8,128)(2,1)S(1)}, u32[]{:S(2)}, u32[]{:S(2)}) async-start(bf16[8,16,1152]{2,1,0:T(8,128)(2,1)} %broadcast_in_dim.71), calls=%async_computation.3 | async-start | bytes 589824 | tf_op jit(solution)/shard_map/all_to_all | solution.py:37
  121.1 50.7 %collective-permute-start.7 = (bf16[72,1152]{1,0:T(8,128)(2,1)S(1)}, bf16[72,1152]{1,0:T(8,128)(2,1)S(1)}, u32[]{:S(2)}, u32[]{:S(2)}) collective-permute-start(bf16[72,1152]{1,0:T(8,128)(2,1)S(1)} %slice.19), channel_id=1, source_target_pairs={{0,8},{8,0},{1,9},{9,1},{2,10},{10,2},{3,11},{11,3},{4,12},{12,4},... | collective-permute-start | bytes 497672 | tf_op jit(solution)/shard_map/ppermute | solution.py:134
  (4 other events, 15.3 us)

commit v3 on v2

v3 whole, which is shorter than its diff:
```python
import functools

import jax
import jax.numpy as jnp
from jax import lax
from jax.experimental import pallas as pl
from jax.experimental.pallas import tpu as pltpu
from jax.sharding import Mesh, PartitionSpec as P

AXES = ("y", "za", "zb", "zh", "x", "c")
SIZES = (4, 4, 4, 2, 4, 2)
COEFF = 0.7978845608
CUBIC = 0.044715
BF16, F32 = jnp.bfloat16, jnp.float32


def size_of(*names):
    count = 1
    for name in names:
        count *= SIZES[AXES.index(name)]
    return count


def from_others(value, axis):
    count = size_of(axis)
    moved = [
        lax.ppermute(value, axis, [(i, (i + k) % count) for i in range(count)])
        for k in range(1, count)
    ]
    return [value] + moved


def exchange(copies, *axes):
    return lax.all_to_all(copies, axes, split_axis=0, concat_axis=0, tiled=True)


def local(body, outs, *args, smem=(), scratch=(), flops=0, moved=0):
    vmem = pl.BlockSpec(memory_space=pltpu.VMEM)
    in_specs = [pl.BlockSpec(memory_space=pltpu.SMEM) if i in smem else vmem for i in range(len(args))]
    return pl.pallas_call(
        body,
        out_shape=[jax.ShapeDtypeStruct(shape, dtype) for shape, dtype in outs],
        in_specs=in_specs,
        out_specs=[vmem] * len(outs),
        scratch_shapes=[pltpu.VMEM(shape, dtype) for shape, dtype in scratch],
        compiler_params=pltpu.CompilerParams(vmem_limit_bytes=40 * 1024 * 1024),
        cost_estimate=pl.CostEstimate(flops=flops, bytes_accessed=moved, transcendentals=0),
    )(*args)


def image_kernel(image_ref, out_ref):
    images = image_ref[...].astype(F32)
    norm = jnp.sqrt(jnp.sum(images * images, axis=-1, keepdims=True) + 1e-06)
    image = (images / norm).astype(BF16)
    for k in range(out_ref.shape[0]):
        out_ref[k] = image


def front_kernel(
    count_ref, token_ref, gain_ref, weight_ref, bias_ref, masked_ref, unit_ref, pooled_ref, share_ref, act_ref
):
    rows, width = pooled_ref.shape
    length = token_ref.shape[0] // rows
    values = token_ref[...].astype(F32)
    center = jnp.mean(values, axis=-1, keepdims=True)
    spread = jnp.mean((values - center) ** 2, axis=-1, keepdims=True)
    gain = gain_ref[...].reshape(1, width)
    normed = ((values - center) * lax.rsqrt(spread + 1e-06) * gain).astype(BF16)
    pre = jnp.dot(normed, weight_ref[...], preferred_element_type=F32)
    pre = pre + bias_ref[...].reshape(1, width)
    act_ref[...] = 0.5 * pre * (1.0 + jnp.tanh(COEFF * (pre + CUBIC * pre * pre * pre)))
    slot = lax.broadcasted_iota(jnp.int32, (length, 1), 0)
    lives = []
    for p in range(rows):
        live = (slot < count_ref[p]).astype(F32)
        inverse = 1.0 / jnp.full((length, 1), count_ref[p], jnp.int32).astype(F32)
        part = act_ref[p * length : (p + 1) * length, :] * (live * inverse)
        pooled_ref[p : p + 1, :] = jnp.sum(part, axis=0, keepdims=True)
        share_ref[p : p + 1, :] = jnp.broadcast_to(inverse[:1], (1, share_ref.shape[1]))
        lives.append(live)
    masked_ref[...] = normed * jnp.concatenate(lives, axis=0).astype(BF16)
    pooled = pooled_ref[...]
    size = jnp.sqrt(jnp.sum(pooled * pooled, axis=-1, keepdims=True) + 1e-06)
    unit_ref[...] = (pooled / size).astype(BF16)


def stack_kernel(*refs):
    *piece_refs, out_ref = refs
    block = piece_refs[0].shape[0]
    for k, ref in enumerate(piece_refs):
        out_ref[k * block : (k + 1) * block, :] = ref[...]


def copies_kernel(image_ref, out_ref):
    for k in range(out_ref.shape[0]):
        for j in range(image_ref.shape[0]):
            rows = image_ref.shape[1]
            out_ref[k, j * rows : (j + 1) * rows, :] = image_ref[j]


def logit_kernel(scale_ref, shift_ref, *refs):
    *unit_refs, image_ref, out_ref = refs
    near, rows, width = out_ref.shape
    group = rows * size_of("y", "za", "zb")
    units = jnp.concatenate([ref[...] for ref in unit_refs], axis=0)
    images = image_ref[...]
    temper = jnp.exp(jnp.full((1, 1), scale_ref[0], F32))
    cosine = lax.dot_general(units, images, (((1,), (1,)), ((), ())), preferred_element_type=F32)
    logit = temper * cosine + shift_ref[0]
    unit_at = lax.broadcasted_iota(jnp.int32, cosine.shape, 0)
    image_at = lax.broadcasted_iota(jnp.int32, cosine.shape, 1)
    offset = (lax.axis_index("y") * size_of("za") + lax.axis_index("za")) * rows
    label = jnp.where((unit_at == image_at - offset) & (unit_at < rows), 1.0, -1.0)
    dlogit = (-label / (1.0 + jnp.exp(label * logit)) / group).astype(BF16)
    terms = jnp.dot(dlogit, images, preferred_element_type=F32).astype(BF16)
    for k in range(near):
        owner = lax.rem(lax.axis_index("zb") + near - k, near)
        out_ref[owner] = terms[k * rows : (k + 1) * rows]


def share_kernel(scale_ref, term_ref, pooled_ref, inverse_ref, out_ref):
    temper = jnp.exp(jnp.full((1, 1), scale_ref[0], F32))
    pooled = pooled_ref[...]
    size = jnp.sqrt(jnp.sum(pooled * pooled, axis=-1, keepdims=True) + 1e-06)
    unit = pooled / size
    total = term_ref[0].astype(F32)
    for k in range(1, term_ref.shape[0]):
        total = total + term_ref[k].astype(F32)
    dunit = temper * total
    dpooled = (dunit - unit * jnp.sum(unit * dunit, axis=-1, keepdims=True)) / size
    share = (dpooled * inverse_ref[:, :1]).astype(BF16)
    for k in range(out_ref.shape[0]):
        out_ref[k] = share


def slope_kernel(weight_ref, bias_ref, *refs):
    *piece_refs, first_ref, second_ref, column_ref = refs
    width = weight_ref.shape[0]
    block = piece_refs[0].shape[0]
    part = column_ref.shape[0] // 2
    split = first_ref.shape[1]
    here = lax.axis_index("x") * size_of("c") + lax.axis_index("c")
    team = size_of("x", "c")
    half = lax.axis_index("zh")
    row = lax.broadcasted_iota(jnp.int32, (2 * part, width), 0)
    source = lax.broadcasted_iota(jnp.int32, (2 * part, width), 1)
    near = (half * team + here) * part
    far = ((1 - half) * team + here) * part - part
    pick = jnp.where(source == row + jnp.where(row < part, near, far), 1.0, 0.0).astype(BF16)
    bias = bias_ref[...].reshape(1, width)
    at = 0
    for ref in piece_refs:
        for begin in range(0, ref.shape[0], block):
            piece = ref[begin : begin + block, :]
            pre = jnp.dot(piece, weight_ref[...], preferred_element_type=F32) + bias
            square = pre * pre
            hyper = jnp.tanh(COEFF * (pre + CUBIC * pre * square))
            slope = 0.5 * (1.0 + hyper) + 0.5 * pre * (1.0 - hyper * hyper) * COEFF * (
                1.0 + 3.0 * CUBIC * square
            )
            slope = slope.astype(BF16)
            first_ref[at : at + block, :] = slope[:, :split]
            second_ref[at : at + block, :] = slope[:, split:]
            columns = lax.dot_general(
                pick, piece, (((1,), (1,)), ((), ())), preferred_element_type=F32
            )
            column_ref[:, at : at + block] = columns.astype(BF16)
            at += block


def grad_kernel(begin, share_ref, slope_ref, column_ref, far_ref, near_ref, dpre_ref):
    team, rows, _ = share_ref.shape
    total, cols = slope_ref.shape
    block = total // team
    along, cores = size_of("x"), size_of("c")
    part = near_ref.shape[0]
    x, c = lax.axis_index("x"), lax.axis_index("c")
    for j in range(cores):
        for k in range(along):
            at = (j * along + k) * block
            owner = lax.rem(x + along - k, along) * cores + lax.rem(c + j, cores)
            share = share_ref[owner, :, begin : begin + cols].astype(F32)
            share = jnp.broadcast_to(share[:, None, :], (rows, block // rows, cols)).reshape(block, cols)
            slope = slope_ref[at : at + block, :].astype(F32)
            dpre_ref[at : at + block, :] = (share * slope).astype(BF16)
    both = jnp.dot(column_ref[...], dpre_ref[...], preferred_element_type=F32)
    near_ref[...] = both[:part]
    far_ref[...] = both[part:].astype(BF16)


def add_kernel(near1_ref, near2_ref, away1_ref, away2_ref, out_ref):
    split = near1_ref.shape[1]
    out_ref[0, :, :split] = near1_ref[...] + away1_ref[...].astype(F32)
    out_ref[0, :, split:] = near2_ref[...] + away2_ref[...].astype(F32)


def on_device(
    tokens, token_count, image_embed, norm_gain, head_weight, head_bias, logit_scale, logit_bias
):
    rows, length, width = tokens.shape
    part = width // size_of("zh", "x", "c")
    team = size_of("x", "c")
    flat = rows * length
    total = team * flat
    split = (width // 2 + 127) // 128 * 128
    swap = [(0, 1), (1, 0)]

    (image,) = local(image_kernel, [((size_of("za"), rows, width), BF16)], image_embed)
    tokens, image = lax.optimization_barrier((tokens, image))
    some_images = exchange(image, "za")

    masked, unit, pooled, inverse = local(
        front_kernel,
        [((flat, width), BF16), ((rows, width), BF16), ((rows, width), F32), ((rows, 128), F32)],
        token_count,
        tokens.reshape(flat, width),
        norm_gain,
        head_weight,
        head_bias,
        smem=(0,),
        scratch=[((flat, width), F32)],
        flops=2 * flat * width * width,
        moved=2 * width * width,
    )
    units = from_others(unit, "zb")
    masked, units = lax.optimization_barrier((masked, units))
    by_x = from_others(masked, "x")
    by_x, units, some_images = lax.optimization_barrier((by_x, units, some_images))
    (copies,) = local(
        copies_kernel, [((size_of("y"), size_of("za") * rows, width), BF16)], some_images
    )
    (stacked,) = local(stack_kernel, [((size_of("x") * flat, width), BF16)], *by_x)
    other = lax.ppermute(stacked, "c", swap)
    all_images = exchange(copies, "y").reshape(-1, width)
    (terms,) = local(
        logit_kernel,
        [((size_of("zb"), rows, width), BF16)],
        logit_scale,
        logit_bias,
        *units,
        all_images,
        smem=(0, 1),
    )
    terms, other = lax.optimization_barrier((terms, other))
    terms = exchange(terms, "zb")
    first, second, columns = local(
        slope_kernel,
        [((total, split), BF16), ((total, width - split), BF16), ((2 * part, total), BF16)],
        head_weight,
        head_bias,
        *by_x,
        other,
        flops=2 * total * width * width,
        moved=2 * width * width + 4 * total * width,
    )
    (share,) = local(
        share_kernel,
        [((team, rows, width), BF16)],
        logit_scale,
        terms,
        pooled,
        inverse,
        smem=(0,),
    )
    share, first, second, columns = lax.optimization_barrier((share, first, second, columns))
    shares = exchange(share, "x", "c")
    away, near = [], []
    for begin, slope in ((0, first), (split, second)):
        cols = slope.shape[1]
        far, mine = local(
            functools.partial(grad_kernel, begin),
            [((part, cols), BF16), ((part, cols), F32)],
            shares,
            slope,
            columns,
            scratch=[((total, cols), BF16)],
            flops=4 * part * total * cols,
            moved=2 * total * cols,
        )
        away.append(lax.ppermute(far, "zh", swap))
        near.append(mine)
    (grad,) = local(add_kernel, [((1, part, width), F32)], *near, *away)
    return grad


def solution(mesh):
    fine = Mesh(mesh.devices.reshape(SIZES), AXES)
    in_specs = (
        P(AXES, None, None),
        P(AXES),
        P(AXES, None),
        P(),
        P(),
        P(),
        P(),
        P(),
    )
    out_specs = P(("y", "za", "zb"), ("zh", "x", "c"), None)
    return jax.shard_map(
        on_device, mesh=fine, in_specs=in_specs, out_specs=out_specs, check_vma=False
    )
```

time: 174 us -> 183 us (1.052)
  the two profiles are of different devices: /device:TPU:288 before, /device:TPU:1 now
where the time goes in v3:
time: 183 us; the launch traced here: 181 us
  starting transfers between devices  80.4 us (44%)
  waiting for transfers between devices  54.2 us (30%)
  local copies, waits for them, and re-layouts  18.8 us (10%)
  Pallas kernels  13.4 us (7%)
  blocking collectives  13 us (7%)
    ppermute x2, waiting for transfers between devices, on_device(): away.append(lax.ppermute(far, 'zh', swap))  37.2 us
    all_to_all x3, starting transfers between devices, exchange(): return lax.all_to_all(copies, axes, split_axis=0, concat_axis=0, tiled=True)  30.3 us
    ppermute x2, starting transfers between devices, on_device(): away.append(lax.ppermute(far, 'zh', swap))  23.6 us
    ppermute x6, starting transfers between devices, from_others(): lax.ppermute(value, axis, [(i, (i + k) % count) for i in range(count)])  21.6 us
    unnamed x58, local copies, waits for them, and re-layouts  18.8 us
    pallas_call x10, Pallas kernels, local(): pl.pallas_call(body, out_shape=[jax.ShapeDtypeStruct(shape, dtype) for sh...  13.4 us
    all_to_all x1, blocking collectives, exchange(): return lax.all_to_all(copies, axes, split_axis=0, concat_axis=0, tiled=True)  13 us
    all_to_all x3, waiting for transfers between devices, exchange(): return lax.all_to_all(copies, axes, split_axis=0, concat_axis=0, tiled=True)  8.73 us
  transfers between devices with their start and end apart: 12, of which 5 were waited for; matrix products, arithmetic and copies ran while one was open for 0% of the time, Pallas kernels for 5%

profile of v3, /device:TPU:1, one launch (start us, length us, event | category | flops | bytes accessed | tf_op | source)
XLA Modules:
  0.0 181.3 jit_solution(8327745709856133820)
XLA Ops:
  1.5 22.3 %all-to-all-start = ((bf16[4,16,1152]{2,1,0:T(8,128)(2,1)}), bf16[4,16,1152]{2,1,0:T(8,128)(2,1)S(1)}, u32[]{:S(2)}, u32[]{:S(2)}) async-start(bf16[4,16,1152]{2,1,0:T(8,128)(2,1)} %shard_map.82), calls=%async_computation | async-start | bytes 294912 | tf_op jit(solution)/shard_map/all_to_all | solution.py:34
  23.8 1.7 copy-done
  28.6 1.6 shard_map.83
  30.8 3.5 %collective-permute-start = (bf16[16,1152]{1,0:T(8,128)(2,1)S(1)}, bf16[16,1152]{1,0:T(8,128)(2,1)S(1)}, u32[]{:S(2)}, u32[]{:S(2)}) collective-permute-start(bf16[16,1152]{1,0:T(8,128)(2,1)S(1)} %get-tuple-element.47.refs_0_), channel_id=1, source_target_pairs={{0,16},{16,32},{32,48},{48,0},{1,17},{17,33},{33,49},{49,1},{2,18}... | collective-permute-start | bytes 110600 | tf_op jit(solution)/shard_map/ppermute | solution.py:27
  34.4 4.9 %collective-permute-start.1 = (bf16[16,1152]{1,0:T(8,128)(2,1)S(1)}, bf16[16,1152]{1,0:T(8,128)(2,1)S(1)}, u32[]{:S(2)}, u32[]{:S(2)}) collective-permute-start(bf16[16,1152]{1,0:T(8,128)(2,1)S(1)} %get-tuple-element.47.refs_0_), channel_id=1, source_target_pairs={{0,32},{16,48},{32,0},{48,16},{1,33},{17,49},{33,1},{49,17},{2,34}... | collective-permute-start | bytes 110600 | tf_op jit(solution)/shard_map/ppermute | solution.py:27
  39.3 2.6 %collective-permute-start.2 = (bf16[16,1152]{1,0:T(8,128)(2,1)S(1)}, bf16[16,1152]{1,0:T(8,128)(2,1)S(1)}, u32[]{:S(2)}, u32[]{:S(2)}) collective-permute-start(bf16[16,1152]{1,0:T(8,128)(2,1)S(1)} %get-tuple-element.47.refs_0_), channel_id=1, source_target_pairs={{0,48},{16,0},{32,16},{48,32},{1,49},{17,1},{33,17},{49,33},{2,50}... | collective-permute-start | bytes 110600 | tf_op jit(solution)/shard_map/ppermute | solution.py:27
  44.9 3.1 %collective-permute-start.3 = (bf16[128,1152]{1,0:T(8,128)(2,1)S(1)}, bf16[128,1152]{1,0:T(8,128)(2,1)S(1)}, u32[]{:S(2)}, u32[]{:S(2)}) collective-permute-start(bf16[128,1152]{1,0:T(8,128)(2,1)S(1)} %get-tuple-element.52.refs_0_), channel_id=1, source_target_pairs={{0,2},{2,4},{4,6},{6,0},{1,3},{3,5},{5,7},{7,1},{8,10},{10,12},{12... | collective-permute-start | bytes 884744 | tf_op jit(solution)/shard_map/ppermute | solution.py:27
  48.0 4.4 %collective-permute-start.4 = (bf16[128,1152]{1,0:T(8,128)(2,1)S(1)}, bf16[128,1152]{1,0:T(8,128)(2,1)S(1)}, u32[]{:S(2)}, u32[]{:S(2)}) collective-permute-start(bf16[128,1152]{1,0:T(8,128)(2,1)S(1)} %get-tuple-element.52.refs_0_), channel_id=1, source_target_pairs={{0,4},{2,6},{4,0},{6,2},{1,5},{3,7},{5,1},{7,3},{8,12},{10,14},{12... | collective-permute-start | bytes 884744 | tf_op jit(solution)/shard_map/ppermute | solution.py:27
  52.4 3.1 %collective-permute-start.5 = (bf16[128,1152]{1,0:T(8,128)(2,1)S(1)}, bf16[128,1152]{1,0:T(8,128)(2,1)S(1)}, u32[]{:S(2)}, u32[]{:S(2)}) collective-permute-start(bf16[128,1152]{1,0:T(8,128)(2,1)S(1)} %get-tuple-element.52.refs_0_), channel_id=1, source_target_pairs={{0,6},{2,0},{4,2},{6,4},{1,7},{3,1},{5,3},{7,5},{8,14},{10,8},{12,... | collective-permute-start | bytes 884744 | tf_op jit(solution)/shard_map/ppermute | solution.py:27
  55.5 6.0 %collective-permute-done.4.refs_2_ = bf16[128,1152]{1,0:T(8,128)(2,1)S(1)} collective-permute-done((bf16[128,1152]{1,0:T(8,128)(2,1)S(1)}, bf16[128,1152]{1,0:T(8,128)(2,1)S(1)}, u32[]{:S(2)}, u32[]{:S(2)}) %collective-permute-start.4) | collective-permute-done | bytes 294944 | tf_op jit(solution)/shard_map/ppermute | solution.py:27
  61.4 1.8 %collective-permute-done.5.refs_3_ = bf16[128,1152]{1,0:T(8,128)(2,1)S(1)} collective-permute-done((bf16[128,1152]{1,0:T(8,128)(2,1)S(1)}, bf16[128,1152]{1,0:T(8,128)(2,1)S(1)}, u32[]{:S(2)}, u32[]{:S(2)}) %collective-permute-start.5) | collective-permute-done | bytes 294944 | tf_op jit(solution)/shard_map/ppermute | solution.py:27
  63.2 1.1 shard_map.86
  64.4 4.9 %collective-permute-start.6 = (bf16[512,1152]{1,0:T(8,128)(2,1)}, bf16[512,1152]{1,0:T(8,128)(2,1)}, u32[]{:S(2)}, u32[]{:S(2)}) collective-permute-start(bf16[512,1152]{1,0:T(8,128)(2,1)} %shard_map.86), channel_id=1, source_target_pairs={{0,1},{1,0},{2,3},{3,2},{4,5},{5,4},{6,7},{7,6},{8,9},{9,8},{10,11... | collective-permute-start | bytes 3538952 | tf_op jit(solution)/shard_map/ppermute | solution.py:233
  70.1 4.3 %all-to-all-start.1 = ((bf16[4,64,1152]{2,1,0:T(8,128)(2,1)}), bf16[4,64,1152]{2,1,0:T(8,128)(2,1)S(1)}, u32[]{:S(2)}, u32[]{:S(2)}) async-start(bf16[4,64,1152]{2,1,0:T(8,128)(2,1)} %copy-done.2), calls=%async_computation.1 | async-start | bytes 1179648 | tf_op jit(solution)/shard_map/all_to_all | solution.py:34
  75.7 8.7 %all-to-all-done.1 = bf16[4,64,1152]{2,1,0:T(8,128)(2,1)S(1)} async-done(((bf16[4,64,1152]{2,1,0:T(8,128)(2,1)}), bf16[4,64,1152]{2,1,0:T(8,128)(2,1)S(1)}, u32[]{:S(2)}, u32[]{:S(2)}) %all-to-all-start.1) | async-done | bytes 589856 | tf_op jit(solution)/shard_map/all_to_all | solution.py:34
  87.5 1.3 shard_map.85
  88.8 3.8 %all-to-all-start.2 = ((bf16[4,16,1152]{2,1,0:T(8,128)(2,1)}), bf16[4,16,1152]{2,1,0:T(8,128)(2,1)S(1)}, u32[]{:S(2)}, u32[]{:S(2)}) async-start(bf16[4,16,1152]{2,1,0:T(8,128)(2,1)} %shard_map.85), calls=%async_computation.2 | async-start | bytes 294912 | tf_op jit(solution)/shard_map/all_to_all | solution.py:34
  95.5 6.4 %shard_map.88 = (bf16[1024,640]{1,0:T(8,128)(2,1)S(1)}, bf16[1024,512]{1,0:T(8,128)(2,1)S(1)}, bf16[144,1024]{1,0:T(8,128)(2,1)S(1)}) custom-call(bf16[1152,1152]{1,0:T(8,128)(2,1)S(1)} %copy-done.1, f32[1152]{0:T(1024)S(1)} %copy-done.27, bf16[128,1152]{1,0:T(8,128)(2,1)S(1)} %get-tuple-element.52.refs_0_, bf16[128,1152]{1,0:T(8,128)(2,1)S(1)} %copy-done.9, ...), custom_call_target="tpu_custom_call" | custom-call | flops 2717908992 | bytes 7372800 | tf_op jit(solution)/shard_map/pallas_call | solution.py:40
  101.9 1.1 copy-done.3
  104.3 13.0 %all_to_all.20.share_ref = bf16[8,16,1152]{2,1,0:T(8,128)(2,1)S(1)} all-to-all(bf16[8,16,1152]{2,1,0:T(8,128)(2,1)S(1)} %shard_map.87), channel_id=1, replica_groups=mesh['y'=4,'za'=4,'zb'=4,'zh'=2,'x'=4,'c'=2] {'x','c'}, dimensions={0} | all-to-all | bytes 589824 | tf_op jit(solution)/shard_map/all_to_all | solution.py:34
  117.2 1.3 copy-done.4
  119.2 12.2 %collective-permute-start.7 = (bf16[72,640]{1,0:T(8,128)(2,1)S(1)}, bf16[72,640]{1,0:T(8,128)(2,1)S(1)}, u32[]{:S(2)}, u32[]{:S(2)}) collective-permute-start(bf16[72,640]{1,0:T(8,128)(2,1)S(1)} %get-tuple-element.69), channel_id=1, source_target_pairs={{0,8},{8,0},{1,9},{9,1},{2,10},{10,2},{3,11},{11,3},{4,12},{12,4},... | collective-permute-start | bytes 276488 | tf_op jit(solution)/shard_map/ppermute | solution.py:280
  131.9 11.4 %collective-permute-start.8 = (bf16[72,512]{1,0:T(8,128)(2,1)S(1)}, bf16[72,512]{1,0:T(8,128)(2,1)S(1)}, u32[]{:S(2)}, u32[]{:S(2)}) collective-permute-start(bf16[72,512]{1,0:T(8,128)(2,1)S(1)} %get-tuple-element.70), channel_id=1, source_target_pairs={{0,8},{8,0},{1,9},{9,1},{2,10},{10,2},{3,11},{11,3},{4,12},{12,4},... | collective-permute-start | bytes 221192 | tf_op jit(solution)/shard_map/ppermute | solution.py:280
  143.3 37.2 %collective-permute-done.8.away2_ref = bf16[72,512]{1,0:T(8,128)(2,1)S(1)} collective-permute-done((bf16[72,512]{1,0:T(8,128)(2,1)S(1)}, bf16[72,512]{1,0:T(8,128)(2,1)S(1)}, u32[]{:S(2)}, u32[]{:S(2)}) %collective-permute-start.8) | collective-permute-done | bytes 73760 | tf_op jit(solution)/shard_map/ppermute | solution.py:280
  (69 shorter events, 18.0 us)
Async XLA Ops:
  1.5 61.7 %all-to-all-start = ((bf16[4,16,1152]{2,1,0:T(8,128)(2,1)}), bf16[4,16,1152]{2,1,0:T(8,128)(2,1)S(1)}, u32[]{:S(2)}, u32[]{:S(2)}) async-start(bf16[4,16,1152]{2,1,0:T(8,128)(2,1)} %shard_map.82), calls=%async_computation | async-start | bytes 294912 | tf_op jit(solution)/shard_map/all_to_all | solution.py:34
  23.8 1.7 copy-start
  30.8 11.7 %collective-permute-start = (bf16[16,1152]{1,0:T(8,128)(2,1)S(1)}, bf16[16,1152]{1,0:T(8,128)(2,1)S(1)}, u32[]{:S(2)}, u32[]{:S(2)}) collective-permute-start(bf16[16,1152]{1,0:T(8,128)(2,1)S(1)} %get-tuple-element.47.refs_0_), channel_id=1, source_target_pairs={{0,16},{16,32},{32,48},{48,0},{1,17},{17,33},{33,49},{49,1},{2,18}... | collective-permute-start | bytes 110600 | tf_op jit(solution)/shard_map/ppermute | solution.py:27
  34.4 8.8 %collective-permute-start.1 = (bf16[16,1152]{1,0:T(8,128)(2,1)S(1)}, bf16[16,1152]{1,0:T(8,128)(2,1)S(1)}, u32[]{:S(2)}, u32[]{:S(2)}) collective-permute-start(bf16[16,1152]{1,0:T(8,128)(2,1)S(1)} %get-tuple-element.47.refs_0_), channel_id=1, source_target_pairs={{0,32},{16,48},{32,0},{48,16},{1,33},{17,49},{33,1},{49,17},{2,34}... | collective-permute-start | bytes 110600 | tf_op jit(solution)/shard_map/ppermute | solution.py:27
  39.3 5.0 %collective-permute-start.2 = (bf16[16,1152]{1,0:T(8,128)(2,1)S(1)}, bf16[16,1152]{1,0:T(8,128)(2,1)S(1)}, u32[]{:S(2)}, u32[]{:S(2)}) collective-permute-start(bf16[16,1152]{1,0:T(8,128)(2,1)S(1)} %get-tuple-element.47.refs_0_), channel_id=1, source_target_pairs={{0,48},{16,0},{32,16},{48,32},{1,49},{17,1},{33,17},{49,33},{2,50}... | collective-permute-start | bytes 110600 | tf_op jit(solution)/shard_map/ppermute | solution.py:27
  44.9 10.6 %collective-permute-start.3 = (bf16[128,1152]{1,0:T(8,128)(2,1)S(1)}, bf16[128,1152]{1,0:T(8,128)(2,1)S(1)}, u32[]{:S(2)}, u32[]{:S(2)}) collective-permute-start(bf16[128,1152]{1,0:T(8,128)(2,1)S(1)} %get-tuple-element.52.refs_0_), channel_id=1, source_target_pairs={{0,2},{2,4},{4,6},{6,0},{1,3},{3,5},{5,7},{7,1},{8,10},{10,12},{12... | collective-permute-start | bytes 884744 | tf_op jit(solution)/shard_map/ppermute | solution.py:27
  48.0 13.4 %collective-permute-start.4 = (bf16[128,1152]{1,0:T(8,128)(2,1)S(1)}, bf16[128,1152]{1,0:T(8,128)(2,1)S(1)}, u32[]{:S(2)}, u32[]{:S(2)}) collective-permute-start(bf16[128,1152]{1,0:T(8,128)(2,1)S(1)} %get-tuple-element.52.refs_0_), channel_id=1, source_target_pairs={{0,4},{2,6},{4,0},{6,2},{1,5},{3,7},{5,1},{7,3},{8,12},{10,14},{12... | collective-permute-start | bytes 884744 | tf_op jit(solution)/shard_map/ppermute | solution.py:27
  52.4 10.9 %collective-permute-start.5 = (bf16[128,1152]{1,0:T(8,128)(2,1)S(1)}, bf16[128,1152]{1,0:T(8,128)(2,1)S(1)}, u32[]{:S(2)}, u32[]{:S(2)}) collective-permute-start(bf16[128,1152]{1,0:T(8,128)(2,1)S(1)} %get-tuple-element.52.refs_0_), channel_id=1, source_target_pairs={{0,6},{2,0},{4,2},{6,4},{1,7},{3,1},{5,3},{7,5},{8,14},{10,8},{12,... | collective-permute-start | bytes 884744 | tf_op jit(solution)/shard_map/ppermute | solution.py:27
  55.4 13.9 %copy-start.8 = (bf16[128,1152]{1,0:T(8,128)(2,1)}, bf16[128,1152]{1,0:T(8,128)(2,1)S(1)}, u32[]{:S(2)}) copy-start(bf16[128,1152]{1,0:T(8,128)(2,1)S(1)} %collective-permute-done.3.refs_1_) | copy-start | bytes 884740
  61.4 3.0 %copy-start.10 = (bf16[128,1152]{1,0:T(8,128)(2,1)}, bf16[128,1152]{1,0:T(8,128)(2,1)S(1)}, u32[]{:S(2)}) copy-start(bf16[128,1152]{1,0:T(8,128)(2,1)S(1)} %collective-permute-done.4.refs_2_) | copy-start | bytes 884740
  63.2 1.1 copy-start.12
  63.2 29.4 %copy-start.27 = (f32[1152]{0:T(1024)S(1)}, f32[1152]{0:T(1024)}, u32[]{:S(2)}) copy-start(f32[1152]{0:T(1024)} %bias_ref.3) | copy-start | bytes 13828
  64.4 24.5 %collective-permute-start.6 = (bf16[512,1152]{1,0:T(8,128)(2,1)}, bf16[512,1152]{1,0:T(8,128)(2,1)}, u32[]{:S(2)}, u32[]{:S(2)}) collective-permute-start(bf16[512,1152]{1,0:T(8,128)(2,1)} %shard_map.86), channel_id=1, source_target_pairs={{0,1},{1,0},{2,3},{3,2},{4,5},{5,4},{6,7},{7,6},{8,9},{9,8},{10,11... | collective-permute-start | bytes 3538952 | tf_op jit(solution)/shard_map/ppermute | solution.py:233
  69.2 23.4 %copy-start.1 = (bf16[1152,1152]{1,0:T(8,128)(2,1)S(1)}, bf16[1152,1152]{1,0:T(8,128)(2,1)}, u32[]{:S(2)}) copy-start(bf16[1152,1152]{1,0:T(8,128)(2,1)} %weight_ref.3) | copy-start | bytes 7962628
  70.1 14.3 %all-to-all-start.1 = ((bf16[4,64,1152]{2,1,0:T(8,128)(2,1)}), bf16[4,64,1152]{2,1,0:T(8,128)(2,1)S(1)}, u32[]{:S(2)}, u32[]{:S(2)}) async-start(bf16[4,64,1152]{2,1,0:T(8,128)(2,1)} %copy-done.2), calls=%async_computation.1 | async-start | bytes 1179648 | tf_op jit(solution)/shard_map/all_to_all | solution.py:34
  88.8 15.2 %all-to-all-start.2 = ((bf16[4,16,1152]{2,1,0:T(8,128)(2,1)}), bf16[4,16,1152]{2,1,0:T(8,128)(2,1)S(1)}, u32[]{:S(2)}, u32[]{:S(2)}) async-start(bf16[4,16,1152]{2,1,0:T(8,128)(2,1)} %shard_map.85), calls=%async_computation.2 | async-start | bytes 294912 | tf_op jit(solution)/shard_map/all_to_all | solution.py:34
  92.6 1.0 copy-start.9
  95.5 8.5 %copy-start.15 = (f32[16,1152]{1,0:T(8,128)S(1)}, f32[16,1152]{1,0:T(8,128)}, u32[]{:S(2)}) copy-start(f32[16,1152]{1,0:T(8,128)} %copy-done.14) | copy-start | bytes 221188
  101.9 1.1 copy-start.3
  103.0 1.0 copy-start.5
  104.0 27.4 %copy-start.6 = (bf16[1024,512]{1,0:T(8,128)(2,1)S(1)}, bf16[1024,512]{1,0:T(8,128)(2,1)}, u32[]{:S(2)}) copy-start(bf16[1024,512]{1,0:T(8,128)(2,1)} %copy-done.5) | copy-start | bytes 3145732
  117.2 1.3 copy-start.4
  119.2 61.3 %collective-permute-start.7 = (bf16[72,640]{1,0:T(8,128)(2,1)S(1)}, bf16[72,640]{1,0:T(8,128)(2,1)S(1)}, u32[]{:S(2)}, u32[]{:S(2)}) collective-permute-start(bf16[72,640]{1,0:T(8,128)(2,1)S(1)} %get-tuple-element.69), channel_id=1, source_target_pairs={{0,8},{8,0},{1,9},{9,1},{2,10},{10,2},{3,11},{11,3},{4,12},{12,4},... | collective-permute-start | bytes 276488 | tf_op jit(solution)/shard_map/ppermute | solution.py:280
  131.9 48.6 %collective-permute-start.8 = (bf16[72,512]{1,0:T(8,128)(2,1)S(1)}, bf16[72,512]{1,0:T(8,128)(2,1)S(1)}, u32[]{:S(2)}, u32[]{:S(2)}) collective-permute-start(bf16[72,512]{1,0:T(8,128)(2,1)S(1)} %get-tuple-element.70), channel_id=1, source_target_pairs={{0,8},{8,0},{1,9},{9,1},{2,10},{10,2},{3,11},{11,3},{4,12},{12,4},... | collective-permute-start | bytes 221192 | tf_op jit(solution)/shard_map/ppermute | solution.py:280
  (17 other events, 12.6 us)

commit v4 on v3

v4 whole, which is shorter than its diff:
```python
import jax
import jax.numpy as jnp
from jax import lax
from jax.experimental import pallas as pl
from jax.experimental.pallas import tpu as pltpu
from jax.sharding import Mesh, PartitionSpec as P

AXES = ("y", "za", "zb", "zh", "x", "c")
SIZES = (4, 4, 4, 2, 4, 2)
VMEM_LIMIT = 60 * 1024 * 1024
COEFF = 0.7978845608
CUBIC = 0.044715
BF16, F32 = jnp.bfloat16, jnp.float32


def size_of(*names):
    count = 1
    for name in names:
        count *= SIZES[AXES.index(name)]
    return count


def from_others(value, axis):
    count = size_of(axis)
    moved = [
        lax.ppermute(value, axis, [(i, (i + k) % count) for i in range(count)])
        for k in range(1, count)
    ]
    return [value] + moved


def exchange(copies, *axes):
    return lax.all_to_all(copies, axes, split_axis=0, concat_axis=0, tiled=True)


def local(body, outs, *args, smem=(), scratch=(), flops=0, moved=0):
    def whole(shape, space):
        return pl.BlockSpec(shape, lambda i: (0,) * len(shape), memory_space=space)

    return pl.pallas_call(
        body,
        grid=(1,),
        out_shape=[jax.ShapeDtypeStruct(shape, dtype) for shape, dtype in outs],
        in_specs=[whole(v.shape, pltpu.SMEM if i in smem else None) for i, v in enumerate(args)],
        out_specs=[whole(shape, None) for shape, _ in outs],
        scratch_shapes=[pltpu.VMEM(shape, dtype) for shape, dtype in scratch],
        compiler_params=pltpu.CompilerParams(vmem_limit_bytes=VMEM_LIMIT),
        cost_estimate=pl.CostEstimate(flops=flops, bytes_accessed=moved, transcendentals=0),
    )(*args)


def first_kernel(count_ref, image_ref, token_ref, copies_ref, live_ref):
    images = image_ref[...].astype(F32)
    norm = jnp.sqrt(jnp.sum(images * images, axis=-1, keepdims=True) + 1e-06)
    image = (images / norm).astype(BF16)
    for k in range(copies_ref.shape[0]):
        copies_ref[k] = image
    rows = image_ref.shape[0]
    length = token_ref.shape[0] // rows
    slot = lax.broadcasted_iota(jnp.int32, (length, 1), 0)
    lives = [(slot < count_ref[p]).astype(F32) for p in range(rows)]
    live_ref[...] = token_ref[...] * jnp.concatenate(lives, axis=0).astype(BF16)


def layer(token_ref, gain_ref, weight_ref, bias_ref, slope_ref, column_ref):
    width = token_ref.shape[1]
    values = token_ref[...].astype(F32)
    center = jnp.mean(values, axis=-1, keepdims=True)
    spread = jnp.mean((values - center) ** 2, axis=-1, keepdims=True)
    gain = gain_ref[...].reshape(1, width)
    normed = ((values - center) * lax.rsqrt(spread + 1e-06) * gain).astype(BF16)
    pre = jnp.dot(normed, weight_ref[...], preferred_element_type=F32)
    pre = pre + bias_ref[...].reshape(1, width)
    square = pre * pre
    hyper = jnp.tanh(COEFF * (pre + CUBIC * pre * square))
    slope = 0.5 * (1.0 + hyper) + 0.5 * pre * (1.0 - hyper * hyper) * COEFF * (
        1.0 + 3.0 * CUBIC * square
    )
    slope_ref[...] = slope.astype(BF16)
    half, cores = column_ref.shape[0], size_of("c")
    part = half // size_of("x", "c")
    row = lax.broadcasted_iota(jnp.int32, (half, width), 0)
    source = lax.broadcasted_iota(jnp.int32, (half, width), 1) - lax.axis_index("zh") * half
    core = lax.axis_index("c")
    rest = half // cores
    mine = row < rest
    place = jnp.where(mine, row, row - rest)
    group = place * 0
    for k in range(1, size_of("x")):
        group = group + jnp.where(place >= k * part, 1, 0)
    wanted = (group * cores + jnp.where(mine, core, 1 - core)) * part + place - group * part
    pick = jnp.where(source == wanted, 1.0, 0.0).astype(BF16)
    columns = lax.dot_general(pick, normed, (((1,), (1,)), ((), ())), preferred_element_type=F32)
    column_ref[...] = columns.astype(BF16)
    return 0.5 * pre * (1.0 + hyper)


def front_kernel(
    count_ref, token_ref, gain_ref, weight_ref, bias_ref,
    unit_ref, pooled_ref, inverse_ref, slope_ref, column_ref, act_ref,
):
    rows = pooled_ref.shape[0]
    length = token_ref.shape[0] // rows
    act_ref[...] = layer(token_ref, gain_ref, weight_ref, bias_ref, slope_ref, column_ref)
    slot = lax.broadcasted_iota(jnp.int32, (length, 1), 0)
    for p in range(rows):
        live = (slot < count_ref[p]).astype(F32)
        inverse = 1.0 / jnp.full((length, 1), count_ref[p], jnp.int32).astype(F32)
        part = act_ref[p * length : (p + 1) * length, :] * (live * inverse)
        pooled_ref[p : p + 1, :] = jnp.sum(part, axis=0, keepdims=True)
        inverse_ref[p : p + 1, :] = jnp.broadcast_to(inverse[:1], (1, inverse_ref.shape[1]))
    pooled = pooled_ref[...]
    size = jnp.sqrt(jnp.sum(pooled * pooled, axis=-1, keepdims=True) + 1e-06)
    unit_ref[...] = (pooled / size).astype(BF16)


def partner_kernel(token_ref, gain_ref, weight_ref, bias_ref, slope_ref, column_ref):
    layer(token_ref, gain_ref, weight_ref, bias_ref, slope_ref, column_ref)


def copies_kernel(image_ref, out_ref):
    rows = image_ref.shape[1]
    for k in range(out_ref.shape[0]):
        for j in range(image_ref.shape[0]):
            out_ref[k, j * rows : (j + 1) * rows, :] = image_ref[j]


def logit_kernel(scale_ref, shift_ref, *refs):
    *unit_refs, image_ref, out_ref = refs
    near, rows, width = out_ref.shape
    group = rows * size_of("y", "za", "zb")
    units = jnp.concatenate([ref[...] for ref in unit_refs], axis=0)
    images = image_ref[...]
    temper = jnp.exp(jnp.full((1, 1), scale_ref[0], F32))
    cosine = lax.dot_general(units, images, (((1,), (1,)), ((), ())), preferred_element_type=F32)
    logit = temper * cosine + shift_ref[0]
    unit_at = lax.broadcasted_iota(jnp.int32, cosine.shape, 0)
    image_at = lax.broadcasted_iota(jnp.int32, cosine.shape, 1)
    offset = (lax.axis_index("y") * size_of("za") + lax.axis_index("za")) * rows
    label = jnp.where((unit_at == image_at - offset) & (unit_at < rows), 1.0, -1.0)
    dlogit = (-label / (1.0 + jnp.exp(label * logit)) / group).astype(BF16)
    terms = jnp.dot(dlogit, images, preferred_element_type=F32).astype(BF16)
    for k in range(near):
        owner = lax.rem(lax.axis_index("zb") + near - k, near)
        out_ref[owner] = terms[k * rows : (k + 1) * rows]


def share_kernel(scale_ref, term_ref, pooled_ref, inverse_ref, out_ref):
    temper = jnp.exp(jnp.full((1, 1), scale_ref[0], F32))
    pooled = pooled_ref[...]
    size = jnp.sqrt(jnp.sum(pooled * pooled, axis=-1, keepdims=True) + 1e-06)
    unit = pooled / size
    total = term_ref[0].astype(F32)
    for k in range(1, term_ref.shape[0]):
        total = total + term_ref[k].astype(F32)
    dunit = temper * total
    dpooled = (dunit - unit * jnp.sum(unit * dunit, axis=-1, keepdims=True)) / size
    out_ref[...] = (dpooled * inverse_ref[:, :1]).astype(BF16)


def grad_kernel(*refs):
    *in_refs, keep_ref, send_ref = refs
    rest = keep_ref.shape[0]
    total = None
    for share_ref, slope_ref, column_ref in (in_refs[:3], in_refs[3:]):
        rows, width = share_ref.shape
        flat = slope_ref.shape[0]
        share = share_ref[...].astype(F32)
        share = jnp.broadcast_to(share[:, None, :], (rows, flat // rows, width)).reshape(flat, width)
        dpre = (share * slope_ref[...].astype(F32)).astype(BF16)
        grad = jnp.dot(column_ref[...], dpre, preferred_element_type=F32)
        total = grad if total is None else total + grad
    keep_ref[...] = total[:rest]
    send_ref[...] = total[rest:].astype(BF16)


def core_kernel(keep_ref, away_ref, out_ref):
    total = keep_ref[...] + away_ref[...].astype(F32)
    part = out_ref.shape[1]
    for k in range(out_ref.shape[0]):
        out_ref[k] = total[k * part : (k + 1) * part].astype(BF16)


def sum_kernel(in_ref, out_ref):
    total = in_ref[0].astype(F32)
    for k in range(1, in_ref.shape[0]):
        total = total + in_ref[k].astype(F32)
    out_ref[0] = total


def on_device(
    tokens, token_count, image_embed, norm_gain, head_weight, head_bias, logit_scale, logit_bias
):
    rows, length, width = tokens.shape
    part = width // size_of("zh", "x", "c")
    flat = rows * length
    half = width // 2
    swap = [(0, 1), (1, 0)]

    image, alive = local(
        first_kernel,
        [((size_of("za"), rows, width), BF16), ((flat, width), BF16)],
        token_count,
        image_embed,
        tokens.reshape(flat, width),
        smem=(0,),
    )
    partner = lax.ppermute(alive, "zh", swap)

    def own(image, alive, norm_gain, head_weight, head_bias):
        some_images = exchange(image, "za")
        unit, pooled, inverse, slope, columns = local(
            front_kernel,
            [
                ((rows, width), BF16),
                ((rows, width), F32),
                ((rows, 128), F32),
                ((flat, width), BF16),
                ((half, flat), BF16),
            ],
            token_count,
            alive,
            norm_gain,
            head_weight,
            head_bias,
            smem=(0,),
            scratch=[((flat, width), F32)],
            flops=2 * flat * width * width,
            moved=2 * width * width,
        )
        units = from_others(unit, "zb")
        units, some_images = lax.optimization_barrier((units, some_images))
        (copies,) = local(
            copies_kernel, [((size_of("y"), size_of("za") * rows, width), BF16)], some_images
        )
        all_images = exchange(copies, "y").reshape(-1, width)
        (terms,) = local(
            logit_kernel,
            [((size_of("zb"), rows, width), BF16)],
            logit_scale,
            logit_bias,
            *units,
            all_images,
            smem=(0, 1),
        )
        terms = exchange(terms, "zb")
        (share,) = local(
            share_kernel, [((rows, width), BF16)], logit_scale, terms, pooled, inverse, smem=(0,)
        )
        return share, slope, columns

    def none(*_):
        return (
            jnp.zeros((rows, width), BF16),
            jnp.zeros((flat, width), BF16),
            jnp.zeros((half, flat), BF16),
        )

    share, slope, columns = lax.cond(
        token_count[0] > 0, own, none, image, alive, norm_gain, head_weight, head_bias
    )
    away_share = lax.ppermute(share, "zh", swap)
    away_slope, away_columns = local(
        partner_kernel,
        [((flat, width), BF16), ((half, flat), BF16)],
        partner,
        norm_gain,
        head_weight,
        head_bias,
    )
    keep, send = local(
        grad_kernel,
        [((half // 2, width), F32), ((half // 2, width), BF16)],
        share,
        slope,
        columns,
        away_share,
        away_slope,
        away_columns,
    )
    away = lax.ppermute(send, "c", swap)
    (parts,) = local(core_kernel, [((size_of("x"), part, width), BF16)], keep, away)
    (grad,) = local(sum_kernel, [((1, part, width), F32)], exchange(parts, "x"))
    return grad


def solution(mesh):
    fine = Mesh(mesh.devices.reshape(SIZES), AXES)
    in_specs = (
        P(AXES, None, None),
        P(AXES),
        P(AXES, None),
        P(),
        P(),
        P(),
        P(),
        P(),
    )
    out_specs = P(("y", "za", "zb"), ("zh", "x", "c"), None)
    return jax.shard_map(
        on_device, mesh=fine, in_specs=in_specs, out_specs=out_specs, check_vma=False
    )
```

time: 183 us -> 183 us (level)
  blocking collectives: 13 us -> 38 us
  starting transfers between devices: 80.4 us -> 56.7 us
  local copies, waits for them, and re-layouts: 18.8 us -> 2.82 us
  Pallas kernels: 13.4 us -> 24.5 us
  waiting for transfers between devices: 54.2 us -> 59.6 us
    ppermute x6 -> x3, waiting for transfers between devices: 8.29 us -> 38 us  [from_others(): lax.ppermute(value, axis, [(i, (i + k) % count) for i in range(count)])]
    all_to_all x1 -> x3, blocking collectives: 13 us -> 38 us  [exchange(): return lax.all_to_all(copies, axes, split_axis=0, concat_axis=0, tiled=True)]
    all_to_all x3 -> x1, starting transfers between devices: 30.3 us -> 7.02 us  [exchange(): return lax.all_to_all(copies, axes, split_axis=0, concat_axis=0, tiled=True)]
    ppermute x3, waiting for transfers between devices: 37.2 us -> 14.5 us  [the longest x1 12.6 us: on_device(): away_share = lax.ppermute(share, 'zh', swap)]
    unnamed x58 -> x6, local copies, waits for them, and re-layouts: 18.8 us -> 2.16 us
    ppermute x6 -> x3, starting transfers between devices: 21.6 us -> 8.37 us  [from_others(): lax.ppermute(value, axis, [(i, (i + k) % count) for i in range(count)])]
    ppermute x3, starting transfers between devices: 28.5 us -> 41.3 us  [the longest x1 29.5 us: on_device(): partner = lax.ppermute(alive, 'zh', swap)]
    pallas_call x10 -> x9, Pallas kernels: 13.4 us -> 24.5 us  [local(): pl.pallas_call(body, grid=(1,), out_shape=[jax.ShapeDtypeStruct(shape, dt...]
  transfers between devices with their start and end apart: 12 -> 7, of which waited for: 5 -> 6; matrix products, arithmetic and copies ran while one was open for 0% -> 0% of each run, Pallas kernels for 5% -> 8%
where the time goes in v4:
time: 183 us; the launch traced here: 182 us
  waiting for transfers between devices  59.6 us (33%)
  starting transfers between devices  56.7 us (31%)
  blocking collectives  38 us (21%)
  Pallas kernels  24.5 us (13%)
  local copies, waits for them, and re-layouts  2.82 us (2%)
    all_to_all x3, blocking collectives, exchange(): return lax.all_to_all(copies, axes, split_axis=0, concat_axis=0, tiled=True)  38 us
    ppermute x3, waiting for transfers between devices, from_others(): lax.ppermute(value, axis, [(i, (i + k) % count) for i in range(count)])  38 us
    ppermute x1, starting transfers between devices, on_device(): partner = lax.ppermute(alive, 'zh', swap)  29.5 us
    pallas_call x9, Pallas kernels, local(): pl.pallas_call(body, grid=(1,), out_shape=[jax.ShapeDtypeStruct(shape, dt...  24.5 us
    ppermute x1, waiting for transfers between devices, on_device(): away_share = lax.ppermute(share, 'zh', swap)  12.6 us
    ppermute x3, starting transfers between devices, from_others(): lax.ppermute(value, axis, [(i, (i + k) % count) for i in range(count)])  8.37 us
    all_to_all x1, waiting for transfers between devices, exchange(): return lax.all_to_all(copies, axes, split_axis=0, concat_axis=0, tiled=True)  7.13 us
    all_to_all x1, starting transfers between devices, exchange(): return lax.all_to_all(copies, axes, split_axis=0, concat_axis=0, tiled=True)  7.02 us
  transfers between devices with their start and end apart: 7, of which 6 were waited for; matrix products, arithmetic and copies ran while one was open for 0% of the time, Pallas kernels for 8%

profile of v4, /device:TPU:1, one launch (start us, length us, event | category | flops | bytes accessed | tf_op | source)
XLA Modules:
  0.0 182.4 jit_solution(12416508420874771441)
XLA Ops:
  0.0 1.8 %shard_map.84 = (bf16[4,16,1152]{2,1,0:T(8,128)(2,1)}, bf16[128,1152]{1,0:T(8,128)(2,1)}) custom-call(s32[16]{0:T(128)} %count_ref.1, bf16[16,1152]{1,0:T(8,128)(2,1)} %image_ref.1, bf16[128,1152]{1,0:T(8,128)(2,1)} %bitcast.5), custom_call_target="tpu_custom_call" | custom-call | tf_op jit(solution)/shard_map/pallas_call | solution.py:40
  1.8 29.5 %collective-permute-start.4 = (bf16[128,1152]{1,0:T(8,128)(2,1)}, bf16[128,1152]{1,0:T(8,128)(2,1)S(1)}, u32[]{:S(2)}, u32[]{:S(2)}) collective-permute-start(bf16[128,1152]{1,0:T(8,128)(2,1)} %get-tuple-element.48), channel_id=1, source_target_pairs={{0,8},{8,0},{1,9},{9,1},{2,10},{10,2},{3,11},{11,3},{4,12},{12,4},... | collective-permute-start | bytes 884744 | tf_op jit(solution)/shard_map/ppermute | solution.py:208
  32.0 95.8 %conditional.1 = (bf16[16,1152]{1,0:T(8,128)(2,1)S(1)}, bf16[128,1152]{1,0:T(8,128)(2,1)S(1)}, bf16[576,128]{1,0:T(8,128)(2,1)S(1)}) conditional(s32[]{:T(128)} %bitcast.1, () %tuple.14, (s32[16]{0:T(128)}, bf16[128,1152]{1,0:T(8,128)(2,1)}, f32[1152]{0:T(1024)}, bf16[1152,1152]{1,0:T(8,128)(2,1)}, f32[1152]{0:T(1024)}, ...), branch_computations={%region_0.0_spmd, %region_1.0_spmd} | conditional | flops 339738624 | bytes 6045984 | solution.py:259
  32.0 7.0 %all-to-all-start = ((bf16[4,16,1152]{2,1,0:T(8,128)(2,1)}), bf16[4,16,1152]{2,1,0:T(8,128)(2,1)S(1)}, u32[]{:S(2)}, u32[]{:S(2)}) async-start(bf16[4,16,1152]{2,1,0:T(8,128)(2,1)} %get-tuple-element.29), calls=%async_computation | async-start | bytes 294912 | tf_op jit(solution)/shard_map/cond/branch_1_fun/all_to_all | solution.py:33
  39.0 3.9 %branch_1_fun.4 = (bf16[16,1152]{1,0:T(8,128)(2,1)}, f32[16,1152]{1,0:T(8,128)}, f32[16,128]{1,0:T(8,128)}, bf16[128,1152]{1,0:T(8,128)(2,1)S(1)}, bf16[576,128]{1,0:T(8,128)(2,1)S(1)}) custom-call(s32[16]{0:T(128)} %get-tuple-element.23.count_ref, bf16[128,1152]{1,0:T(8,128)(2,1)} %get-tuple-element.24.token_ref, f32[1152]{0:T(1024)} %get-tuple-element.25.gain_ref, ...), custom_call_target="tpu_custom_call" | custom-call | flops 339738624 | bytes 2654208 | tf_op jit(solution)/shard_map/cond/branch_1_fun/pallas_call | solution.py:40
  43.0 3.5 %collective-permute-start.2 = (bf16[16,1152]{1,0:T(8,128)(2,1)}, bf16[16,1152]{1,0:T(8,128)(2,1)S(1)}, u32[]{:S(2)}, u32[]{:S(2)}) collective-permute-start(bf16[16,1152]{1,0:T(8,128)(2,1)} %get-tuple-element.30.refs_0_), channel_id=1, source_target_pairs={{0,48},{16,0},{32,16},{48,32},{1,49},{17,1},{33,17},{49,33},{2,50}... | collective-permute-start | bytes 110600 | tf_op jit(solution)/shard_map/cond/branch_1_fun/ppermute | solution.py:26
  46.5 2.2 %collective-permute-start.1 = (bf16[16,1152]{1,0:T(8,128)(2,1)}, bf16[16,1152]{1,0:T(8,128)(2,1)S(1)}, u32[]{:S(2)}, u32[]{:S(2)}) collective-permute-start(bf16[16,1152]{1,0:T(8,128)(2,1)} %get-tuple-element.30.refs_0_), channel_id=1, source_target_pairs={{0,32},{16,48},{32,0},{48,16},{1,33},{17,49},{33,1},{49,17},{2,34}... | collective-permute-start | bytes 110600 | tf_op jit(solution)/shard_map/cond/branch_1_fun/ppermute | solution.py:26
  48.7 2.6 %collective-permute-start = (bf16[16,1152]{1,0:T(8,128)(2,1)}, bf16[16,1152]{1,0:T(8,128)(2,1)S(1)}, u32[]{:S(2)}, u32[]{:S(2)}) collective-permute-start(bf16[16,1152]{1,0:T(8,128)(2,1)} %get-tuple-element.30.refs_0_), channel_id=1, source_target_pairs={{0,16},{16,32},{32,48},{48,0},{1,17},{17,33},{33,49},{49,1},{2,18}... | collective-permute-start | bytes 110600 | tf_op jit(solution)/shard_map/cond/branch_1_fun/ppermute | solution.py:26
  51.4 25.1 %collective-permute-done.2.refs_3_ = bf16[16,1152]{1,0:T(8,128)(2,1)S(1)} collective-permute-done((bf16[16,1152]{1,0:T(8,128)(2,1)}, bf16[16,1152]{1,0:T(8,128)(2,1)S(1)}, u32[]{:S(2)}, u32[]{:S(2)}) %collective-permute-start.2) | collective-permute-done | bytes 36896 | tf_op jit(solution)/shard_map/cond/branch_1_fun/ppermute | solution.py:26
  76.5 7.3 %collective-permute-done.1.refs_2_ = bf16[16,1152]{1,0:T(8,128)(2,1)S(1)} collective-permute-done((bf16[16,1152]{1,0:T(8,128)(2,1)}, bf16[16,1152]{1,0:T(8,128)(2,1)S(1)}, u32[]{:S(2)}, u32[]{:S(2)}) %collective-permute-start.1) | collective-permute-done | bytes 36896 | tf_op jit(solution)/shard_map/cond/branch_1_fun/ppermute | solution.py:26
  83.8 5.5 %collective-permute-done.refs_1_ = bf16[16,1152]{1,0:T(8,128)(2,1)S(1)} collective-permute-done((bf16[16,1152]{1,0:T(8,128)(2,1)}, bf16[16,1152]{1,0:T(8,128)(2,1)S(1)}, u32[]{:S(2)}, u32[]{:S(2)}) %collective-permute-start) | collective-permute-done | bytes 36896 | tf_op jit(solution)/shard_map/cond/branch_1_fun/ppermute | solution.py:26
  89.4 7.1 %all-to-all-done.image_ref = bf16[4,16,1152]{2,1,0:T(8,128)(2,1)S(1)} async-done(((bf16[4,16,1152]{2,1,0:T(8,128)(2,1)}), bf16[4,16,1152]{2,1,0:T(8,128)(2,1)S(1)}, u32[]{:S(2)}, u32[]{:S(2)}) %all-to-all-start) | async-done | bytes 147488 | tf_op jit(solution)/shard_map/cond/branch_1_fun/all_to_all | solution.py:33
  98.9 13.8 %all_to_all.17 = bf16[4,64,1152]{2,1,0:T(8,128)(2,1)} all-to-all(bf16[4,64,1152]{2,1,0:T(8,128)(2,1)} %branch_1_fun.5), channel_id=1, replica_groups=mesh['y'=4,'za'=4,'zb'=4,'zh'=2,'x'=4,'c'=2] {'y'}, dimensions={0} | all-to-all | bytes 1179648 | tf_op jit(solution)/shard_map/cond/branch_1_fun/all_to_all | solution.py:33
  112.7 3.8 %branch_1_fun.6 = bf16[4,16,1152]{2,1,0:T(8,128)(2,1)} custom-call(f32[1]{0:T(128)} %get-tuple-element.59.scale_ref, f32[1]{0:T(128)} %get-tuple-element.60.shift_ref, bf16[16,1152]{1,0:T(8,128)(2,1)} %get-tuple-element.30.refs_0_, bf16[16,1152]{1,0:T(8,128)(2,1)} %copy-done.5, bf16[16,1152]{1,0:T(8,128)(2,1)} %copy-done.4, bf16[16,1152]{1,0:T(8,128)(2,1)} %copy-done.3, ...), custom_call_target="tpu_custom_call" | custom-call | tf_op jit(solution)/shard_map/cond/branch_1_fun/pallas_call | solution.py:40
  116.5 9.5 %all_to_all.18.term_ref = bf16[4,16,1152]{2,1,0:T(8,128)(2,1)} all-to-all(bf16[4,16,1152]{2,1,0:T(8,128)(2,1)} %branch_1_fun.6), channel_id=1, replica_groups=mesh['y'=4,'za'=4,'zb'=4,'zh'=2,'x'=4,'c'=2] {'zb'}, dimensions={0} | all-to-all | bytes 294912 | tf_op jit(solution)/shard_map/cond/branch_1_fun/all_to_all | solution.py:33
  127.8 5.8 %collective-permute-start.3 = (bf16[16,1152]{1,0:T(8,128)(2,1)S(1)}, bf16[16,1152]{1,0:T(8,128)(2,1)S(1)}, u32[]{:S(2)}, u32[]{:S(2)}) collective-permute-start(bf16[16,1152]{1,0:T(8,128)(2,1)S(1)} %get-tuple-element.50.refs_0_), channel_id=1, source_target_pairs={{0,8},{8,0},{1,9},{9,1},{2,10},{10,2},{3,11},{11,3},{4,12},{12,4},... | collective-permute-start | bytes 110600 | tf_op jit(solution)/shard_map/ppermute | solution.py:262
  134.3 3.9 %shard_map.85 = (bf16[128,1152]{1,0:T(8,128)(2,1)}, bf16[576,128]{1,0:T(8,128)(2,1)}) custom-call(bf16[128,1152]{1,0:T(8,128)(2,1)} %copy-done.2, f32[1152]{0:T(1024)} %gain_ref.1, bf16[1152,1152]{1,0:T(8,128)(2,1)} %weight_ref.1, f32[1152]{0:T(1024)} %bias_ref.1), custom_call_target="tpu_custom_call" | custom-call | tf_op jit(solution)/shard_map/pallas_call | solution.py:40
  138.2 12.6 %collective-permute-done.3.refs_3_ = bf16[16,1152]{1,0:T(8,128)(2,1)S(1)} collective-permute-done((bf16[16,1152]{1,0:T(8,128)(2,1)S(1)}, bf16[16,1152]{1,0:T(8,128)(2,1)S(1)}, u32[]{:S(2)}, u32[]{:S(2)}) %collective-permute-start.3) | collective-permute-done | bytes 36896 | tf_op jit(solution)/shard_map/ppermute | solution.py:262
  151.4 3.1 %shard_map.86 = (f32[288,1152]{1,0:T(8,128)}, bf16[288,1152]{1,0:T(8,128)(2,1)}) custom-call(bf16[16,1152]{1,0:T(8,128)(2,1)S(1)} %get-tuple-element.50.refs_0_, bf16[128,1152]{1,0:T(8,128)(2,1)S(1)} %get-tuple-element.51.refs_1_, bf16[576,128]{1,0:T(8,128)(2,1)S(1)} %get-tuple-element.52.refs_2_, bf16[16,1152]{1,0:T(8,128)(2,1)} %copy-done.6, ...), custom_call_target="tpu_custom_call" | custom-call | tf_op jit(solution)/shard_map/pallas_call | solution.py:40
  154.6 6.0 %collective-permute-start.5 = (bf16[288,1152]{1,0:T(8,128)(2,1)}, bf16[288,1152]{1,0:T(8,128)(2,1)S(1)}, u32[]{:S(2)}, u32[]{:S(2)}) collective-permute-start(bf16[288,1152]{1,0:T(8,128)(2,1)} %get-tuple-element.56), channel_id=1, source_target_pairs={{0,1},{1,0},{2,3},{3,2},{4,5},{5,4},{6,7},{7,6},{8,9},{9,8},{10,11... | collective-permute-start | bytes 1990664 | tf_op jit(solution)/shard_map/ppermute | solution.py:281
  160.6 1.9 %collective-permute-done.5.away_ref = bf16[288,1152]{1,0:T(8,128)(2,1)S(1)} collective-permute-done((bf16[288,1152]{1,0:T(8,128)(2,1)}, bf16[288,1152]{1,0:T(8,128)(2,1)S(1)}, u32[]{:S(2)}, u32[]{:S(2)}) %collective-permute-start.5) | collective-permute-done | bytes 663584 | tf_op jit(solution)/shard_map/ppermute | solution.py:281
  163.3 2.4 %shard_map.87 = bf16[4,72,1152]{2,1,0:T(8,128)(2,1)} custom-call(f32[288,1152]{1,0:T(8,128)} %get-tuple-element.55.keep_ref, bf16[288,1152]{1,0:T(8,128)(2,1)} %copy-done), custom_call_target="tpu_custom_call" | custom-call | tf_op jit(solution)/shard_map/pallas_call | solution.py:40
  165.8 14.7 %all_to_all.19.in_ref = bf16[4,72,1152]{2,1,0:T(8,128)(2,1)} all-to-all(bf16[4,72,1152]{2,1,0:T(8,128)(2,1)} %shard_map.87), channel_id=1, replica_groups=mesh['y'=4,'za'=4,'zb'=4,'zh'=2,'x'=4,'c'=2] {'x'}, dimensions={0} | all-to-all | bytes 1327104 | tf_op jit(solution)/shard_map/all_to_all | solution.py:33
  180.5 1.9 %shard_map.88 = f32[1,72,1152]{2,1,0:T(8,128)} custom-call(bf16[4,72,1152]{2,1,0:T(8,128)(2,1)} %all_to_all.19.in_ref), custom_call_target="tpu_custom_call" | custom-call | tf_op jit(solution)/shard_map/pallas_call | solution.py:40
  (17 shorter events, 6.4 us)
Async XLA Ops:
  1.8 131.7 %collective-permute-start.4 = (bf16[128,1152]{1,0:T(8,128)(2,1)}, bf16[128,1152]{1,0:T(8,128)(2,1)S(1)}, u32[]{:S(2)}, u32[]{:S(2)}) collective-permute-start(bf16[128,1152]{1,0:T(8,128)(2,1)} %get-tuple-element.48), channel_id=1, source_target_pairs={{0,8},{8,0},{1,9},{9,1},{2,10},{10,2},{3,11},{11,3},{4,12},{12,4},... | collective-permute-start | bytes 884744 | tf_op jit(solution)/shard_map/ppermute | solution.py:208
  32.0 64.5 %all-to-all-start = ((bf16[4,16,1152]{2,1,0:T(8,128)(2,1)}), bf16[4,16,1152]{2,1,0:T(8,128)(2,1)S(1)}, u32[]{:S(2)}, u32[]{:S(2)}) async-start(bf16[4,16,1152]{2,1,0:T(8,128)(2,1)} %get-tuple-element.29), calls=%async_computation | async-start | bytes 294912 | tf_op jit(solution)/shard_map/cond/branch_1_fun/all_to_all | solution.py:33
  43.0 33.5 %collective-permute-start.2 = (bf16[16,1152]{1,0:T(8,128)(2,1)}, bf16[16,1152]{1,0:T(8,128)(2,1)S(1)}, u32[]{:S(2)}, u32[]{:S(2)}) collective-permute-start(bf16[16,1152]{1,0:T(8,128)(2,1)} %get-tuple-element.30.refs_0_), channel_id=1, source_target_pairs={{0,48},{16,0},{32,16},{48,32},{1,49},{17,1},{33,17},{49,33},{2,50}... | collective-permute-start | bytes 110600 | tf_op jit(solution)/shard_map/cond/branch_1_fun/ppermute | solution.py:26
  46.5 37.3 %collective-permute-start.1 = (bf16[16,1152]{1,0:T(8,128)(2,1)}, bf16[16,1152]{1,0:T(8,128)(2,1)S(1)}, u32[]{:S(2)}, u32[]{:S(2)}) collective-permute-start(bf16[16,1152]{1,0:T(8,128)(2,1)} %get-tuple-element.30.refs_0_), channel_id=1, source_target_pairs={{0,32},{16,48},{32,0},{48,16},{1,33},{17,49},{33,1},{49,17},{2,34}... | collective-permute-start | bytes 110600 | tf_op jit(solution)/shard_map/cond/branch_1_fun/ppermute | solution.py:26
  48.7 40.6 %collective-permute-start = (bf16[16,1152]{1,0:T(8,128)(2,1)}, bf16[16,1152]{1,0:T(8,128)(2,1)S(1)}, u32[]{:S(2)}, u32[]{:S(2)}) collective-permute-start(bf16[16,1152]{1,0:T(8,128)(2,1)} %get-tuple-element.30.refs_0_), channel_id=1, source_target_pairs={{0,16},{16,32},{32,48},{48,0},{1,17},{17,33},{33,49},{49,1},{2,18}... | collective-permute-start | bytes 110600 | tf_op jit(solution)/shard_map/cond/branch_1_fun/ppermute | solution.py:26
  76.5 36.2 %copy-start.3 = (bf16[16,1152]{1,0:T(8,128)(2,1)}, bf16[16,1152]{1,0:T(8,128)(2,1)S(1)}, u32[]{:S(2)}) copy-start(bf16[16,1152]{1,0:T(8,128)(2,1)S(1)} %collective-permute-done.2.refs_3_) | copy-start | bytes 110596 | tf_op jit(solution)/shard_map/cond
  83.8 28.9 %copy-start.4 = (bf16[16,1152]{1,0:T(8,128)(2,1)}, bf16[16,1152]{1,0:T(8,128)(2,1)S(1)}, u32[]{:S(2)}) copy-start(bf16[16,1152]{1,0:T(8,128)(2,1)S(1)} %collective-permute-done.1.refs_2_) | copy-start | bytes 110596 | tf_op jit(solution)/shard_map/cond
  89.4 23.3 %copy-start.5 = (bf16[16,1152]{1,0:T(8,128)(2,1)}, bf16[16,1152]{1,0:T(8,128)(2,1)S(1)}, u32[]{:S(2)}) copy-start(bf16[16,1152]{1,0:T(8,128)(2,1)S(1)} %collective-permute-done.refs_1_) | copy-start | bytes 110596 | tf_op jit(solution)/shard_map/cond
  96.5 0.6 copy-start.1
  127.8 23.0 %collective-permute-start.3 = (bf16[16,1152]{1,0:T(8,128)(2,1)S(1)}, bf16[16,1152]{1,0:T(8,128)(2,1)S(1)}, u32[]{:S(2)}, u32[]{:S(2)}) collective-permute-start(bf16[16,1152]{1,0:T(8,128)(2,1)S(1)} %get-tuple-element.50.refs_0_), channel_id=1, source_target_pairs={{0,8},{8,0},{1,9},{9,1},{2,10},{10,2},{3,11},{11,3},{4,12},{12,4},... | collective-permute-start | bytes 110600 | tf_op jit(solution)/shard_map/ppermute | solution.py:262
  133.6 0.7 copy-start.2
  150.8 0.6 copy-start.6
  154.6 8.0 %collective-permute-start.5 = (bf16[288,1152]{1,0:T(8,128)(2,1)}, bf16[288,1152]{1,0:T(8,128)(2,1)S(1)}, u32[]{:S(2)}, u32[]{:S(2)}) collective-permute-start(bf16[288,1152]{1,0:T(8,128)(2,1)} %get-tuple-element.56), channel_id=1, source_target_pairs={{0,1},{1,0},{2,3},{3,2},{4,5},{5,4},{6,7},{7,6},{8,9},{9,8},{10,11... | collective-permute-start | bytes 1990664 | tf_op jit(solution)/shard_map/ppermute | solution.py:281
  162.5 0.8 copy-start

commit v5 on v3

v5 whole, which is shorter than its diff:
```python
import jax
import jax.numpy as jnp
from jax import lax
from jax.experimental import pallas as pl
from jax.experimental.pallas import tpu as pltpu
from jax.sharding import Mesh, PartitionSpec as P

AXES = ("y", "za", "zb", "zh", "x", "c")
SIZES = (4, 4, 4, 2, 4, 2)
VMEM_LIMIT = 60 * 1024 * 1024
COEFF = 0.7978845608
CUBIC = 0.044715
BF16, F32 = jnp.bfloat16, jnp.float32


def size_of(*names):
    count = 1
    for name in names:
        count *= SIZES[AXES.index(name)]
    return count


def from_others(value, axis):
    count = size_of(axis)
    moved = [
        lax.ppermute(value, axis, [(i, (i + k) % count) for i in range(count)])
        for k in range(1, count)
    ]
    return [value] + moved


def exchange(copies, *axes):
    return lax.all_to_all(copies, axes, split_axis=0, concat_axis=0, tiled=True)


def local(body, outs, *args, smem=(), scratch=(), flops=0, moved=0):
    def whole(shape, space):
        return pl.BlockSpec(shape, lambda i: (0,) * len(shape), memory_space=space)

    return pl.pallas_call(
        body,
        grid=(1,),
        out_shape=[jax.ShapeDtypeStruct(shape, dtype) for shape, dtype in outs],
        in_specs=[whole(v.shape, pltpu.SMEM if i in smem else None) for i, v in enumerate(args)],
        out_specs=[whole(shape, None) for shape, _ in outs],
        scratch_shapes=[pltpu.VMEM(shape, dtype) for shape, dtype in scratch],
        compiler_params=pltpu.CompilerParams(vmem_limit_bytes=VMEM_LIMIT),
        cost_estimate=pl.CostEstimate(flops=flops, bytes_accessed=moved, transcendentals=0),
    )(*args)


def image_kernel(image_ref, copies_ref):
    images = image_ref[...].astype(F32)
    norm = jnp.sqrt(jnp.sum(images * images, axis=-1, keepdims=True) + 1e-06)
    image = (images / norm).astype(BF16)
    for k in range(copies_ref.shape[0]):
        copies_ref[k] = image


def front_kernel(
    count_ref, token_ref, gain_ref, weight_ref, bias_ref,
    masked_ref, unit_ref, pooled_ref, inverse_ref, act_ref,
):
    rows, width = pooled_ref.shape
    length = token_ref.shape[0] // rows
    values = token_ref[...].astype(F32)
    center = jnp.mean(values, axis=-1, keepdims=True)
    spread = jnp.mean((values - center) ** 2, axis=-1, keepdims=True)
    gain = gain_ref[...].reshape(1, width)
    normed = ((values - center) * lax.rsqrt(spread + 1e-06) * gain).astype(BF16)
    pre = jnp.dot(normed, weight_ref[...], preferred_element_type=F32)
    pre = pre + bias_ref[...].reshape(1, width)
    act_ref[...] = 0.5 * pre * (1.0 + jnp.tanh(COEFF * (pre + CUBIC * pre * pre * pre)))
    slot = lax.broadcasted_iota(jnp.int32, (length, 1), 0)
    lives = []
    for p in range(rows):
        live = (slot < count_ref[p]).astype(F32)
        inverse = 1.0 / jnp.full((length, 1), count_ref[p], jnp.int32).astype(F32)
        part = act_ref[p * length : (p + 1) * length, :] * (live * inverse)
        pooled_ref[p : p + 1, :] = jnp.sum(part, axis=0, keepdims=True)
        inverse_ref[p : p + 1, :] = jnp.broadcast_to(inverse[:1], (1, inverse_ref.shape[1]))
        lives.append(live)
    masked_ref[...] = normed * jnp.concatenate(lives, axis=0).astype(BF16)
    pooled = pooled_ref[...]
    size = jnp.sqrt(jnp.sum(pooled * pooled, axis=-1, keepdims=True) + 1e-06)
    unit_ref[...] = (pooled / size).astype(BF16)


def slope_kernel(weight_ref, bias_ref, *refs):
    *piece_refs, slope_ref, column_ref = refs
    width = weight_ref.shape[0]
    cores = size_of("c")
    part = column_ref.shape[0] // (2 * cores)
    row = lax.broadcasted_iota(jnp.int32, (2 * cores * part, width), 0)
    source = lax.broadcasted_iota(jnp.int32, (2 * cores * part, width), 1)
    shift = row * 0
    for j in range(cores):
        for far in range(2):
            block = 2 * j + far
            half = (lax.axis_index("zh") + far) % 2
            core = (lax.axis_index("c") + j) % cores
            begin = (half * size_of("x", "c") + lax.axis_index("x") * cores + core) * part
            shift = jnp.where(row >= block * part, begin - block * part, shift)
    pick = jnp.where(source == row + shift, 1.0, 0.0).astype(BF16)
    bias = bias_ref[...].reshape(1, width)
    at = 0
    for ref in piece_refs:
        piece = ref[...]
        block = piece.shape[0]
        pre = jnp.dot(piece, weight_ref[...], preferred_element_type=F32) + bias
        square = pre * pre
        hyper = jnp.tanh(COEFF * (pre + CUBIC * pre * square))
        slope = 0.5 * (1.0 + hyper) + 0.5 * pre * (1.0 - hyper * hyper) * COEFF * (
            1.0 + 3.0 * CUBIC * square
        )
        slope_ref[at : at + block, :] = slope.astype(BF16)
        columns = lax.dot_general(pick, piece, (((1,), (1,)), ((), ())), preferred_element_type=F32)
        column_ref[:, at : at + block] = columns.astype(BF16)
        at += block


def copies_kernel(image_ref, out_ref):
    rows = image_ref.shape[1]
    for k in range(out_ref.shape[0]):
        for j in range(image_ref.shape[0]):
            out_ref[k, j * rows : (j + 1) * rows, :] = image_ref[j]


def logit_kernel(scale_ref, shift_ref, *refs):
    *unit_refs, image_ref, out_ref = refs
    near, rows, width = out_ref.shape
    group = rows * size_of("y", "za", "zb")
    units = jnp.concatenate([ref[...] for ref in unit_refs], axis=0)
    images = image_ref[...]
    temper = jnp.exp(jnp.full((1, 1), scale_ref[0], F32))
    cosine = lax.dot_general(units, images, (((1,), (1,)), ((), ())), preferred_element_type=F32)
    logit = temper * cosine + shift_ref[0]
    unit_at = lax.broadcasted_iota(jnp.int32, cosine.shape, 0)
    image_at = lax.broadcasted_iota(jnp.int32, cosine.shape, 1)
    offset = (lax.axis_index("y") * size_of("za") + lax.axis_index("za")) * rows
    label = jnp.where((unit_at == image_at - offset) & (unit_at < rows), 1.0, -1.0)
    dlogit = (-label / (1.0 + jnp.exp(label * logit)) / group).astype(BF16)
    terms = jnp.dot(dlogit, images, preferred_element_type=F32).astype(BF16)
    for k in range(near):
        owner = lax.rem(lax.axis_index("zb") + near - k, near)
        out_ref[owner] = terms[k * rows : (k + 1) * rows]


def share_kernel(scale_ref, term_ref, pooled_ref, inverse_ref, out_ref):
    temper = jnp.exp(jnp.full((1, 1), scale_ref[0], F32))
    pooled = pooled_ref[...]
    size = jnp.sqrt(jnp.sum(pooled * pooled, axis=-1, keepdims=True) + 1e-06)
    unit = pooled / size
    total = term_ref[0].astype(F32)
    for k in range(1, term_ref.shape[0]):
        total = total + term_ref[k].astype(F32)
    dunit = temper * total
    dpooled = (dunit - unit * jnp.sum(unit * dunit, axis=-1, keepdims=True)) / size
    share = (dpooled * inverse_ref[:, :1]).astype(BF16)
    for k in range(out_ref.shape[0]):
        out_ref[k] = share


def grad_kernel(share_ref, slope_ref, column_ref, keep_ref, send_ref, dpre_ref):
    along, rows, width = share_ref.shape
    block = slope_ref.shape[0] // along
    rest = keep_ref.shape[0]
    for k in range(along):
        owner = lax.rem(lax.axis_index("x") + along - k, along)
        share = share_ref[owner].astype(F32)
        share = jnp.broadcast_to(share[:, None, :], (rows, block // rows, width)).reshape(block, width)
        slope = slope_ref[k * block : (k + 1) * block, :].astype(F32)
        dpre_ref[k * block : (k + 1) * block, :] = (share * slope).astype(BF16)
    total = jnp.dot(column_ref[...], dpre_ref[...], preferred_element_type=F32)
    keep_ref[...] = total[:rest]
    send_ref[...] = total[rest:].astype(BF16)


def core_kernel(keep_ref, away_ref, near_ref, far_ref):
    total = keep_ref[...] + away_ref[...].astype(F32)
    part = near_ref.shape[0]
    near_ref[...] = total[:part]
    far_ref[...] = total[part:].astype(BF16)


def add_kernel(near_ref, away_ref, out_ref):
    out_ref[0] = near_ref[...] + away_ref[...].astype(F32)


def on_device(
    tokens, token_count, image_embed, norm_gain, head_weight, head_bias, logit_scale, logit_bias
):
    rows, length, width = tokens.shape
    part = width // size_of("zh", "x", "c")
    flat = rows * length
    total = size_of("x") * flat
    swap = [(0, 1), (1, 0)]

    (image,) = local(image_kernel, [((size_of("za"), rows, width), BF16)], image_embed)
    tokens, image = lax.optimization_barrier((tokens, image))
    some_images = exchange(image, "za")

    masked, unit, pooled, inverse = local(
        front_kernel,
        [((flat, width), BF16), ((rows, width), BF16), ((rows, width), F32), ((rows, 128), F32)],
        token_count,
        tokens.reshape(flat, width),
        norm_gain,
        head_weight,
        head_bias,
        smem=(0,),
        scratch=[((flat, width), F32)],
        flops=2 * flat * width * width,
        moved=2 * width * width,
    )
    units = from_others(unit, "zb")
    by_x = from_others(masked, "x")
    units, some_images = lax.optimization_barrier((units, some_images))
    (copies,) = local(
        copies_kernel, [((size_of("y"), size_of("za") * rows, width), BF16)], some_images
    )
    all_images = exchange(copies, "y").reshape(-1, width)
    (terms,) = local(
        logit_kernel,
        [((size_of("zb"), rows, width), BF16)],
        logit_scale,
        logit_bias,
        *units,
        all_images,
        smem=(0, 1),
    )
    terms, by_x = lax.optimization_barrier((terms, by_x))
    terms = exchange(terms, "zb")
    slope, columns = local(
        slope_kernel,
        [((total, width), BF16), ((4 * part, total), BF16)],
        head_weight,
        head_bias,
        *by_x,
        flops=2 * total * width * width,
        moved=2 * width * width + 4 * total * width,
    )
    (share,) = local(
        share_kernel,
        [((size_of("x"), rows, width), BF16)],
        logit_scale,
        terms,
        pooled,
        inverse,
        smem=(0,),
    )
    share, slope, columns = lax.optimization_barrier((share, slope, columns))
    shares = exchange(share, "x")
    keep, send = local(
        grad_kernel,
        [((2 * part, width), F32), ((2 * part, width), BF16)],
        shares,
        slope,
        columns,
        scratch=[((total, width), BF16)],
        flops=8 * part * total * width,
        moved=2 * total * width,
    )
    away = lax.ppermute(send, "c", swap)
    near, far = local(core_kernel, [((part, width), F32), ((part, width), BF16)], keep, away)
    away = lax.ppermute(far, "zh", swap)
    (grad,) = local(add_kernel, [((1, part, width), F32)], near, away)
    return grad


def solution(mesh):
    fine = Mesh(mesh.devices.reshape(SIZES), AXES)
    in_specs = (
        P(AXES, None, None),
        P(AXES),
        P(AXES, None),
        P(),
        P(),
        P(),
        P(),
        P(),
    )
    out_specs = P(("y", "za", "zb"), ("zh", "x", "c"), None)
    return jax.shard_map(
        on_device, mesh=fine, in_specs=in_specs, out_specs=out_specs, check_vma=False
    )
```

time: 183 us -> 152 us (0.83)
  the two profiles are of different devices: /device:TPU:1 before, /device:TPU:457 now
where the time goes in v5:
time: 152 us; the launch traced here: 151 us
  starting transfers between devices  62.4 us (41%)
  waiting for transfers between devices  50.5 us (33%)
  Pallas kernels  24 us (16%)
  blocking collectives  8.93 us (6%)
  local copies, waits for them, and re-layouts  3.54 us (2%)
    ppermute x1, waiting for transfers between devices, on_device(): away = lax.ppermute(far, 'zh', swap)  39.1 us
    all_to_all x3, starting transfers between devices, exchange(): return lax.all_to_all(copies, axes, split_axis=0, concat_axis=0, tiled=True)  26 us
    pallas_call x9, Pallas kernels, local(): pl.pallas_call(body, grid=(1,), out_shape=[jax.ShapeDtypeStruct(shape, dt...  24 us
    ppermute x6, starting transfers between devices, from_others(): lax.ppermute(value, axis, [(i, (i + k) % count) for i in range(count)])  18.8 us
    ppermute x1, starting transfers between devices, on_device(): away = lax.ppermute(far, 'zh', swap)  11.8 us
    ppermute x6, waiting for transfers between devices, from_others(): lax.ppermute(value, axis, [(i, (i + k) % count) for i in range(count)])  9.93 us
    all_to_all x1, blocking collectives, exchange(): return lax.all_to_all(copies, axes, split_axis=0, concat_axis=0, tiled=True)  8.93 us
    ppermute x1, starting transfers between devices, on_device(): away = lax.ppermute(send, 'c', swap)  5.83 us
  transfers between devices with their start and end apart: 11, of which 5 were waited for; matrix products, arithmetic and copies ran while one was open for 0% of the time, Pallas kernels for 8%

profile of v5, /device:TPU:457, one launch (start us, length us, event | category | flops | bytes accessed | tf_op | source)
XLA Modules:
  0.0 150.9 jit_solution(7113140004382799747)
XLA Ops:
  0.0 1.5 %shard_map.82 = bf16[4,16,1152]{2,1,0:T(8,128)(2,1)} custom-call(bf16[16,1152]{1,0:T(8,128)(2,1)} %image_ref.1), custom_call_target="tpu_custom_call" | custom-call | tf_op jit(solution)/shard_map/pallas_call | solution.py:40
  1.5 16.3 %all-to-all-start = ((bf16[4,16,1152]{2,1,0:T(8,128)(2,1)}), bf16[4,16,1152]{2,1,0:T(8,128)(2,1)S(1)}, u32[]{:S(2)}, u32[]{:S(2)}) async-start(bf16[4,16,1152]{2,1,0:T(8,128)(2,1)} %shard_map.82), calls=%async_computation | async-start | bytes 294912 | tf_op jit(solution)/shard_map/all_to_all | solution.py:33
  17.8 3.7 %shard_map.83 = (bf16[128,1152]{1,0:T(8,128)(2,1)}, bf16[16,1152]{1,0:T(8,128)(2,1)}, f32[16,1152]{1,0:T(8,128)}, f32[16,128]{1,0:T(8,128)}) custom-call(s32[16]{0:T(128)} %count_ref.1, bf16[128,1152]{1,0:T(8,128)(2,1)} %bitcast.3, f32[1152]{0:T(1024)} %gain_ref.1, bf16[1152,1152]{1,0:T(8,128)(2,1)} %weight_ref.3, f32[1152]{0:T(1024)} %bias_ref.3), custom_call_target="tpu_custom_call" | custom-call | flops 339738624 | bytes 2654208 | tf_op jit(solution)/shard_map/pallas_call | solution.py:40
  21.5 1.9 %collective-permute-start.2 = (bf16[16,1152]{1,0:T(8,128)(2,1)}, bf16[16,1152]{1,0:T(8,128)(2,1)S(1)}, u32[]{:S(2)}, u32[]{:S(2)}) collective-permute-start(bf16[16,1152]{1,0:T(8,128)(2,1)} %get-tuple-element.33.refs_0_), channel_id=1, source_target_pairs={{0,48},{16,0},{32,16},{48,32},{1,49},{17,1},{33,17},{49,33},{2,50}... | collective-permute-start | bytes 110600 | tf_op jit(solution)/shard_map/ppermute | solution.py:26
  23.4 5.6 %collective-permute-start.1 = (bf16[16,1152]{1,0:T(8,128)(2,1)}, bf16[16,1152]{1,0:T(8,128)(2,1)S(1)}, u32[]{:S(2)}, u32[]{:S(2)}) collective-permute-start(bf16[16,1152]{1,0:T(8,128)(2,1)} %get-tuple-element.33.refs_0_), channel_id=1, source_target_pairs={{0,32},{16,48},{32,0},{48,16},{1,33},{17,49},{33,1},{49,17},{2,34}... | collective-permute-start | bytes 110600 | tf_op jit(solution)/shard_map/ppermute | solution.py:26
  29.1 1.9 %collective-permute-start = (bf16[16,1152]{1,0:T(8,128)(2,1)}, bf16[16,1152]{1,0:T(8,128)(2,1)S(1)}, u32[]{:S(2)}, u32[]{:S(2)}) collective-permute-start(bf16[16,1152]{1,0:T(8,128)(2,1)} %get-tuple-element.33.refs_0_), channel_id=1, source_target_pairs={{0,16},{16,32},{32,48},{48,0},{1,17},{17,33},{33,49},{49,1},{2,18}... | collective-permute-start | bytes 110600 | tf_op jit(solution)/shard_map/ppermute | solution.py:26
  32.1 1.9 %collective-permute-done.refs_1_ = bf16[16,1152]{1,0:T(8,128)(2,1)S(1)} collective-permute-done((bf16[16,1152]{1,0:T(8,128)(2,1)}, bf16[16,1152]{1,0:T(8,128)(2,1)S(1)}, u32[]{:S(2)}, u32[]{:S(2)}) %collective-permute-start) | collective-permute-done | bytes 36896 | tf_op jit(solution)/shard_map/ppermute | solution.py:26
  34.6 1.8 %shard_map.84 = bf16[4,64,1152]{2,1,0:T(8,128)(2,1)} custom-call(bf16[4,16,1152]{2,1,0:T(8,128)(2,1)} %copy-done.2), custom_call_target="tpu_custom_call" | custom-call | tf_op jit(solution)/shard_map/pallas_call | solution.py:40
  36.4 4.3 %all-to-all-start.1 = ((bf16[4,64,1152]{2,1,0:T(8,128)(2,1)}), bf16[4,64,1152]{2,1,0:T(8,128)(2,1)S(1)}, u32[]{:S(2)}, u32[]{:S(2)}) async-start(bf16[4,64,1152]{2,1,0:T(8,128)(2,1)} %shard_map.84), calls=%async_computation.1 | async-start | bytes 1179648 | tf_op jit(solution)/shard_map/all_to_all | solution.py:33
  40.8 4.4 %collective-permute-start.5 = (bf16[128,1152]{1,0:T(8,128)(2,1)}, bf16[128,1152]{1,0:T(8,128)(2,1)S(1)}, u32[]{:S(2)}, u32[]{:S(2)}) collective-permute-start(bf16[128,1152]{1,0:T(8,128)(2,1)} %get-tuple-element.42.refs_0_), channel_id=1, source_target_pairs={{0,6},{2,0},{4,2},{6,4},{1,7},{3,1},{5,3},{7,5},{8,14},{10,8},{12,... | collective-permute-start | bytes 884744 | tf_op jit(solution)/shard_map/ppermute | solution.py:26
  45.2 2.4 %collective-permute-start.4 = (bf16[128,1152]{1,0:T(8,128)(2,1)}, bf16[128,1152]{1,0:T(8,128)(2,1)S(1)}, u32[]{:S(2)}, u32[]{:S(2)}) collective-permute-start(bf16[128,1152]{1,0:T(8,128)(2,1)} %get-tuple-element.42.refs_0_), channel_id=1, source_target_pairs={{0,4},{2,6},{4,0},{6,2},{1,5},{3,7},{5,1},{7,3},{8,12},{10,14},{12... | collective-permute-start | bytes 884744 | tf_op jit(solution)/shard_map/ppermute | solution.py:26
  47.6 2.5 %collective-permute-start.3 = (bf16[128,1152]{1,0:T(8,128)(2,1)}, bf16[128,1152]{1,0:T(8,128)(2,1)S(1)}, u32[]{:S(2)}, u32[]{:S(2)}) collective-permute-start(bf16[128,1152]{1,0:T(8,128)(2,1)} %get-tuple-element.42.refs_0_), channel_id=1, source_target_pairs={{0,2},{2,4},{4,6},{6,0},{1,3},{3,5},{5,7},{7,1},{8,10},{10,12},{12... | collective-permute-start | bytes 884744 | tf_op jit(solution)/shard_map/ppermute | solution.py:26
  52.3 2.5 %shard_map.85 = bf16[4,16,1152]{2,1,0:T(8,128)(2,1)} custom-call(f32[1]{0:T(128)S(6)} %copy.9.scale_ref, f32[1]{0:T(128)S(6)} %copy.10.shift_ref, bf16[16,1152]{1,0:T(8,128)(2,1)} %get-tuple-element.33.refs_0_, bf16[16,1152]{1,0:T(8,128)(2,1)} %copy-done.7, bf16[16,1152]{1,0:T(8,128)(2,1)} %copy-done.6, bf16[16,1152]{1,0:T(8,128)(2,1)} %copy-done.5, ...), custom_call_target="tpu_custom_call" | custom-call | tf_op jit(solution)/shard_map/pallas_call | solution.py:40
  54.8 7.0 %collective-permute-done.3.refs_1_ = bf16[128,1152]{1,0:T(8,128)(2,1)S(1)} collective-permute-done((bf16[128,1152]{1,0:T(8,128)(2,1)}, bf16[128,1152]{1,0:T(8,128)(2,1)S(1)}, u32[]{:S(2)}, u32[]{:S(2)}) %collective-permute-start.3) | collective-permute-done | bytes 294944 | tf_op jit(solution)/shard_map/ppermute | solution.py:26
  61.7 5.4 %all-to-all-start.2 = ((bf16[4,16,1152]{2,1,0:T(8,128)(2,1)}), bf16[4,16,1152]{2,1,0:T(8,128)(2,1)S(1)}, u32[]{:S(2)}, u32[]{:S(2)}) async-start(bf16[4,16,1152]{2,1,0:T(8,128)(2,1)} %shard_map.85), calls=%async_computation.2 | async-start | bytes 294912 | tf_op jit(solution)/shard_map/all_to_all | solution.py:33
  67.1 6.0 %shard_map.87 = (bf16[512,1152]{1,0:T(8,128)(2,1)}, bf16[288,512]{1,0:T(8,128)(2,1)}) custom-call(bf16[1152,1152]{1,0:T(8,128)(2,1)} %weight_ref.3, f32[1152]{0:T(1024)} %bias_ref.3, bf16[128,1152]{1,0:T(8,128)(2,1)} %get-tuple-element.42.refs_0_, bf16[128,1152]{1,0:T(8,128)(2,1)} %copy-done.10, bf16[128,1152]{1,0:T(8,128)(2,1)} %copy-done.9, ...), custom_call_target="tpu_custom_call" | custom-call | flops 1358954496 | bytes 5013504 | tf_op jit(solution)/shard_map/pallas_call | solution.py:40
  73.8 1.8 %shard_map.86 = bf16[4,16,1152]{2,1,0:T(8,128)(2,1)} custom-call(f32[1]{0:T(128)S(6)} %copy.9.scale_ref, bf16[4,16,1152]{2,1,0:T(8,128)(2,1)} %copy-done.1, f32[16,1152]{1,0:T(8,128)} %get-tuple-element.40.pooled_ref, f32[16,128]{1,0:T(8,128)} %get-tuple-element.41.inverse_ref), custom_call_target="tpu_custom_call" | custom-call | tf_op jit(solution)/shard_map/pallas_call | solution.py:40
  75.6 8.9 %all_to_all.20.share_ref = bf16[4,16,1152]{2,1,0:T(8,128)(2,1)} all-to-all(bf16[4,16,1152]{2,1,0:T(8,128)(2,1)} %shard_map.86), channel_id=1, replica_groups=mesh['y'=4,'za'=4,'zb'=4,'zh'=2,'x'=4,'c'=2] {'x'}, dimensions={0} | all-to-all | bytes 294912 | tf_op jit(solution)/shard_map/all_to_all | solution.py:33
  84.5 2.9 %shard_map.88 = (f32[144,1152]{1,0:T(8,128)}, bf16[144,1152]{1,0:T(8,128)(2,1)}) custom-call(bf16[4,16,1152]{2,1,0:T(8,128)(2,1)} %all_to_all.20.share_ref, bf16[512,1152]{1,0:T(8,128)(2,1)} %get-tuple-element.49.slope_ref, bf16[288,512]{1,0:T(8,128)(2,1)} %get-tuple-element.50.column_ref), custom_call_target="tpu_custom_call" | custom-call | flops 339738624 | bytes 1179648 | tf_op jit(solution)/shard_map/pallas_call | solution.py:40
  87.5 5.8 %collective-permute-start.6 = (bf16[144,1152]{1,0:T(8,128)(2,1)}, bf16[144,1152]{1,0:T(8,128)(2,1)S(1)}, u32[]{:S(2)}, u32[]{:S(2)}) collective-permute-start(bf16[144,1152]{1,0:T(8,128)(2,1)} %get-tuple-element.52), channel_id=1, source_target_pairs={{0,1},{1,0},{2,3},{3,2},{4,5},{5,4},{6,7},{7,6},{8,9},{9,8},{10,11... | collective-permute-start | bytes 995336 | tf_op jit(solution)/shard_map/ppermute | solution.py:264
  95.5 2.0 %shard_map.89 = (f32[72,1152]{1,0:T(8,128)}, bf16[72,1152]{1,0:T(8,128)(2,1)}) custom-call(f32[144,1152]{1,0:T(8,128)} %get-tuple-element.51.keep_ref, bf16[144,1152]{1,0:T(8,128)(2,1)} %copy-done.3), custom_call_target="tpu_custom_call" | custom-call | tf_op jit(solution)/shard_map/pallas_call | solution.py:40
  97.5 11.8 %collective-permute-start.7 = (bf16[72,1152]{1,0:T(8,128)(2,1)}, bf16[72,1152]{1,0:T(8,128)(2,1)S(1)}, u32[]{:S(2)}, u32[]{:S(2)}) collective-permute-start(bf16[72,1152]{1,0:T(8,128)(2,1)} %get-tuple-element.54), channel_id=1, source_target_pairs={{0,8},{8,0},{1,9},{9,1},{2,10},{10,2},{3,11},{11,3},{4,12},{12,4},... | collective-permute-start | bytes 497672 | tf_op jit(solution)/shard_map/ppermute | solution.py:266
  109.3 39.1 %collective-permute-done.7.away_ref = bf16[72,1152]{1,0:T(8,128)(2,1)S(1)} collective-permute-done((bf16[72,1152]{1,0:T(8,128)(2,1)}, bf16[72,1152]{1,0:T(8,128)(2,1)S(1)}, u32[]{:S(2)}, u32[]{:S(2)}) %collective-permute-start.7) | collective-permute-done | bytes 165920 | tf_op jit(solution)/shard_map/ppermute | solution.py:266
  149.2 1.8 %shard_map.90 = f32[1,72,1152]{2,1,0:T(8,128)} custom-call(f32[72,1152]{1,0:T(8,128)} %get-tuple-element.53.near_ref, bf16[72,1152]{1,0:T(8,128)(2,1)} %copy-done.4), custom_call_target="tpu_custom_call" | custom-call | tf_op jit(solution)/shard_map/pallas_call | solution.py:40
  (30 shorter events, 6.1 us)
Async XLA Ops:
  1.5 32.4 %all-to-all-start = ((bf16[4,16,1152]{2,1,0:T(8,128)(2,1)}), bf16[4,16,1152]{2,1,0:T(8,128)(2,1)S(1)}, u32[]{:S(2)}, u32[]{:S(2)}) async-start(bf16[4,16,1152]{2,1,0:T(8,128)(2,1)} %shard_map.82), calls=%async_computation | async-start | bytes 294912 | tf_op jit(solution)/shard_map/all_to_all | solution.py:33
  21.5 9.5 %collective-permute-start.2 = (bf16[16,1152]{1,0:T(8,128)(2,1)}, bf16[16,1152]{1,0:T(8,128)(2,1)S(1)}, u32[]{:S(2)}, u32[]{:S(2)}) collective-permute-start(bf16[16,1152]{1,0:T(8,128)(2,1)} %get-tuple-element.33.refs_0_), channel_id=1, source_target_pairs={{0,48},{16,0},{32,16},{48,32},{1,49},{17,1},{33,17},{49,33},{2,50}... | collective-permute-start | bytes 110600 | tf_op jit(solution)/shard_map/ppermute | solution.py:26
  23.4 8.7 %collective-permute-start.1 = (bf16[16,1152]{1,0:T(8,128)(2,1)}, bf16[16,1152]{1,0:T(8,128)(2,1)S(1)}, u32[]{:S(2)}, u32[]{:S(2)}) collective-permute-start(bf16[16,1152]{1,0:T(8,128)(2,1)} %get-tuple-element.33.refs_0_), channel_id=1, source_target_pairs={{0,32},{16,48},{32,0},{48,16},{1,33},{17,49},{33,1},{49,17},{2,34}... | collective-permute-start | bytes 110600 | tf_op jit(solution)/shard_map/ppermute | solution.py:26
  29.1 4.9 %collective-permute-start = (bf16[16,1152]{1,0:T(8,128)(2,1)}, bf16[16,1152]{1,0:T(8,128)(2,1)S(1)}, u32[]{:S(2)}, u32[]{:S(2)}) collective-permute-start(bf16[16,1152]{1,0:T(8,128)(2,1)} %get-tuple-element.33.refs_0_), channel_id=1, source_target_pairs={{0,16},{16,32},{32,48},{48,0},{1,17},{17,33},{33,49},{49,1},{2,18}... | collective-permute-start | bytes 110600 | tf_op jit(solution)/shard_map/ppermute | solution.py:26
  31.0 20.4 %copy-start.5 = (bf16[16,1152]{1,0:T(8,128)(2,1)}, bf16[16,1152]{1,0:T(8,128)(2,1)S(1)}, u32[]{:S(2)}) copy-start(bf16[16,1152]{1,0:T(8,128)(2,1)S(1)} %collective-permute-done.2.refs_3_) | copy-start | bytes 110596
  32.1 19.4 %copy-start.6 = (bf16[16,1152]{1,0:T(8,128)(2,1)}, bf16[16,1152]{1,0:T(8,128)(2,1)S(1)}, u32[]{:S(2)}) copy-start(bf16[16,1152]{1,0:T(8,128)(2,1)S(1)} %collective-permute-done.1.refs_2_) | copy-start | bytes 110596
  34.0 17.5 %copy-start.7 = (bf16[16,1152]{1,0:T(8,128)(2,1)}, bf16[16,1152]{1,0:T(8,128)(2,1)S(1)}, u32[]{:S(2)}) copy-start(bf16[16,1152]{1,0:T(8,128)(2,1)S(1)} %collective-permute-done.refs_1_) | copy-start | bytes 110596
  34.0 0.7 copy-start.2
  36.4 15.0 %all-to-all-start.1 = ((bf16[4,64,1152]{2,1,0:T(8,128)(2,1)}), bf16[4,64,1152]{2,1,0:T(8,128)(2,1)S(1)}, u32[]{:S(2)}, u32[]{:S(2)}) async-start(bf16[4,64,1152]{2,1,0:T(8,128)(2,1)} %shard_map.84), calls=%async_computation.1 | async-start | bytes 1179648 | tf_op jit(solution)/shard_map/all_to_all | solution.py:33
  40.8 14.0 %collective-permute-start.5 = (bf16[128,1152]{1,0:T(8,128)(2,1)}, bf16[128,1152]{1,0:T(8,128)(2,1)S(1)}, u32[]{:S(2)}, u32[]{:S(2)}) collective-permute-start(bf16[128,1152]{1,0:T(8,128)(2,1)} %get-tuple-element.42.refs_0_), channel_id=1, source_target_pairs={{0,6},{2,0},{4,2},{6,4},{1,7},{3,1},{5,3},{7,5},{8,14},{10,8},{12,... | collective-permute-start | bytes 884744 | tf_op jit(solution)/shard_map/ppermute | solution.py:26
  45.2 9.6 %collective-permute-start.4 = (bf16[128,1152]{1,0:T(8,128)(2,1)}, bf16[128,1152]{1,0:T(8,128)(2,1)S(1)}, u32[]{:S(2)}, u32[]{:S(2)}) collective-permute-start(bf16[128,1152]{1,0:T(8,128)(2,1)} %get-tuple-element.42.refs_0_), channel_id=1, source_target_pairs={{0,4},{2,6},{4,0},{6,2},{1,5},{3,7},{5,1},{7,3},{8,12},{10,14},{12... | collective-permute-start | bytes 884744 | tf_op jit(solution)/shard_map/ppermute | solution.py:26
  47.6 14.1 %collective-permute-start.3 = (bf16[128,1152]{1,0:T(8,128)(2,1)}, bf16[128,1152]{1,0:T(8,128)(2,1)S(1)}, u32[]{:S(2)}, u32[]{:S(2)}) collective-permute-start(bf16[128,1152]{1,0:T(8,128)(2,1)} %get-tuple-element.42.refs_0_), channel_id=1, source_target_pairs={{0,2},{2,4},{4,6},{6,0},{1,3},{3,5},{5,7},{7,1},{8,10},{10,12},{12... | collective-permute-start | bytes 884744 | tf_op jit(solution)/shard_map/ppermute | solution.py:26
  51.4 0.8 copy-start
  54.7 12.4 %copy-start.8 = (bf16[128,1152]{1,0:T(8,128)(2,1)}, bf16[128,1152]{1,0:T(8,128)(2,1)S(1)}, u32[]{:S(2)}) copy-start(bf16[128,1152]{1,0:T(8,128)(2,1)S(1)} %collective-permute-done.5.refs_3_) | copy-start | bytes 884740
  54.7 12.4 %copy-start.9 = (bf16[128,1152]{1,0:T(8,128)(2,1)}, bf16[128,1152]{1,0:T(8,128)(2,1)S(1)}, u32[]{:S(2)}) copy-start(bf16[128,1152]{1,0:T(8,128)(2,1)S(1)} %collective-permute-done.4.refs_2_) | copy-start | bytes 884740
  61.7 5.4 %copy-start.10 = (bf16[128,1152]{1,0:T(8,128)(2,1)}, bf16[128,1152]{1,0:T(8,128)(2,1)S(1)}, u32[]{:S(2)}) copy-start(bf16[128,1152]{1,0:T(8,128)(2,1)S(1)} %collective-permute-done.3.refs_1_) | copy-start | bytes 884740
  61.7 11.4 %all-to-all-start.2 = ((bf16[4,16,1152]{2,1,0:T(8,128)(2,1)}), bf16[4,16,1152]{2,1,0:T(8,128)(2,1)S(1)}, u32[]{:S(2)}, u32[]{:S(2)}) async-start(bf16[4,16,1152]{2,1,0:T(8,128)(2,1)} %shard_map.85), calls=%async_computation.2 | async-start | bytes 294912 | tf_op jit(solution)/shard_map/all_to_all | solution.py:33
  73.1 0.7 copy-start.1
  87.5 7.3 %collective-permute-start.6 = (bf16[144,1152]{1,0:T(8,128)(2,1)}, bf16[144,1152]{1,0:T(8,128)(2,1)S(1)}, u32[]{:S(2)}, u32[]{:S(2)}) collective-permute-start(bf16[144,1152]{1,0:T(8,128)(2,1)} %get-tuple-element.52), channel_id=1, source_target_pairs={{0,1},{1,0},{2,3},{3,2},{4,5},{5,4},{6,7},{7,6},{8,9},{9,8},{10,11... | collective-permute-start | bytes 995336 | tf_op jit(solution)/shard_map/ppermute | solution.py:264
  94.8 0.7 copy-start.3
  97.5 51.0 %collective-permute-start.7 = (bf16[72,1152]{1,0:T(8,128)(2,1)}, bf16[72,1152]{1,0:T(8,128)(2,1)S(1)}, u32[]{:S(2)}, u32[]{:S(2)}) collective-permute-start(bf16[72,1152]{1,0:T(8,128)(2,1)} %get-tuple-element.54), channel_id=1, source_target_pairs={{0,8},{8,0},{1,9},{9,1},{2,10},{10,2},{3,11},{11,3},{4,12},{12,4},... | collective-permute-start | bytes 497672 | tf_op jit(solution)/shard_map/ppermute | solution.py:266
  148.5 0.7 copy-start.4

commit v6 on v5

--- a/solution.py
+++ b/solution.py
@@ -7,7 +7,6 @@
 
 AXES = ("y", "za", "zb", "zh", "x", "c")
 SIZES = (4, 4, 4, 2, 4, 2)
-VMEM_LIMIT = 60 * 1024 * 1024
 COEFF = 0.7978845608
 CUBIC = 0.044715
 BF16, F32 = jnp.bfloat16, jnp.float32
@@ -33,7 +32,7 @@
     return lax.all_to_all(copies, axes, split_axis=0, concat_axis=0, tiled=True)
 
 
-def local(body, outs, *args, smem=(), scratch=(), flops=0, moved=0):
+def local(body, outs, *args, smem=(), scratch=(), flops=0, moved=0, limit=12):
     def whole(shape, space):
         return pl.BlockSpec(shape, lambda i: (0,) * len(shape), memory_space=space)
 
@@ -44,7 +43,7 @@
         in_specs=[whole(v.shape, pltpu.SMEM if i in smem else None) for i, v in enumerate(args)],
         out_specs=[whole(shape, None) for shape, _ in outs],
         scratch_shapes=[pltpu.VMEM(shape, dtype) for shape, dtype in scratch],
-        compiler_params=pltpu.CompilerParams(vmem_limit_bytes=VMEM_LIMIT),
+        compiler_params=pltpu.CompilerParams(vmem_limit_bytes=limit * 1024 * 1024),
         cost_estimate=pl.CostEstimate(flops=flops, bytes_accessed=moved, transcendentals=0),
     )(*args)
 
@@ -212,10 +211,13 @@
         scratch=[((flat, width), F32)],
         flops=2 * flat * width * width,
         moved=2 * width * width,
+        limit=60,
     )
     units = from_others(unit, "zb")
     by_x = from_others(masked, "x")
-    units, some_images = lax.optimization_barrier((units, some_images))
+    mine, *early, last = by_x
+    early, units, some_images = lax.optimization_barrier((early, units, some_images))
+    by_x = [mine, *early, last]
     (copies,) = local(
         copies_kernel, [((size_of("y"), size_of("za") * rows, width), BF16)], some_images
     )
@@ -239,6 +241,7 @@
         *by_x,
         flops=2 * total * width * width,
         moved=2 * width * width + 4 * total * width,
+        limit=60,
     )
     (share,) = local(
         share_kernel,
@@ -260,6 +263,7 @@
         scratch=[((total, width), BF16)],
         flops=8 * part * total * width,
         moved=2 * total * width,
+        limit=24,
     )
     away = lax.ppermute(send, "c", swap)
     near, far = local(core_kernel, [((part, width), F32), ((part, width), BF16)], keep, away)

time: 152 us -> 143 us (0.941)
  the two profiles are of different devices: /device:TPU:457 before, /device:TPU:289 now
where the time goes in v6:
time: 143 us; the launch traced here: 142 us
  starting transfers between devices  69.7 us (49%)
  waiting for transfers between devices  43.2 us (30%)
  Pallas kernels  14.5 us (10%)
  blocking collectives  9.25 us (6%)
  local copies, waits for them, and re-layouts  3.79 us (3%)
  between operations  1.44 us (1%)
    ppermute x1, waiting for transfers between devices, on_device(): away = lax.ppermute(far, 'zh', swap)  38.9 us
    all_to_all x3, starting transfers between devices, exchange(): return lax.all_to_all(copies, axes, split_axis=0, concat_axis=0, tiled=True)  28.1 us
    ppermute x6, starting transfers between devices, from_others(): lax.ppermute(value, axis, [(i, (i + k) % count) for i in range(count)])  22.2 us
    pallas_call x9, Pallas kernels, local(): pl.pallas_call(body, grid=(1,), out_shape=[jax.ShapeDtypeStruct(shape, dt...  14.5 us
    ppermute x1, starting transfers between devices, on_device(): away = lax.ppermute(far, 'zh', swap)  12.1 us
    all_to_all x1, blocking collectives, exchange(): return lax.all_to_all(copies, axes, split_axis=0, concat_axis=0, tiled=True)  9.25 us
    ppermute x1, starting transfers between devices, on_device(): away = lax.ppermute(send, 'c', swap)  7.27 us
    unnamed x18, local copies, waits for them, and re-layouts  3.79 us
  transfers between devices with their start and end apart: 11, of which 4 were waited for; matrix products, arithmetic and copies ran while one was open for 0% of the time, Pallas kernels for 8%

profile of v6, /device:TPU:289, one launch (start us, length us, event | category | flops | bytes accessed | tf_op | source)
XLA Modules:
  0.0 141.8 jit_solution(2812562117184651516)
XLA Ops:
  1.5 18.1 %all-to-all-start = ((bf16[4,16,1152]{2,1,0:T(8,128)(2,1)}), bf16[4,16,1152]{2,1,0:T(8,128)(2,1)S(1)}, u32[]{:S(2)}, u32[]{:S(2)}) async-start(bf16[4,16,1152]{2,1,0:T(8,128)(2,1)} %shard_map.82), calls=%async_computation | async-start | bytes 294912 | tf_op jit(solution)/shard_map/all_to_all | solution.py:32
  19.6 3.7 %shard_map.83 = (bf16[128,1152]{1,0:T(8,128)(2,1)}, bf16[16,1152]{1,0:T(8,128)(2,1)}, f32[16,1152]{1,0:T(8,128)}, f32[16,128]{1,0:T(8,128)}) custom-call(s32[16]{0:T(128)} %count_ref.1, bf16[128,1152]{1,0:T(8,128)(2,1)} %bitcast.3, f32[1152]{0:T(1024)} %gain_ref.1, bf16[1152,1152]{1,0:T(8,128)(2,1)} %weight_ref.3, f32[1152]{0:T(1024)} %bias_ref.3), custom_call_target="tpu_custom_call" | custom-call | flops 339738624 | bytes 2654208 | tf_op jit(solution)/shard_map/pallas_call | solution.py:39
  23.3 4.6 %collective-permute-start.1 = (bf16[128,1152]{1,0:T(8,128)(2,1)}, bf16[128,1152]{1,0:T(8,128)(2,1)S(1)}, u32[]{:S(2)}, u32[]{:S(2)}) collective-permute-start(bf16[128,1152]{1,0:T(8,128)(2,1)} %get-tuple-element.46.refs_0_), channel_id=1, source_target_pairs={{0,4},{2,6},{4,0},{6,2},{1,5},{3,7},{5,1},{7,3},{8,12},{10,14},{12... | collective-permute-start | bytes 884744 | tf_op jit(solution)/shard_map/ppermute | solution.py:25
  28.0 2.2 %collective-permute-start = (bf16[128,1152]{1,0:T(8,128)(2,1)}, bf16[128,1152]{1,0:T(8,128)(2,1)S(1)}, u32[]{:S(2)}, u32[]{:S(2)}) collective-permute-start(bf16[128,1152]{1,0:T(8,128)(2,1)} %get-tuple-element.46.refs_0_), channel_id=1, source_target_pairs={{0,2},{2,4},{4,6},{6,0},{1,3},{3,5},{5,7},{7,1},{8,10},{10,12},{12... | collective-permute-start | bytes 884744 | tf_op jit(solution)/shard_map/ppermute | solution.py:25
  30.2 1.9 %collective-permute-start.4 = (bf16[16,1152]{1,0:T(8,128)(2,1)}, bf16[16,1152]{1,0:T(8,128)(2,1)S(1)}, u32[]{:S(2)}, u32[]{:S(2)}) collective-permute-start(bf16[16,1152]{1,0:T(8,128)(2,1)} %get-tuple-element.36.refs_0_), channel_id=1, source_target_pairs={{0,48},{16,0},{32,16},{48,32},{1,49},{17,1},{33,17},{49,33},{2,50}... | collective-permute-start | bytes 110600 | tf_op jit(solution)/shard_map/ppermute | solution.py:25
  32.1 4.9 %collective-permute-start.3 = (bf16[16,1152]{1,0:T(8,128)(2,1)}, bf16[16,1152]{1,0:T(8,128)(2,1)S(1)}, u32[]{:S(2)}, u32[]{:S(2)}) collective-permute-start(bf16[16,1152]{1,0:T(8,128)(2,1)} %get-tuple-element.36.refs_0_), channel_id=1, source_target_pairs={{0,32},{16,48},{32,0},{48,16},{1,33},{17,49},{33,1},{49,17},{2,34}... | collective-permute-start | bytes 110600 | tf_op jit(solution)/shard_map/ppermute | solution.py:25
  37.0 4.3 %collective-permute-start.2 = (bf16[16,1152]{1,0:T(8,128)(2,1)}, bf16[16,1152]{1,0:T(8,128)(2,1)S(1)}, u32[]{:S(2)}, u32[]{:S(2)}) collective-permute-start(bf16[16,1152]{1,0:T(8,128)(2,1)} %get-tuple-element.36.refs_0_), channel_id=1, source_target_pairs={{0,16},{16,32},{32,48},{48,0},{1,17},{17,33},{33,49},{49,1},{2,18}... | collective-permute-start | bytes 110600 | tf_op jit(solution)/shard_map/ppermute | solution.py:25
  41.3 1.3 collective-permute-done.2.refs_1_
  42.7 0.9 shard_map.84
  43.6 4.2 %all-to-all-start.1 = ((bf16[4,64,1152]{2,1,0:T(8,128)(2,1)}), bf16[4,64,1152]{2,1,0:T(8,128)(2,1)S(1)}, u32[]{:S(2)}, u32[]{:S(2)}) async-start(bf16[4,64,1152]{2,1,0:T(8,128)(2,1)} %shard_map.84), calls=%async_computation.1 | async-start | bytes 1179648 | tf_op jit(solution)/shard_map/all_to_all | solution.py:32
  47.8 4.3 %collective-permute-start.5 = (bf16[128,1152]{1,0:T(8,128)(2,1)}, bf16[128,1152]{1,0:T(8,128)(2,1)S(1)}, u32[]{:S(2)}, u32[]{:S(2)}) collective-permute-start(bf16[128,1152]{1,0:T(8,128)(2,1)} %get-tuple-element.46.refs_0_), channel_id=1, source_target_pairs={{0,6},{2,0},{4,2},{6,4},{1,7},{3,1},{5,3},{7,5},{8,14},{10,8},{12,... | collective-permute-start | bytes 884744 | tf_op jit(solution)/shard_map/ppermute | solution.py:25
  53.4 1.7 %all-to-all-done.1 = bf16[4,64,1152]{2,1,0:T(8,128)(2,1)S(1)} async-done(((bf16[4,64,1152]{2,1,0:T(8,128)(2,1)}), bf16[4,64,1152]{2,1,0:T(8,128)(2,1)S(1)}, u32[]{:S(2)}, u32[]{:S(2)}) %all-to-all-start.1) | async-done | bytes 589856 | tf_op jit(solution)/shard_map/all_to_all | solution.py:32
  55.1 0.8 copy-done.4
  55.9 1.3 shard_map.85
  57.2 5.8 %all-to-all-start.2 = ((bf16[4,16,1152]{2,1,0:T(8,128)(2,1)}), bf16[4,16,1152]{2,1,0:T(8,128)(2,1)S(1)}, u32[]{:S(2)}, u32[]{:S(2)}) async-start(bf16[4,16,1152]{2,1,0:T(8,128)(2,1)} %shard_map.85), calls=%async_computation.2 | async-start | bytes 294912 | tf_op jit(solution)/shard_map/all_to_all | solution.py:32
  63.0 6.0 %shard_map.87 = (bf16[512,1152]{1,0:T(8,128)(2,1)}, bf16[288,512]{1,0:T(8,128)(2,1)}) custom-call(bf16[1152,1152]{1,0:T(8,128)(2,1)} %weight_ref.3, f32[1152]{0:T(1024)} %bias_ref.3, bf16[128,1152]{1,0:T(8,128)(2,1)} %get-tuple-element.46.refs_0_, bf16[128,1152]{1,0:T(8,128)(2,1)} %copy-done.7, bf16[128,1152]{1,0:T(8,128)(2,1)} %copy-done.6, ...), custom_call_target="tpu_custom_call" | custom-call | flops 1358954496 | bytes 5013504 | tf_op jit(solution)/shard_map/pallas_call | solution.py:39
  69.3 9.3 %all_to_all.20.share_ref = bf16[4,16,1152]{2,1,0:T(8,128)(2,1)S(1)} all-to-all(bf16[4,16,1152]{2,1,0:T(8,128)(2,1)S(1)} %shard_map.86), channel_id=1, replica_groups=mesh['y'=4,'za'=4,'zb'=4,'zh'=2,'x'=4,'c'=2] {'x'}, dimensions={0} | all-to-all | bytes 294912 | tf_op jit(solution)/shard_map/all_to_all | solution.py:32
  78.5 1.3 copy-done
  79.8 1.0 copy-done.1
  81.4 7.3 %collective-permute-start.6 = (bf16[144,1152]{1,0:T(8,128)(2,1)S(1)}, bf16[144,1152]{1,0:T(8,128)(2,1)S(1)}, u32[]{:S(2)}, u32[]{:S(2)}) collective-permute-start(bf16[144,1152]{1,0:T(8,128)(2,1)S(1)} %get-tuple-element.56), channel_id=1, source_target_pairs={{0,1},{1,0},{2,3},{3,2},{4,5},{5,4},{6,7},{7,6},{8,9},{9,8},{10,11... | collective-permute-start | bytes 995336 | tf_op jit(solution)/shard_map/ppermute | solution.py:268
  88.7 1.2 collective-permute-done.6.away_ref
  90.0 12.1 %collective-permute-start.7 = (bf16[72,1152]{1,0:T(8,128)(2,1)S(1)}, bf16[72,1152]{1,0:T(8,128)(2,1)S(1)}, u32[]{:S(2)}, u32[]{:S(2)}) collective-permute-start(bf16[72,1152]{1,0:T(8,128)(2,1)S(1)} %get-tuple-element.58), channel_id=1, source_target_pairs={{0,8},{8,0},{1,9},{9,1},{2,10},{10,2},{3,11},{11,3},{4,12},{12,4},... | collective-permute-start | bytes 497672 | tf_op jit(solution)/shard_map/ppermute | solution.py:270
  102.2 38.9 %collective-permute-done.7.away_ref = bf16[72,1152]{1,0:T(8,128)(2,1)S(1)} collective-permute-done((bf16[72,1152]{1,0:T(8,128)(2,1)S(1)}, bf16[72,1152]{1,0:T(8,128)(2,1)S(1)}, u32[]{:S(2)}, u32[]{:S(2)}) %collective-permute-start.7) | collective-permute-done | bytes 165920 | tf_op jit(solution)/shard_map/ppermute | solution.py:270
  141.1 0.8 shard_map.90
  (26 shorter events, 2.5 us)
Async XLA Ops:
  0.0 0.8 copy-start.3
  1.5 41.1 %all-to-all-start = ((bf16[4,16,1152]{2,1,0:T(8,128)(2,1)}), bf16[4,16,1152]{2,1,0:T(8,128)(2,1)S(1)}, u32[]{:S(2)}, u32[]{:S(2)}) async-start(bf16[4,16,1152]{2,1,0:T(8,128)(2,1)} %shard_map.82), calls=%async_computation | async-start | bytes 294912 | tf_op jit(solution)/shard_map/all_to_all | solution.py:32
  23.3 19.3 %collective-permute-start.1 = (bf16[128,1152]{1,0:T(8,128)(2,1)}, bf16[128,1152]{1,0:T(8,128)(2,1)S(1)}, u32[]{:S(2)}, u32[]{:S(2)}) collective-permute-start(bf16[128,1152]{1,0:T(8,128)(2,1)} %get-tuple-element.46.refs_0_), channel_id=1, source_target_pairs={{0,4},{2,6},{4,0},{6,2},{1,5},{3,7},{5,1},{7,3},{8,12},{10,14},{12... | collective-permute-start | bytes 884744 | tf_op jit(solution)/shard_map/ppermute | solution.py:25
  28.0 14.7 %collective-permute-start = (bf16[128,1152]{1,0:T(8,128)(2,1)}, bf16[128,1152]{1,0:T(8,128)(2,1)S(1)}, u32[]{:S(2)}, u32[]{:S(2)}) collective-permute-start(bf16[128,1152]{1,0:T(8,128)(2,1)} %get-tuple-element.46.refs_0_), channel_id=1, source_target_pairs={{0,2},{2,4},{4,6},{6,0},{1,3},{3,5},{5,7},{7,1},{8,10},{10,12},{12... | collective-permute-start | bytes 884744 | tf_op jit(solution)/shard_map/ppermute | solution.py:25
  30.2 11.1 %collective-permute-start.4 = (bf16[16,1152]{1,0:T(8,128)(2,1)}, bf16[16,1152]{1,0:T(8,128)(2,1)S(1)}, u32[]{:S(2)}, u32[]{:S(2)}) collective-permute-start(bf16[16,1152]{1,0:T(8,128)(2,1)} %get-tuple-element.36.refs_0_), channel_id=1, source_target_pairs={{0,48},{16,0},{32,16},{48,32},{1,49},{17,1},{33,17},{49,33},{2,50}... | collective-permute-start | bytes 110600 | tf_op jit(solution)/shard_map/ppermute | solution.py:25
  32.1 9.2 %collective-permute-start.3 = (bf16[16,1152]{1,0:T(8,128)(2,1)}, bf16[16,1152]{1,0:T(8,128)(2,1)S(1)}, u32[]{:S(2)}, u32[]{:S(2)}) collective-permute-start(bf16[16,1152]{1,0:T(8,128)(2,1)} %get-tuple-element.36.refs_0_), channel_id=1, source_target_pairs={{0,32},{16,48},{32,0},{48,16},{1,33},{17,49},{33,1},{49,17},{2,34}... | collective-permute-start | bytes 110600 | tf_op jit(solution)/shard_map/ppermute | solution.py:25
  37.0 5.6 %collective-permute-start.2 = (bf16[16,1152]{1,0:T(8,128)(2,1)}, bf16[16,1152]{1,0:T(8,128)(2,1)S(1)}, u32[]{:S(2)}, u32[]{:S(2)}) collective-permute-start(bf16[16,1152]{1,0:T(8,128)(2,1)} %get-tuple-element.36.refs_0_), channel_id=1, source_target_pairs={{0,16},{16,32},{32,48},{48,0},{1,17},{17,33},{33,49},{49,1},{2,18}... | collective-permute-start | bytes 110600 | tf_op jit(solution)/shard_map/ppermute | solution.py:25
  42.7 20.3 %copy-start.6 = (bf16[128,1152]{1,0:T(8,128)(2,1)}, bf16[128,1152]{1,0:T(8,128)(2,1)S(1)}, u32[]{:S(2)}) copy-start(bf16[128,1152]{1,0:T(8,128)(2,1)S(1)} %collective-permute-done.1.refs_2_) | copy-start | bytes 884740
  42.7 20.3 %copy-start.7 = (bf16[128,1152]{1,0:T(8,128)(2,1)}, bf16[128,1152]{1,0:T(8,128)(2,1)S(1)}, u32[]{:S(2)}) copy-start(bf16[128,1152]{1,0:T(8,128)(2,1)S(1)} %collective-permute-done.refs_1_) | copy-start | bytes 884740
  43.6 11.5 %all-to-all-start.1 = ((bf16[4,64,1152]{2,1,0:T(8,128)(2,1)}), bf16[4,64,1152]{2,1,0:T(8,128)(2,1)S(1)}, u32[]{:S(2)}, u32[]{:S(2)}) async-start(bf16[4,64,1152]{2,1,0:T(8,128)(2,1)} %shard_map.84), calls=%async_computation.1 | async-start | bytes 1179648 | tf_op jit(solution)/shard_map/all_to_all | solution.py:32
  47.8 9.4 %collective-permute-start.5 = (bf16[128,1152]{1,0:T(8,128)(2,1)}, bf16[128,1152]{1,0:T(8,128)(2,1)S(1)}, u32[]{:S(2)}, u32[]{:S(2)}) collective-permute-start(bf16[128,1152]{1,0:T(8,128)(2,1)} %get-tuple-element.46.refs_0_), channel_id=1, source_target_pairs={{0,6},{2,0},{4,2},{6,4},{1,7},{3,1},{5,3},{7,5},{8,14},{10,8},{12,... | collective-permute-start | bytes 884744 | tf_op jit(solution)/shard_map/ppermute | solution.py:25
  55.1 0.8 copy-start.4
  57.2 11.9 %copy-start.2 = (f32[16,1152]{1,0:T(8,128)S(1)}, f32[16,1152]{1,0:T(8,128)}, u32[]{:S(2)}) copy-start(f32[16,1152]{1,0:T(8,128)} %get-tuple-element.44.pooled_ref) | copy-start | bytes 221188
  57.2 11.9 %copy-start.5 = (f32[16,128]{1,0:T(8,128)S(1)}, f32[16,128]{1,0:T(8,128)}, u32[]{:S(2)}) copy-start(f32[16,128]{1,0:T(8,128)} %get-tuple-element.45.inverse_ref) | copy-start | bytes 24580
  57.2 5.8 %copy-start.8 = (bf16[128,1152]{1,0:T(8,128)(2,1)}, bf16[128,1152]{1,0:T(8,128)(2,1)S(1)}, u32[]{:S(2)}) copy-start(bf16[128,1152]{1,0:T(8,128)(2,1)S(1)} %collective-permute-done.5.refs_3_) | copy-start | bytes 884740
  57.2 11.9 %all-to-all-start.2 = ((bf16[4,16,1152]{2,1,0:T(8,128)(2,1)}), bf16[4,16,1152]{2,1,0:T(8,128)(2,1)S(1)}, u32[]{:S(2)}, u32[]{:S(2)}) async-start(bf16[4,16,1152]{2,1,0:T(8,128)(2,1)} %shard_map.85), calls=%async_computation.2 | async-start | bytes 294912 | tf_op jit(solution)/shard_map/all_to_all | solution.py:32
  78.5 1.3 copy-start
  79.8 1.0 copy-start.1
  81.4 8.5 %collective-permute-start.6 = (bf16[144,1152]{1,0:T(8,128)(2,1)S(1)}, bf16[144,1152]{1,0:T(8,128)(2,1)S(1)}, u32[]{:S(2)}, u32[]{:S(2)}) collective-permute-start(bf16[144,1152]{1,0:T(8,128)(2,1)S(1)} %get-tuple-element.56), channel_id=1, source_target_pairs={{0,1},{1,0},{2,3},{3,2},{4,5},{5,4},{6,7},{7,6},{8,9},{9,8},{10,11... | collective-permute-start | bytes 995336 | tf_op jit(solution)/shard_map/ppermute | solution.py:268
  90.0 51.0 %collective-permute-start.7 = (bf16[72,1152]{1,0:T(8,128)(2,1)S(1)}, bf16[72,1152]{1,0:T(8,128)(2,1)S(1)}, u32[]{:S(2)}, u32[]{:S(2)}) collective-permute-start(bf16[72,1152]{1,0:T(8,128)(2,1)S(1)} %get-tuple-element.58), channel_id=1, source_target_pairs={{0,8},{8,0},{1,9},{9,1},{2,10},{10,2},{3,11},{11,3},{4,12},{12,4},... | collective-permute-start | bytes 497672 | tf_op jit(solution)/shard_map/ppermute | solution.py:270

commit v7 on v6

--- a/solution.py
+++ b/solution.py
@@ -215,9 +215,7 @@
     )
     units = from_others(unit, "zb")
     by_x = from_others(masked, "x")
-    mine, *early, last = by_x
-    early, units, some_images = lax.optimization_barrier((early, units, some_images))
-    by_x = [mine, *early, last]
+    units, some_images = lax.optimization_barrier((units, some_images))
     (copies,) = local(
         copies_kernel, [((size_of("y"), size_of("za") * rows, width), BF16)], some_images
     )
@@ -231,7 +229,9 @@
         all_images,
         smem=(0, 1),
     )
-    terms, by_x = lax.optimization_barrier((terms, by_x))
+    mine, first, *rest = by_x
+    terms, rest = lax.optimization_barrier((terms, rest))
+    by_x = [mine, first, *rest]
     terms = exchange(terms, "zb")
     slope, columns = local(
         slope_kernel,
@@ -252,7 +252,6 @@
         inverse,
         smem=(0,),
     )
-    share, slope, columns = lax.optimization_barrier((share, slope, columns))
     shares = exchange(share, "x")
     keep, send = local(
         grad_kernel,

time: 143 us -> 140 us (0.979)
  the two profiles are of different devices: /device:TPU:289 before, /device:TPU:457 now
where the time goes in v7:
time: 140 us; the launch traced here: 139 us
  starting transfers between devices  70.3 us (50%)
  waiting for transfers between devices  47.6 us (34%)
  Pallas kernels  15 us (11%)
  local copies, waits for them, and re-layouts  4.48 us (3%)
  between operations  1.44 us (1%)
    ppermute x1, waiting for transfers between devices, on_device(): away = lax.ppermute(far, 'zh', swap)  39.2 us
    all_to_all x4, starting transfers between devices, exchange(): return lax.all_to_all(copies, axes, split_axis=0, concat_axis=0, tiled=True)  30.1 us
    ppermute x6, starting transfers between devices, from_others(): lax.ppermute(value, axis, [(i, (i + k) % count) for i in range(count)])  20.3 us
    pallas_call x9, Pallas kernels, local(): pl.pallas_call(body, grid=(1,), out_shape=[jax.ShapeDtypeStruct(shape, dt...  15 us
    ppermute x1, starting transfers between devices, on_device(): away = lax.ppermute(far, 'zh', swap)  12 us
    ppermute x1, starting transfers between devices, on_device(): away = lax.ppermute(send, 'c', swap)  7.93 us
    ppermute x6, waiting for transfers between devices, from_others(): lax.ppermute(value, axis, [(i, (i + k) % count) for i in range(count)])  7.06 us
    unnamed x20, local copies, waits for them, and re-layouts  4.48 us
  transfers between devices with their start and end apart: 12, of which 6 were waited for; matrix products, arithmetic and copies ran while one was open for 0% of the time, Pallas kernels for 9%

profile of v7, /device:TPU:457, one launch (start us, length us, event | category | flops | bytes accessed | tf_op | source)
XLA Modules:
  0.0 138.9 jit_solution(12894346296718803358)
XLA Ops:
  1.5 16.3 %all-to-all-start = ((bf16[4,16,1152]{2,1,0:T(8,128)(2,1)}), bf16[4,16,1152]{2,1,0:T(8,128)(2,1)S(1)}, u32[]{:S(2)}, u32[]{:S(2)}) async-start(bf16[4,16,1152]{2,1,0:T(8,128)(2,1)} %shard_map.82), calls=%async_computation | async-start | bytes 294912 | tf_op jit(solution)/shard_map/all_to_all | solution.py:32
  17.8 3.7 %shard_map.83 = (bf16[128,1152]{1,0:T(8,128)(2,1)}, bf16[16,1152]{1,0:T(8,128)(2,1)}, f32[16,1152]{1,0:T(8,128)}, f32[16,128]{1,0:T(8,128)}) custom-call(s32[16]{0:T(128)} %count_ref.1, bf16[128,1152]{1,0:T(8,128)(2,1)} %bitcast.3, f32[1152]{0:T(1024)} %gain_ref.1, bf16[1152,1152]{1,0:T(8,128)(2,1)} %weight_ref.3, f32[1152]{0:T(1024)} %bias_ref.3), custom_call_target="tpu_custom_call" | custom-call | flops 339738624 | bytes 2654208 | tf_op jit(solution)/shard_map/pallas_call | solution.py:39
  21.5 2.1 %collective-permute-start.2 = (bf16[16,1152]{1,0:T(8,128)(2,1)}, bf16[16,1152]{1,0:T(8,128)(2,1)S(1)}, u32[]{:S(2)}, u32[]{:S(2)}) collective-permute-start(bf16[16,1152]{1,0:T(8,128)(2,1)} %get-tuple-element.28.refs_0_), channel_id=1, source_target_pairs={{0,48},{16,0},{32,16},{48,32},{1,49},{17,1},{33,17},{49,33},{2,50}... | collective-permute-start | bytes 110600 | tf_op jit(solution)/shard_map/ppermute | solution.py:25
  23.6 5.6 %collective-permute-start.1 = (bf16[16,1152]{1,0:T(8,128)(2,1)}, bf16[16,1152]{1,0:T(8,128)(2,1)S(1)}, u32[]{:S(2)}, u32[]{:S(2)}) collective-permute-start(bf16[16,1152]{1,0:T(8,128)(2,1)} %get-tuple-element.28.refs_0_), channel_id=1, source_target_pairs={{0,32},{16,48},{32,0},{48,16},{1,33},{17,49},{33,1},{49,17},{2,34}... | collective-permute-start | bytes 110600 | tf_op jit(solution)/shard_map/ppermute | solution.py:25
  29.2 1.9 %collective-permute-start = (bf16[16,1152]{1,0:T(8,128)(2,1)}, bf16[16,1152]{1,0:T(8,128)(2,1)S(1)}, u32[]{:S(2)}, u32[]{:S(2)}) collective-permute-start(bf16[16,1152]{1,0:T(8,128)(2,1)} %get-tuple-element.28.refs_0_), channel_id=1, source_target_pairs={{0,16},{16,32},{32,48},{48,0},{1,17},{17,33},{33,49},{49,1},{2,18}... | collective-permute-start | bytes 110600 | tf_op jit(solution)/shard_map/ppermute | solution.py:25
  31.1 0.9 collective-permute-done.1.refs_2_
  32.1 2.0 %collective-permute-done.refs_1_ = bf16[16,1152]{1,0:T(8,128)(2,1)S(1)} collective-permute-done((bf16[16,1152]{1,0:T(8,128)(2,1)}, bf16[16,1152]{1,0:T(8,128)(2,1)S(1)}, u32[]{:S(2)}, u32[]{:S(2)}) %collective-permute-start) | collective-permute-done | bytes 36896 | tf_op jit(solution)/shard_map/ppermute | solution.py:25
  34.1 0.9 shard_map.84
  35.0 4.4 %all-to-all-start.1 = ((bf16[4,64,1152]{2,1,0:T(8,128)(2,1)}), bf16[4,64,1152]{2,1,0:T(8,128)(2,1)S(1)}, u32[]{:S(2)}, u32[]{:S(2)}) async-start(bf16[4,64,1152]{2,1,0:T(8,128)(2,1)} %shard_map.84), calls=%async_computation.1 | async-start | bytes 1179648 | tf_op jit(solution)/shard_map/all_to_all | solution.py:32
  39.3 4.4 %collective-permute-start.4 = (bf16[128,1152]{1,0:T(8,128)(2,1)}, bf16[128,1152]{1,0:T(8,128)(2,1)S(1)}, u32[]{:S(2)}, u32[]{:S(2)}) collective-permute-start(bf16[128,1152]{1,0:T(8,128)(2,1)} %get-tuple-element.33.refs_0_), channel_id=1, source_target_pairs={{0,6},{2,0},{4,2},{6,4},{1,7},{3,1},{5,3},{7,5},{8,14},{10,8},{12,... | collective-permute-start | bytes 884744 | tf_op jit(solution)/shard_map/ppermute | solution.py:25
  43.7 2.4 %collective-permute-start.3 = (bf16[128,1152]{1,0:T(8,128)(2,1)}, bf16[128,1152]{1,0:T(8,128)(2,1)S(1)}, u32[]{:S(2)}, u32[]{:S(2)}) collective-permute-start(bf16[128,1152]{1,0:T(8,128)(2,1)} %get-tuple-element.33.refs_0_), channel_id=1, source_target_pairs={{0,4},{2,6},{4,0},{6,2},{1,5},{3,7},{5,1},{7,3},{8,12},{10,14},{12... | collective-permute-start | bytes 884744 | tf_op jit(solution)/shard_map/ppermute | solution.py:25
  48.2 1.3 shard_map.85
  49.6 3.4 %collective-permute-done.3.refs_2_ = bf16[128,1152]{1,0:T(8,128)(2,1)S(1)} collective-permute-done((bf16[128,1152]{1,0:T(8,128)(2,1)}, bf16[128,1152]{1,0:T(8,128)(2,1)S(1)}, u32[]{:S(2)}, u32[]{:S(2)}) %collective-permute-start.3) | collective-permute-done | bytes 294944 | tf_op jit(solution)/shard_map/ppermute | solution.py:25
  52.9 5.1 %all-to-all-start.2 = ((bf16[4,16,1152]{2,1,0:T(8,128)(2,1)}), bf16[4,16,1152]{2,1,0:T(8,128)(2,1)S(1)}, u32[]{:S(2)}, u32[]{:S(2)}) async-start(bf16[4,16,1152]{2,1,0:T(8,128)(2,1)} %shard_map.85), calls=%async_computation.2 | async-start | bytes 294912 | tf_op jit(solution)/shard_map/all_to_all | solution.py:32
  58.0 3.9 %collective-permute-start.5 = (bf16[128,1152]{1,0:T(8,128)(2,1)S(1)}, bf16[128,1152]{1,0:T(8,128)(2,1)S(1)}, u32[]{:S(2)}, u32[]{:S(2)}) collective-permute-start(bf16[128,1152]{1,0:T(8,128)(2,1)S(1)} %copy-done.6), channel_id=1, source_target_pairs={{0,2},{2,4},{4,6},{6,0},{1,3},{3,5},{5,7},{7,1},{8,10},{10,12},{12... | collective-permute-start | bytes 884744 | tf_op jit(solution)/shard_map/ppermute | solution.py:25
  61.9 0.9 shard_map.86
  62.8 4.4 %all-to-all-start.3 = ((bf16[4,16,1152]{2,1,0:T(8,128)(2,1)}), bf16[4,16,1152]{2,1,0:T(8,128)(2,1)S(1)}, u32[]{:S(2)}, u32[]{:S(2)}) async-start(bf16[4,16,1152]{2,1,0:T(8,128)(2,1)} %shard_map.86), calls=%async_computation.3 | async-start | bytes 294912 | tf_op jit(solution)/shard_map/all_to_all | solution.py:32
  68.7 6.0 %shard_map.87 = (bf16[512,1152]{1,0:T(8,128)(2,1)}, bf16[288,512]{1,0:T(8,128)(2,1)}) custom-call(bf16[1152,1152]{1,0:T(8,128)(2,1)} %weight_ref.3, f32[1152]{0:T(1024)} %bias_ref.3, bf16[128,1152]{1,0:T(8,128)(2,1)} %get-tuple-element.33.refs_0_, bf16[128,1152]{1,0:T(8,128)(2,1)} %copy-done.9, bf16[128,1152]{1,0:T(8,128)(2,1)} %copy-done.8, ...), custom_call_target="tpu_custom_call" | custom-call | flops 1358954496 | bytes 5013504 | tf_op jit(solution)/shard_map/pallas_call | solution.py:39
  74.6 1.3 copy-done
  75.9 1.0 copy-done.1
  77.6 7.9 %collective-permute-start.6 = (bf16[144,1152]{1,0:T(8,128)(2,1)S(1)}, bf16[144,1152]{1,0:T(8,128)(2,1)S(1)}, u32[]{:S(2)}, u32[]{:S(2)}) collective-permute-start(bf16[144,1152]{1,0:T(8,128)(2,1)S(1)} %get-tuple-element.42), channel_id=1, source_target_pairs={{0,1},{1,0},{2,3},{3,2},{4,5},{5,4},{6,7},{7,6},{8,9},{9,8},{10,11... | collective-permute-start | bytes 995336 | tf_op jit(solution)/shard_map/ppermute | solution.py:267
  85.5 1.2 collective-permute-done.6.away_ref
  86.8 12.0 %collective-permute-start.7 = (bf16[72,1152]{1,0:T(8,128)(2,1)S(1)}, bf16[72,1152]{1,0:T(8,128)(2,1)S(1)}, u32[]{:S(2)}, u32[]{:S(2)}) collective-permute-start(bf16[72,1152]{1,0:T(8,128)(2,1)S(1)} %get-tuple-element.44), channel_id=1, source_target_pairs={{0,8},{8,0},{1,9},{9,1},{2,10},{10,2},{3,11},{11,3},{4,12},{12,4},... | collective-permute-start | bytes 497672 | tf_op jit(solution)/shard_map/ppermute | solution.py:269
  98.8 39.2 %collective-permute-done.7.away_ref = bf16[72,1152]{1,0:T(8,128)(2,1)S(1)} collective-permute-done((bf16[72,1152]{1,0:T(8,128)(2,1)S(1)}, bf16[72,1152]{1,0:T(8,128)(2,1)S(1)}, u32[]{:S(2)}, u32[]{:S(2)}) %collective-permute-start.7) | collective-permute-done | bytes 165920 | tf_op jit(solution)/shard_map/ppermute | solution.py:269
  (29 shorter events, 5.3 us)
Async XLA Ops:
  0.0 0.8 copy-start.3
  1.5 32.6 %all-to-all-start = ((bf16[4,16,1152]{2,1,0:T(8,128)(2,1)}), bf16[4,16,1152]{2,1,0:T(8,128)(2,1)S(1)}, u32[]{:S(2)}, u32[]{:S(2)}) async-start(bf16[4,16,1152]{2,1,0:T(8,128)(2,1)} %shard_map.82), calls=%async_computation | async-start | bytes 294912 | tf_op jit(solution)/shard_map/all_to_all | solution.py:32
  21.5 36.5 %copy-start.6 = (bf16[128,1152]{1,0:T(8,128)(2,1)S(1)}, bf16[128,1152]{1,0:T(8,128)(2,1)}, u32[]{:S(2)}) copy-start(bf16[128,1152]{1,0:T(8,128)(2,1)} %get-tuple-element.33.refs_0_) | copy-start | bytes 884740
  21.5 40.4 %copy-start.2 = (f32[16,1152]{1,0:T(8,128)S(1)}, f32[16,1152]{1,0:T(8,128)}, u32[]{:S(2)}) copy-start(f32[16,1152]{1,0:T(8,128)} %get-tuple-element.35.pooled_ref) | copy-start | bytes 221188
  21.5 40.4 %copy-start.5 = (f32[16,128]{1,0:T(8,128)S(1)}, f32[16,128]{1,0:T(8,128)}, u32[]{:S(2)}) copy-start(f32[16,128]{1,0:T(8,128)} %get-tuple-element.36.inverse_ref) | copy-start | bytes 24580
  21.5 9.6 %collective-permute-start.2 = (bf16[16,1152]{1,0:T(8,128)(2,1)}, bf16[16,1152]{1,0:T(8,128)(2,1)S(1)}, u32[]{:S(2)}, u32[]{:S(2)}) collective-permute-start(bf16[16,1152]{1,0:T(8,128)(2,1)} %get-tuple-element.28.refs_0_), channel_id=1, source_target_pairs={{0,48},{16,0},{32,16},{48,32},{1,49},{17,1},{33,17},{49,33},{2,50}... | collective-permute-start | bytes 110600 | tf_op jit(solution)/shard_map/ppermute | solution.py:25
  23.6 8.5 %collective-permute-start.1 = (bf16[16,1152]{1,0:T(8,128)(2,1)}, bf16[16,1152]{1,0:T(8,128)(2,1)S(1)}, u32[]{:S(2)}, u32[]{:S(2)}) collective-permute-start(bf16[16,1152]{1,0:T(8,128)(2,1)} %get-tuple-element.28.refs_0_), channel_id=1, source_target_pairs={{0,32},{16,48},{32,0},{48,16},{1,33},{17,49},{33,1},{49,17},{2,34}... | collective-permute-start | bytes 110600 | tf_op jit(solution)/shard_map/ppermute | solution.py:25
  29.2 4.9 %collective-permute-start = (bf16[16,1152]{1,0:T(8,128)(2,1)}, bf16[16,1152]{1,0:T(8,128)(2,1)S(1)}, u32[]{:S(2)}, u32[]{:S(2)}) collective-permute-start(bf16[16,1152]{1,0:T(8,128)(2,1)} %get-tuple-element.28.refs_0_), channel_id=1, source_target_pairs={{0,16},{16,32},{32,48},{48,0},{1,17},{17,33},{33,49},{49,1},{2,18}... | collective-permute-start | bytes 110600 | tf_op jit(solution)/shard_map/ppermute | solution.py:25
  35.0 12.5 %all-to-all-start.1 = ((bf16[4,64,1152]{2,1,0:T(8,128)(2,1)}), bf16[4,64,1152]{2,1,0:T(8,128)(2,1)S(1)}, u32[]{:S(2)}, u32[]{:S(2)}) async-start(bf16[4,64,1152]{2,1,0:T(8,128)(2,1)} %shard_map.84), calls=%async_computation.1 | async-start | bytes 1179648 | tf_op jit(solution)/shard_map/all_to_all | solution.py:32
  39.3 10.2 %collective-permute-start.4 = (bf16[128,1152]{1,0:T(8,128)(2,1)}, bf16[128,1152]{1,0:T(8,128)(2,1)S(1)}, u32[]{:S(2)}, u32[]{:S(2)}) collective-permute-start(bf16[128,1152]{1,0:T(8,128)(2,1)} %get-tuple-element.33.refs_0_), channel_id=1, source_target_pairs={{0,6},{2,0},{4,2},{6,4},{1,7},{3,1},{5,3},{7,5},{8,14},{10,8},{12,... | collective-permute-start | bytes 884744 | tf_op jit(solution)/shard_map/ppermute | solution.py:25
  43.7 9.2 %collective-permute-start.3 = (bf16[128,1152]{1,0:T(8,128)(2,1)}, bf16[128,1152]{1,0:T(8,128)(2,1)S(1)}, u32[]{:S(2)}, u32[]{:S(2)}) collective-permute-start(bf16[128,1152]{1,0:T(8,128)(2,1)} %get-tuple-element.33.refs_0_), channel_id=1, source_target_pairs={{0,4},{2,6},{4,0},{6,2},{1,5},{3,7},{5,1},{7,3},{8,12},{10,14},{12... | collective-permute-start | bytes 884744 | tf_op jit(solution)/shard_map/ppermute | solution.py:25
  47.5 0.8 copy-start.4
  49.6 18.4 %copy-start.7 = (bf16[128,1152]{1,0:T(8,128)(2,1)}, bf16[128,1152]{1,0:T(8,128)(2,1)S(1)}, u32[]{:S(2)}) copy-start(bf16[128,1152]{1,0:T(8,128)(2,1)S(1)} %collective-permute-done.4.refs_3_) | copy-start | bytes 884740
  52.9 15.0 %copy-start.8 = (bf16[128,1152]{1,0:T(8,128)(2,1)}, bf16[128,1152]{1,0:T(8,128)(2,1)S(1)}, u32[]{:S(2)}) copy-start(bf16[128,1152]{1,0:T(8,128)(2,1)S(1)} %collective-permute-done.3.refs_2_) | copy-start | bytes 884740
  52.9 9.0 %all-to-all-start.2 = ((bf16[4,16,1152]{2,1,0:T(8,128)(2,1)}), bf16[4,16,1152]{2,1,0:T(8,128)(2,1)S(1)}, u32[]{:S(2)}, u32[]{:S(2)}) async-start(bf16[4,16,1152]{2,1,0:T(8,128)(2,1)} %shard_map.85), calls=%async_computation.2 | async-start | bytes 294912 | tf_op jit(solution)/shard_map/all_to_all | solution.py:32
  58.0 9.9 %collective-permute-start.5 = (bf16[128,1152]{1,0:T(8,128)(2,1)S(1)}, bf16[128,1152]{1,0:T(8,128)(2,1)S(1)}, u32[]{:S(2)}, u32[]{:S(2)}) collective-permute-start(bf16[128,1152]{1,0:T(8,128)(2,1)S(1)} %copy-done.6), channel_id=1, source_target_pairs={{0,2},{2,4},{4,6},{6,0},{1,3},{3,5},{5,7},{7,1},{8,10},{10,12},{12... | collective-permute-start | bytes 884744 | tf_op jit(solution)/shard_map/ppermute | solution.py:25
  62.8 11.8 %all-to-all-start.3 = ((bf16[4,16,1152]{2,1,0:T(8,128)(2,1)}), bf16[4,16,1152]{2,1,0:T(8,128)(2,1)S(1)}, u32[]{:S(2)}, u32[]{:S(2)}) async-start(bf16[4,16,1152]{2,1,0:T(8,128)(2,1)} %shard_map.86), calls=%async_computation.3 | async-start | bytes 294912 | tf_op jit(solution)/shard_map/all_to_all | solution.py:32
  67.9 0.7 copy-start.9
  74.6 1.3 copy-start
  75.9 1.0 copy-start.1
  77.6 9.2 %collective-permute-start.6 = (bf16[144,1152]{1,0:T(8,128)(2,1)S(1)}, bf16[144,1152]{1,0:T(8,128)(2,1)S(1)}, u32[]{:S(2)}, u32[]{:S(2)}) collective-permute-start(bf16[144,1152]{1,0:T(8,128)(2,1)S(1)} %get-tuple-element.42), channel_id=1, source_target_pairs={{0,1},{1,0},{2,3},{3,2},{4,5},{5,4},{6,7},{7,6},{8,9},{9,8},{10,11... | collective-permute-start | bytes 995336 | tf_op jit(solution)/shard_map/ppermute | solution.py:267
  86.8 51.3 %collective-permute-start.7 = (bf16[72,1152]{1,0:T(8,128)(2,1)S(1)}, bf16[72,1152]{1,0:T(8,128)(2,1)S(1)}, u32[]{:S(2)}, u32[]{:S(2)}) collective-permute-start(bf16[72,1152]{1,0:T(8,128)(2,1)S(1)} %get-tuple-element.44), channel_id=1, source_target_pairs={{0,8},{8,0},{1,9},{9,1},{2,10},{10,2},{3,11},{11,3},{4,12},{12,4},... | collective-permute-start | bytes 497672 | tf_op jit(solution)/shard_map/ppermute | solution.py:269

commit v8 on v7

--- a/solution.py
+++ b/solution.py
@@ -57,7 +57,7 @@
 
 
 def front_kernel(
-    count_ref, token_ref, gain_ref, weight_ref, bias_ref,
+    count_ref, scale_ref, shift_ref, token_ref, gain_ref, weight_ref, bias_ref,
     masked_ref, unit_ref, pooled_ref, inverse_ref, act_ref,
 ):
     rows, width = pooled_ref.shape
@@ -70,6 +70,9 @@
     pre = jnp.dot(normed, weight_ref[...], preferred_element_type=F32)
     pre = pre + bias_ref[...].reshape(1, width)
     act_ref[...] = 0.5 * pre * (1.0 + jnp.tanh(COEFF * (pre + CUBIC * pre * pre * pre)))
+    lane = lax.broadcasted_iota(jnp.int32, (1, inverse_ref.shape[1]), 1)
+    temper = jnp.exp(jnp.full(lane.shape, scale_ref[0], F32))
+    scalars = jnp.where(lane == 1, temper, shift_ref[0])
     slot = lax.broadcasted_iota(jnp.int32, (length, 1), 0)
     lives = []
     for p in range(rows):
@@ -77,7 +80,7 @@
         inverse = 1.0 / jnp.full((length, 1), count_ref[p], jnp.int32).astype(F32)
         part = act_ref[p * length : (p + 1) * length, :] * (live * inverse)
         pooled_ref[p : p + 1, :] = jnp.sum(part, axis=0, keepdims=True)
-        inverse_ref[p : p + 1, :] = jnp.broadcast_to(inverse[:1], (1, inverse_ref.shape[1]))
+        inverse_ref[p : p + 1, :] = jnp.where(lane == 0, inverse[:1], scalars)
         lives.append(live)
     masked_ref[...] = normed * jnp.concatenate(lives, axis=0).astype(BF16)
     pooled = pooled_ref[...]
@@ -125,15 +128,14 @@
             out_ref[k, j * rows : (j + 1) * rows, :] = image_ref[j]
 
 
-def logit_kernel(scale_ref, shift_ref, *refs):
+def logit_kernel(scalar_ref, *refs):
     *unit_refs, image_ref, out_ref = refs
     near, rows, width = out_ref.shape
     group = rows * size_of("y", "za", "zb")
     units = jnp.concatenate([ref[...] for ref in unit_refs], axis=0)
     images = image_ref[...]
-    temper = jnp.exp(jnp.full((1, 1), scale_ref[0], F32))
     cosine = lax.dot_general(units, images, (((1,), (1,)), ((), ())), preferred_element_type=F32)
-    logit = temper * cosine + shift_ref[0]
+    logit = scalar_ref[:1, 1:2] * cosine + scalar_ref[:1, 2:3]
     unit_at = lax.broadcasted_iota(jnp.int32, cosine.shape, 0)
     image_at = lax.broadcasted_iota(jnp.int32, cosine.shape, 1)
     offset = (lax.axis_index("y") * size_of("za") + lax.axis_index("za")) * rows
@@ -145,15 +147,14 @@
         out_ref[owner] = terms[k * rows : (k + 1) * rows]
 
 
-def share_kernel(scale_ref, term_ref, pooled_ref, inverse_ref, out_ref):
-    temper = jnp.exp(jnp.full((1, 1), scale_ref[0], F32))
+def share_kernel(term_ref, pooled_ref, inverse_ref, out_ref):
     pooled = pooled_ref[...]
     size = jnp.sqrt(jnp.sum(pooled * pooled, axis=-1, keepdims=True) + 1e-06)
     unit = pooled / size
     total = term_ref[0].astype(F32)
     for k in range(1, term_ref.shape[0]):
         total = total + term_ref[k].astype(F32)
-    dunit = temper * total
+    dunit = inverse_ref[:, 1:2] * total
     dpooled = (dunit - unit * jnp.sum(unit * dunit, axis=-1, keepdims=True)) / size
     share = (dpooled * inverse_ref[:, :1]).astype(BF16)
     for k in range(out_ref.shape[0]):
@@ -203,11 +204,13 @@
         front_kernel,
         [((flat, width), BF16), ((rows, width), BF16), ((rows, width), F32), ((rows, 128), F32)],
         token_count,
+        logit_scale,
+        logit_bias,
         tokens.reshape(flat, width),
         norm_gain,
         head_weight,
         head_bias,
-        smem=(0,),
+        smem=(0, 1, 2),
         scratch=[((flat, width), F32)],
         flops=2 * flat * width * width,
         moved=2 * width * width,
@@ -223,15 +226,11 @@
     (terms,) = local(
         logit_kernel,
         [((size_of("zb"), rows, width), BF16)],
-        logit_scale,
-        logit_bias,
+        inverse,
         *units,
         all_images,
-        smem=(0, 1),
-    )
-    mine, first, *rest = by_x
-    terms, rest = lax.optimization_barrier((terms, rest))
-    by_x = [mine, first, *rest]
+    )
+    terms, by_x[-1] = lax.optimization_barrier((terms, by_x[-1]))
     terms = exchange(terms, "zb")
     slope, columns = local(
         slope_kernel,
@@ -246,11 +245,9 @@
     (share,) = local(
         share_kernel,
         [((size_of("x"), rows, width), BF16)],
-        logit_scale,
         terms,
         pooled,
         inverse,
-        smem=(0,),
     )
     shares = exchange(share, "x")
     keep, send = local(

time: 140 us -> 142 us (1.014)
  the two profiles are of different devices: /device:TPU:457 before, /device:TPU:449 now
where the time goes in v8:
time: 142 us; the launch traced here: 141 us
  starting transfers between devices  67.2 us (47%)
  waiting for transfers between devices  52.6 us (37%)
  Pallas kernels  15 us (11%)
  local copies, waits for them, and re-layouts  5.19 us (4%)
  between operations  1.44 us (1%)
    ppermute x1, waiting for transfers between devices, on_device(): away = lax.ppermute(far, 'zh', swap)  39.2 us
    all_to_all x4, starting transfers between devices, exchange(): return lax.all_to_all(copies, axes, split_axis=0, concat_axis=0, tiled=True)  29.2 us
    ppermute x6, starting transfers between devices, from_others(): lax.ppermute(value, axis, [(i, (i + k) % count) for i in range(count)])  20.8 us
    pallas_call x9, Pallas kernels, local(): pl.pallas_call(body, grid=(1,), out_shape=[jax.ShapeDtypeStruct(shape, dt...  15 us
    ppermute x1, starting transfers between devices, on_device(): away = lax.ppermute(far, 'zh', swap)  11.8 us
    ppermute x6, waiting for transfers between devices, from_others(): lax.ppermute(value, axis, [(i, (i + k) % count) for i in range(count)])  9.21 us
    ppermute x1, starting transfers between devices, on_device(): away = lax.ppermute(send, 'c', swap)  5.4 us
    unnamed x22, local copies, waits for them, and re-layouts  5.19 us
  transfers between devices with their start and end apart: 12, of which 5 were waited for; matrix products, arithmetic and copies ran while one was open for 0% of the time, Pallas kernels for 8%

profile of v8, /device:TPU:449, one launch (start us, length us, event | category | flops | bytes accessed | tf_op | source)
XLA Modules:
  0.0 141.5 jit_solution(5226071387764293011)
XLA Ops:
  1.5 16.3 %all-to-all-start = ((bf16[4,16,1152]{2,1,0:T(8,128)(2,1)}), bf16[4,16,1152]{2,1,0:T(8,128)(2,1)S(1)}, u32[]{:S(2)}, u32[]{:S(2)}) async-start(bf16[4,16,1152]{2,1,0:T(8,128)(2,1)} %shard_map.82), calls=%async_computation | async-start | bytes 294912 | tf_op jit(solution)/shard_map/all_to_all | solution.py:32
  19.1 3.7 %shard_map.83 = (bf16[128,1152]{1,0:T(8,128)(2,1)}, bf16[16,1152]{1,0:T(8,128)(2,1)}, f32[16,1152]{1,0:T(8,128)}, f32[16,128]{1,0:T(8,128)}) custom-call(s32[16]{0:T(128)} %count_ref.1, f32[1]{0:T(128)S(6)} %copy.9.scale_ref, f32[1]{0:T(128)S(6)} %copy.10.shift_ref, bf16[128,1152]{1,0:T(8,128)(2,1)} %bitcast.3, f32[1152]{0:T(1024)} %gain_ref.1, ...), custom_call_target="tpu_custom_call" | custom-call | flops 339738624 | bytes 2654208 | tf_op jit(solution)/shard_map/pallas_call | solution.py:39
  22.8 2.1 %collective-permute-start.2 = (bf16[16,1152]{1,0:T(8,128)(2,1)}, bf16[16,1152]{1,0:T(8,128)(2,1)S(1)}, u32[]{:S(2)}, u32[]{:S(2)}) collective-permute-start(bf16[16,1152]{1,0:T(8,128)(2,1)} %get-tuple-element.28.refs_0_), channel_id=1, source_target_pairs={{0,48},{16,0},{32,16},{48,32},{1,49},{17,1},{33,17},{49,33},{2,50}... | collective-permute-start | bytes 110600 | tf_op jit(solution)/shard_map/ppermute | solution.py:25
  24.9 5.6 %collective-permute-start.1 = (bf16[16,1152]{1,0:T(8,128)(2,1)}, bf16[16,1152]{1,0:T(8,128)(2,1)S(1)}, u32[]{:S(2)}, u32[]{:S(2)}) collective-permute-start(bf16[16,1152]{1,0:T(8,128)(2,1)} %get-tuple-element.28.refs_0_), channel_id=1, source_target_pairs={{0,32},{16,48},{32,0},{48,16},{1,33},{17,49},{33,1},{49,17},{2,34}... | collective-permute-start | bytes 110600 | tf_op jit(solution)/shard_map/ppermute | solution.py:25
  30.5 1.9 %collective-permute-start = (bf16[16,1152]{1,0:T(8,128)(2,1)}, bf16[16,1152]{1,0:T(8,128)(2,1)S(1)}, u32[]{:S(2)}, u32[]{:S(2)}) collective-permute-start(bf16[16,1152]{1,0:T(8,128)(2,1)} %get-tuple-element.28.refs_0_), channel_id=1, source_target_pairs={{0,16},{16,32},{32,48},{48,0},{1,17},{17,33},{33,49},{49,1},{2,18}... | collective-permute-start | bytes 110600 | tf_op jit(solution)/shard_map/ppermute | solution.py:25
  32.4 3.0 %collective-permute-done.refs_1_ = bf16[16,1152]{1,0:T(8,128)(2,1)S(1)} collective-permute-done((bf16[16,1152]{1,0:T(8,128)(2,1)}, bf16[16,1152]{1,0:T(8,128)(2,1)S(1)}, u32[]{:S(2)}, u32[]{:S(2)}) %collective-permute-start) | collective-permute-done | bytes 36896 | tf_op jit(solution)/shard_map/ppermute | solution.py:25
  35.4 0.9 shard_map.84
  36.3 4.2 %all-to-all-start.1 = ((bf16[4,64,1152]{2,1,0:T(8,128)(2,1)}), bf16[4,64,1152]{2,1,0:T(8,128)(2,1)S(1)}, u32[]{:S(2)}, u32[]{:S(2)}) async-start(bf16[4,64,1152]{2,1,0:T(8,128)(2,1)} %shard_map.84), calls=%async_computation.1 | async-start | bytes 1179648 | tf_op jit(solution)/shard_map/all_to_all | solution.py:32
  40.5 4.4 %collective-permute-start.3 = (bf16[128,1152]{1,0:T(8,128)(2,1)}, bf16[128,1152]{1,0:T(8,128)(2,1)S(1)}, u32[]{:S(2)}, u32[]{:S(2)}) collective-permute-start(bf16[128,1152]{1,0:T(8,128)(2,1)} %get-tuple-element.33.refs_0_), channel_id=1, source_target_pairs={{0,6},{2,0},{4,2},{6,4},{1,7},{3,1},{5,3},{7,5},{8,14},{10,8},{12,... | collective-permute-start | bytes 884744 | tf_op jit(solution)/shard_map/ppermute | solution.py:25
  44.8 2.9 %all-to-all-done.1 = bf16[4,64,1152]{2,1,0:T(8,128)(2,1)S(1)} async-done(((bf16[4,64,1152]{2,1,0:T(8,128)(2,1)}), bf16[4,64,1152]{2,1,0:T(8,128)(2,1)S(1)}, u32[]{:S(2)}, u32[]{:S(2)}) %all-to-all-start.1) | async-done | bytes 589856 | tf_op jit(solution)/shard_map/all_to_all | solution.py:32
  49.2 1.3 shard_map.85
  50.5 5.1 %all-to-all-start.2 = ((bf16[4,16,1152]{2,1,0:T(8,128)(2,1)}), bf16[4,16,1152]{2,1,0:T(8,128)(2,1)S(1)}, u32[]{:S(2)}, u32[]{:S(2)}) async-start(bf16[4,16,1152]{2,1,0:T(8,128)(2,1)} %shard_map.85), calls=%async_computation.2 | async-start | bytes 294912 | tf_op jit(solution)/shard_map/all_to_all | solution.py:32
  55.6 4.6 %collective-permute-start.5 = (bf16[128,1152]{1,0:T(8,128)(2,1)S(1)}, bf16[128,1152]{1,0:T(8,128)(2,1)S(1)}, u32[]{:S(2)}, u32[]{:S(2)}) collective-permute-start(bf16[128,1152]{1,0:T(8,128)(2,1)S(1)} %copy-done.7), channel_id=1, source_target_pairs={{0,4},{2,6},{4,0},{6,2},{1,5},{3,7},{5,1},{7,3},{8,12},{10,14},{12... | collective-permute-start | bytes 884744 | tf_op jit(solution)/shard_map/ppermute | solution.py:25
  60.3 2.2 %collective-permute-start.4 = (bf16[128,1152]{1,0:T(8,128)(2,1)S(1)}, bf16[128,1152]{1,0:T(8,128)(2,1)S(1)}, u32[]{:S(2)}, u32[]{:S(2)}) collective-permute-start(bf16[128,1152]{1,0:T(8,128)(2,1)S(1)} %copy-done.7), channel_id=1, source_target_pairs={{0,2},{2,4},{4,6},{6,0},{1,3},{3,5},{5,7},{7,1},{8,10},{10,12},{12... | collective-permute-start | bytes 884744 | tf_op jit(solution)/shard_map/ppermute | solution.py:25
  62.6 0.9 shard_map.86
  63.4 3.6 %all-to-all-start.3 = ((bf16[4,16,1152]{2,1,0:T(8,128)(2,1)}), bf16[4,16,1152]{2,1,0:T(8,128)(2,1)S(1)}, u32[]{:S(2)}, u32[]{:S(2)}) async-start(bf16[4,16,1152]{2,1,0:T(8,128)(2,1)} %shard_map.86), calls=%async_computation.3 | async-start | bytes 294912 | tf_op jit(solution)/shard_map/all_to_all | solution.py:32
  67.0 6.2 %collective-permute-done.4.refs_1_ = bf16[128,1152]{1,0:T(8,128)(2,1)S(1)} collective-permute-done((bf16[128,1152]{1,0:T(8,128)(2,1)S(1)}, bf16[128,1152]{1,0:T(8,128)(2,1)S(1)}, u32[]{:S(2)}, u32[]{:S(2)}) %collective-permute-start.4) | collective-permute-done | bytes 294944 | tf_op jit(solution)/shard_map/ppermute | solution.py:25
  74.0 6.0 %shard_map.87 = (bf16[512,1152]{1,0:T(8,128)(2,1)}, bf16[288,512]{1,0:T(8,128)(2,1)}) custom-call(bf16[1152,1152]{1,0:T(8,128)(2,1)} %weight_ref.3, f32[1152]{0:T(1024)} %bias_ref.3, bf16[128,1152]{1,0:T(8,128)(2,1)} %get-tuple-element.33.refs_0_, bf16[128,1152]{1,0:T(8,128)(2,1)} %copy-done.10, bf16[128,1152]{1,0:T(8,128)(2,1)} %copy-done.9, ...), custom_call_target="tpu_custom_call" | custom-call | flops 1358954496 | bytes 5013504 | tf_op jit(solution)/shard_map/pallas_call | solution.py:39
  80.0 1.3 copy-done
  81.3 1.0 copy-done.1
  82.9 5.4 %collective-permute-start.6 = (bf16[144,1152]{1,0:T(8,128)(2,1)S(1)}, bf16[144,1152]{1,0:T(8,128)(2,1)S(1)}, u32[]{:S(2)}, u32[]{:S(2)}) collective-permute-start(bf16[144,1152]{1,0:T(8,128)(2,1)S(1)} %get-tuple-element.40), channel_id=1, source_target_pairs={{0,1},{1,0},{2,3},{3,2},{4,5},{5,4},{6,7},{7,6},{8,9},{9,8},{10,11... | collective-permute-start | bytes 995336 | tf_op jit(solution)/shard_map/ppermute | solution.py:264
  88.3 1.2 collective-permute-done.6.away_ref
  89.7 11.8 %collective-permute-start.7 = (bf16[72,1152]{1,0:T(8,128)(2,1)S(1)}, bf16[72,1152]{1,0:T(8,128)(2,1)S(1)}, u32[]{:S(2)}, u32[]{:S(2)}) collective-permute-start(bf16[72,1152]{1,0:T(8,128)(2,1)S(1)} %get-tuple-element.42), channel_id=1, source_target_pairs={{0,8},{8,0},{1,9},{9,1},{2,10},{10,2},{3,11},{11,3},{4,12},{12,4},... | collective-permute-start | bytes 497672 | tf_op jit(solution)/shard_map/ppermute | solution.py:266
  101.5 39.2 %collective-permute-done.7.away_ref = bf16[72,1152]{1,0:T(8,128)(2,1)S(1)} collective-permute-done((bf16[72,1152]{1,0:T(8,128)(2,1)S(1)}, bf16[72,1152]{1,0:T(8,128)(2,1)S(1)}, u32[]{:S(2)}, u32[]{:S(2)}) %collective-permute-start.7) | collective-permute-done | bytes 165920 | tf_op jit(solution)/shard_map/ppermute | solution.py:266
  (31 shorter events, 5.3 us)
Async XLA Ops:
  0.0 0.8 copy-start.4
  1.5 33.9 %all-to-all-start = ((bf16[4,16,1152]{2,1,0:T(8,128)(2,1)}), bf16[4,16,1152]{2,1,0:T(8,128)(2,1)S(1)}, u32[]{:S(2)}, u32[]{:S(2)}) async-start(bf16[4,16,1152]{2,1,0:T(8,128)(2,1)} %shard_map.82), calls=%async_computation | async-start | bytes 294912 | tf_op jit(solution)/shard_map/all_to_all | solution.py:32
  22.8 32.9 %copy-start.7 = (bf16[128,1152]{1,0:T(8,128)(2,1)S(1)}, bf16[128,1152]{1,0:T(8,128)(2,1)}, u32[]{:S(2)}) copy-start(bf16[128,1152]{1,0:T(8,128)(2,1)} %get-tuple-element.33.refs_0_) | copy-start | bytes 884740
  22.8 39.7 %copy-start.2 = (f32[16,1152]{1,0:T(8,128)S(1)}, f32[16,1152]{1,0:T(8,128)}, u32[]{:S(2)}) copy-start(f32[16,1152]{1,0:T(8,128)} %get-tuple-element.35.pooled_ref) | copy-start | bytes 221188
  22.8 39.7 %copy-start.6 = (f32[16,128]{1,0:T(8,128)S(1)}, f32[16,128]{1,0:T(8,128)}, u32[]{:S(2)}) copy-start(f32[16,128]{1,0:T(8,128)} %get-tuple-element.25.scalar_ref.inverse_ref) | copy-start | bytes 24580
  22.8 9.6 %collective-permute-start.2 = (bf16[16,1152]{1,0:T(8,128)(2,1)}, bf16[16,1152]{1,0:T(8,128)(2,1)S(1)}, u32[]{:S(2)}, u32[]{:S(2)}) collective-permute-start(bf16[16,1152]{1,0:T(8,128)(2,1)} %get-tuple-element.28.refs_0_), channel_id=1, source_target_pairs={{0,48},{16,0},{32,16},{48,32},{1,49},{17,1},{33,17},{49,33},{2,50}... | collective-permute-start | bytes 110600 | tf_op jit(solution)/shard_map/ppermute | solution.py:25
  24.9 7.6 %collective-permute-start.1 = (bf16[16,1152]{1,0:T(8,128)(2,1)}, bf16[16,1152]{1,0:T(8,128)(2,1)S(1)}, u32[]{:S(2)}, u32[]{:S(2)}) collective-permute-start(bf16[16,1152]{1,0:T(8,128)(2,1)} %get-tuple-element.28.refs_0_), channel_id=1, source_target_pairs={{0,32},{16,48},{32,0},{48,16},{1,33},{17,49},{33,1},{49,17},{2,34}... | collective-permute-start | bytes 110600 | tf_op jit(solution)/shard_map/ppermute | solution.py:25
  30.5 4.9 %collective-permute-start = (bf16[16,1152]{1,0:T(8,128)(2,1)}, bf16[16,1152]{1,0:T(8,128)(2,1)S(1)}, u32[]{:S(2)}, u32[]{:S(2)}) collective-permute-start(bf16[16,1152]{1,0:T(8,128)(2,1)} %get-tuple-element.28.refs_0_), channel_id=1, source_target_pairs={{0,16},{16,32},{32,48},{48,0},{1,17},{17,33},{33,49},{49,1},{2,18}... | collective-permute-start | bytes 110600 | tf_op jit(solution)/shard_map/ppermute | solution.py:25
  36.3 11.5 %all-to-all-start.1 = ((bf16[4,64,1152]{2,1,0:T(8,128)(2,1)}), bf16[4,64,1152]{2,1,0:T(8,128)(2,1)S(1)}, u32[]{:S(2)}, u32[]{:S(2)}) async-start(bf16[4,64,1152]{2,1,0:T(8,128)(2,1)} %shard_map.84), calls=%async_computation.1 | async-start | bytes 1179648 | tf_op jit(solution)/shard_map/all_to_all | solution.py:32
  40.5 10.1 %collective-permute-start.3 = (bf16[128,1152]{1,0:T(8,128)(2,1)}, bf16[128,1152]{1,0:T(8,128)(2,1)S(1)}, u32[]{:S(2)}, u32[]{:S(2)}) collective-permute-start(bf16[128,1152]{1,0:T(8,128)(2,1)} %get-tuple-element.33.refs_0_), channel_id=1, source_target_pairs={{0,6},{2,0},{4,2},{6,4},{1,7},{3,1},{5,3},{7,5},{8,14},{10,8},{12,... | collective-permute-start | bytes 884744 | tf_op jit(solution)/shard_map/ppermute | solution.py:25
  47.7 0.8 copy-start.3
  48.5 0.7 copy-start.5
  50.5 22.8 %copy-start.8 = (bf16[128,1152]{1,0:T(8,128)(2,1)}, bf16[128,1152]{1,0:T(8,128)(2,1)S(1)}, u32[]{:S(2)}) copy-start(bf16[128,1152]{1,0:T(8,128)(2,1)S(1)} %collective-permute-done.3.refs_3_) | copy-start | bytes 884740
  50.5 12.0 %all-to-all-start.2 = ((bf16[4,16,1152]{2,1,0:T(8,128)(2,1)}), bf16[4,16,1152]{2,1,0:T(8,128)(2,1)S(1)}, u32[]{:S(2)}, u32[]{:S(2)}) async-start(bf16[4,16,1152]{2,1,0:T(8,128)(2,1)} %shard_map.85), calls=%async_computation.2 | async-start | bytes 294912 | tf_op jit(solution)/shard_map/all_to_all | solution.py:32
  55.6 11.4 %collective-permute-start.5 = (bf16[128,1152]{1,0:T(8,128)(2,1)S(1)}, bf16[128,1152]{1,0:T(8,128)(2,1)S(1)}, u32[]{:S(2)}, u32[]{:S(2)}) collective-permute-start(bf16[128,1152]{1,0:T(8,128)(2,1)S(1)} %copy-done.7), channel_id=1, source_target_pairs={{0,4},{2,6},{4,0},{6,2},{1,5},{3,7},{5,1},{7,3},{8,12},{10,14},{12... | collective-permute-start | bytes 884744 | tf_op jit(solution)/shard_map/ppermute | solution.py:25
  60.3 13.0 %collective-permute-start.4 = (bf16[128,1152]{1,0:T(8,128)(2,1)S(1)}, bf16[128,1152]{1,0:T(8,128)(2,1)S(1)}, u32[]{:S(2)}, u32[]{:S(2)}) collective-permute-start(bf16[128,1152]{1,0:T(8,128)(2,1)S(1)} %copy-done.7), channel_id=1, source_target_pairs={{0,2},{2,4},{4,6},{6,0},{1,3},{3,5},{5,7},{7,1},{8,10},{10,12},{12... | collective-permute-start | bytes 884744 | tf_op jit(solution)/shard_map/ppermute | solution.py:25
  63.4 16.6 %all-to-all-start.3 = ((bf16[4,16,1152]{2,1,0:T(8,128)(2,1)}), bf16[4,16,1152]{2,1,0:T(8,128)(2,1)S(1)}, u32[]{:S(2)}, u32[]{:S(2)}) async-start(bf16[4,16,1152]{2,1,0:T(8,128)(2,1)} %shard_map.86), calls=%async_computation.3 | async-start | bytes 294912 | tf_op jit(solution)/shard_map/all_to_all | solution.py:32
  67.0 6.2 %copy-start.9 = (bf16[128,1152]{1,0:T(8,128)(2,1)}, bf16[128,1152]{1,0:T(8,128)(2,1)S(1)}, u32[]{:S(2)}) copy-start(bf16[128,1152]{1,0:T(8,128)(2,1)S(1)} %collective-permute-done.5.refs_2_) | copy-start | bytes 884740
  73.3 0.7 copy-start.10
  80.0 1.3 copy-start
  81.3 1.0 copy-start.1
  82.9 6.6 %collective-permute-start.6 = (bf16[144,1152]{1,0:T(8,128)(2,1)S(1)}, bf16[144,1152]{1,0:T(8,128)(2,1)S(1)}, u32[]{:S(2)}, u32[]{:S(2)}) collective-permute-start(bf16[144,1152]{1,0:T(8,128)(2,1)S(1)} %get-tuple-element.40), channel_id=1, source_target_pairs={{0,1},{1,0},{2,3},{3,2},{4,5},{5,4},{6,7},{7,6},{8,9},{9,8},{10,11... | collective-permute-start | bytes 995336 | tf_op jit(solution)/shard_map/ppermute | solution.py:264
  89.7 51.0 %collective-permute-start.7 = (bf16[72,1152]{1,0:T(8,128)(2,1)S(1)}, bf16[72,1152]{1,0:T(8,128)(2,1)S(1)}, u32[]{:S(2)}, u32[]{:S(2)}) collective-permute-start(bf16[72,1152]{1,0:T(8,128)(2,1)S(1)} %get-tuple-element.42), channel_id=1, source_target_pairs={{0,8},{8,0},{1,9},{9,1},{2,10},{10,2},{3,11},{11,3},{4,12},{12,4},... | collective-permute-start | bytes 497672 | tf_op jit(solution)/shard_map/ppermute | solution.py:266

commit v9 on v7

--- a/solution.py
+++ b/solution.py
@@ -215,7 +215,8 @@
     )
     units = from_others(unit, "zb")
     by_x = from_others(masked, "x")
-    units, some_images = lax.optimization_barrier((units, some_images))
+    mine, *middle, last = by_x
+    last, units, some_images = lax.optimization_barrier((last, units, some_images))
     (copies,) = local(
         copies_kernel, [((size_of("y"), size_of("za") * rows, width), BF16)], some_images
     )
@@ -229,9 +230,8 @@
         all_images,
         smem=(0, 1),
     )
-    mine, first, *rest = by_x
-    terms, rest = lax.optimization_barrier((terms, rest))
-    by_x = [mine, first, *rest]
+    terms, middle[1:], last = lax.optimization_barrier((terms, middle[1:], last))
+    by_x = [mine, *middle, last]
     terms = exchange(terms, "zb")
     slope, columns = local(
         slope_kernel,

time: 140 us -> 142 us (1.014)
  the two profiles are of different devices: /device:TPU:457 before, /device:TPU:296 now
where the time goes in v9:
time: 142 us; the launch traced here: 141 us
  starting transfers between devices  68.4 us (48%)
  waiting for transfers between devices  51.3 us (36%)
  Pallas kernels  15.1 us (11%)
  local copies, waits for them, and re-layouts  4.49 us (3%)
  between operations  1.42 us (1%)
    ppermute x1, waiting for transfers between devices, on_device(): away = lax.ppermute(far, 'zh', swap)  39 us
    all_to_all x4, starting transfers between devices, exchange(): return lax.all_to_all(copies, axes, split_axis=0, concat_axis=0, tiled=True)  32.7 us
    ppermute x6, starting transfers between devices, from_others(): lax.ppermute(value, axis, [(i, (i + k) % count) for i in range(count)])  21.3 us
    pallas_call x9, Pallas kernels, local(): pl.pallas_call(body, grid=(1,), out_shape=[jax.ShapeDtypeStruct(shape, dt...  15.1 us
    ppermute x1, starting transfers between devices, on_device(): away = lax.ppermute(far, 'zh', swap)  12.4 us
    all_to_all x4, waiting for transfers between devices, exchange(): return lax.all_to_all(copies, axes, split_axis=0, concat_axis=0, tiled=True)  6.36 us
    unnamed x20, local copies, waits for them, and re-layouts  4.49 us
    ppermute x6, waiting for transfers between devices, from_others(): lax.ppermute(value, axis, [(i, (i + k) % count) for i in range(count)])  4.28 us
  transfers between devices with their start and end apart: 12, of which 7 were waited for; matrix products, arithmetic and copies ran while one was open for 0% of the time, Pallas kernels for 8%

profile of v9, /device:TPU:296, one launch (start us, length us, event | category | flops | bytes accessed | tf_op | source)
XLA Modules:
  0.0 140.7 jit_solution(4291208558715152907)
XLA Ops:
  1.5 18.6 %all-to-all-start = ((bf16[4,16,1152]{2,1,0:T(8,128)(2,1)}), bf16[4,16,1152]{2,1,0:T(8,128)(2,1)S(1)}, u32[]{:S(2)}, u32[]{:S(2)}) async-start(bf16[4,16,1152]{2,1,0:T(8,128)(2,1)} %shard_map.82), calls=%async_computation | async-start | bytes 294912 | tf_op jit(solution)/shard_map/all_to_all | solution.py:32
  20.2 3.7 %shard_map.83 = (bf16[128,1152]{1,0:T(8,128)(2,1)}, bf16[16,1152]{1,0:T(8,128)(2,1)}, f32[16,1152]{1,0:T(8,128)}, f32[16,128]{1,0:T(8,128)}) custom-call(s32[16]{0:T(128)} %count_ref.1, bf16[128,1152]{1,0:T(8,128)(2,1)} %bitcast.3, f32[1152]{0:T(1024)} %gain_ref.1, bf16[1152,1152]{1,0:T(8,128)(2,1)} %weight_ref.3, f32[1152]{0:T(1024)} %bias_ref.3), custom_call_target="tpu_custom_call" | custom-call | flops 339738624 | bytes 2654208 | tf_op jit(solution)/shard_map/pallas_call | solution.py:39
  23.9 4.8 %collective-permute-start = (bf16[128,1152]{1,0:T(8,128)(2,1)}, bf16[128,1152]{1,0:T(8,128)(2,1)S(1)}, u32[]{:S(2)}, u32[]{:S(2)}) collective-permute-start(bf16[128,1152]{1,0:T(8,128)(2,1)} %get-tuple-element.27.refs_0_), channel_id=1, source_target_pairs={{0,6},{2,0},{4,2},{6,4},{1,7},{3,1},{5,3},{7,5},{8,14},{10,8},{12,... | collective-permute-start | bytes 884744 | tf_op jit(solution)/shard_map/ppermute | solution.py:25
  28.7 2.0 %collective-permute-start.3 = (bf16[16,1152]{1,0:T(8,128)(2,1)}, bf16[16,1152]{1,0:T(8,128)(2,1)S(1)}, u32[]{:S(2)}, u32[]{:S(2)}) collective-permute-start(bf16[16,1152]{1,0:T(8,128)(2,1)} %get-tuple-element.30.refs_0_), channel_id=1, source_target_pairs={{0,48},{16,0},{32,16},{48,32},{1,49},{17,1},{33,17},{49,33},{2,50}... | collective-permute-start | bytes 110600 | tf_op jit(solution)/shard_map/ppermute | solution.py:25
  30.7 5.2 %collective-permute-start.2 = (bf16[16,1152]{1,0:T(8,128)(2,1)}, bf16[16,1152]{1,0:T(8,128)(2,1)S(1)}, u32[]{:S(2)}, u32[]{:S(2)}) collective-permute-start(bf16[16,1152]{1,0:T(8,128)(2,1)} %get-tuple-element.30.refs_0_), channel_id=1, source_target_pairs={{0,32},{16,48},{32,0},{48,16},{1,33},{17,49},{33,1},{49,17},{2,34}... | collective-permute-start | bytes 110600 | tf_op jit(solution)/shard_map/ppermute | solution.py:25
  35.9 4.7 %collective-permute-start.1 = (bf16[16,1152]{1,0:T(8,128)(2,1)}, bf16[16,1152]{1,0:T(8,128)(2,1)S(1)}, u32[]{:S(2)}, u32[]{:S(2)}) collective-permute-start(bf16[16,1152]{1,0:T(8,128)(2,1)} %get-tuple-element.30.refs_0_), channel_id=1, source_target_pairs={{0,16},{16,32},{32,48},{48,0},{1,17},{17,33},{33,49},{49,1},{2,18}... | collective-permute-start | bytes 110600 | tf_op jit(solution)/shard_map/ppermute | solution.py:25
  40.7 1.9 %collective-permute-done.1.refs_1_ = bf16[16,1152]{1,0:T(8,128)(2,1)S(1)} collective-permute-done((bf16[16,1152]{1,0:T(8,128)(2,1)}, bf16[16,1152]{1,0:T(8,128)(2,1)S(1)}, u32[]{:S(2)}, u32[]{:S(2)}) %collective-permute-start.1) | collective-permute-done | bytes 36896 | tf_op jit(solution)/shard_map/ppermute | solution.py:25
  43.5 4.9 %all-to-all-start.1 = ((bf16[4,64,1152]{2,1,0:T(8,128)(2,1)}), bf16[4,64,1152]{2,1,0:T(8,128)(2,1)S(1)}, u32[]{:S(2)}, u32[]{:S(2)}) async-start(bf16[4,64,1152]{2,1,0:T(8,128)(2,1)} %shard_map.84), calls=%async_computation.1 | async-start | bytes 1179648 | tf_op jit(solution)/shard_map/all_to_all | solution.py:32
  48.4 2.7 %collective-permute-start.4 = (bf16[128,1152]{1,0:T(8,128)(2,1)}, bf16[128,1152]{1,0:T(8,128)(2,1)S(1)}, u32[]{:S(2)}, u32[]{:S(2)}) collective-permute-start(bf16[128,1152]{1,0:T(8,128)(2,1)} %get-tuple-element.27.refs_0_), channel_id=1, source_target_pairs={{0,4},{2,6},{4,0},{6,2},{1,5},{3,7},{5,1},{7,3},{8,12},{10,14},{12... | collective-permute-start | bytes 884744 | tf_op jit(solution)/shard_map/ppermute | solution.py:25
  52.4 3.0 %all-to-all-done.1 = bf16[4,64,1152]{2,1,0:T(8,128)(2,1)S(1)} async-done(((bf16[4,64,1152]{2,1,0:T(8,128)(2,1)}), bf16[4,64,1152]{2,1,0:T(8,128)(2,1)S(1)}, u32[]{:S(2)}, u32[]{:S(2)}) %all-to-all-start.1) | async-done | bytes 589856 | tf_op jit(solution)/shard_map/all_to_all | solution.py:32
  56.2 1.3 shard_map.85
  57.5 1.3 collective-permute-done.4.refs_2_
  58.8 5.9 %all-to-all-start.2 = ((bf16[4,16,1152]{2,1,0:T(8,128)(2,1)}), bf16[4,16,1152]{2,1,0:T(8,128)(2,1)S(1)}, u32[]{:S(2)}, u32[]{:S(2)}) async-start(bf16[4,16,1152]{2,1,0:T(8,128)(2,1)} %shard_map.85), calls=%async_computation.2 | async-start | bytes 294912 | tf_op jit(solution)/shard_map/all_to_all | solution.py:32
  64.6 1.9 %collective-permute-start.5 = (bf16[128,1152]{1,0:T(8,128)(2,1)S(1)}, bf16[128,1152]{1,0:T(8,128)(2,1)S(1)}, u32[]{:S(2)}, u32[]{:S(2)}) collective-permute-start(bf16[128,1152]{1,0:T(8,128)(2,1)S(1)} %copy-done.6), channel_id=1, source_target_pairs={{0,2},{2,4},{4,6},{6,0},{1,3},{3,5},{5,7},{7,1},{8,10},{10,12},{12... | collective-permute-start | bytes 884744 | tf_op jit(solution)/shard_map/ppermute | solution.py:25
  66.5 3.4 %all-to-all-done.2.term_ref = bf16[4,16,1152]{2,1,0:T(8,128)(2,1)S(1)} async-done(((bf16[4,16,1152]{2,1,0:T(8,128)(2,1)}), bf16[4,16,1152]{2,1,0:T(8,128)(2,1)S(1)}, u32[]{:S(2)}, u32[]{:S(2)}) %all-to-all-start.2) | async-done | bytes 147488 | tf_op jit(solution)/shard_map/all_to_all | solution.py:32
  70.8 3.3 %all-to-all-start.3 = ((bf16[4,16,1152]{2,1,0:T(8,128)(2,1)}), bf16[4,16,1152]{2,1,0:T(8,128)(2,1)S(1)}, u32[]{:S(2)}, u32[]{:S(2)}) async-start(bf16[4,16,1152]{2,1,0:T(8,128)(2,1)} %shard_map.86), calls=%async_computation.3 | async-start | bytes 294912 | tf_op jit(solution)/shard_map/all_to_all | solution.py:32
  74.1 1.1 collective-permute-done.5.refs_1_
  75.9 6.0 %shard_map.87 = (bf16[512,1152]{1,0:T(8,128)(2,1)}, bf16[288,512]{1,0:T(8,128)(2,1)}) custom-call(bf16[1152,1152]{1,0:T(8,128)(2,1)} %weight_ref.3, f32[1152]{0:T(1024)} %bias_ref.3, bf16[128,1152]{1,0:T(8,128)(2,1)} %get-tuple-element.27.refs_0_, bf16[128,1152]{1,0:T(8,128)(2,1)} %copy-done.9, bf16[128,1152]{1,0:T(8,128)(2,1)} %copy-done.8, ...), custom_call_target="tpu_custom_call" | custom-call | flops 1358954496 | bytes 5013504 | tf_op jit(solution)/shard_map/pallas_call | solution.py:39
  81.9 1.3 copy-done
  83.2 1.0 copy-done.1
  84.8 1.9 %collective-permute-start.6 = (bf16[144,1152]{1,0:T(8,128)(2,1)S(1)}, bf16[144,1152]{1,0:T(8,128)(2,1)S(1)}, u32[]{:S(2)}, u32[]{:S(2)}) collective-permute-start(bf16[144,1152]{1,0:T(8,128)(2,1)S(1)} %get-tuple-element.44), channel_id=1, source_target_pairs={{0,1},{1,0},{2,3},{3,2},{4,5},{5,4},{6,7},{7,6},{8,9},{9,8},{10,11... | collective-permute-start | bytes 995336 | tf_op jit(solution)/shard_map/ppermute | solution.py:267
  86.8 1.6 %collective-permute-done.6.away_ref = bf16[144,1152]{1,0:T(8,128)(2,1)S(1)} collective-permute-done((bf16[144,1152]{1,0:T(8,128)(2,1)S(1)}, bf16[144,1152]{1,0:T(8,128)(2,1)S(1)}, u32[]{:S(2)}, u32[]{:S(2)}) %collective-permute-start.6) | collective-permute-done | bytes 331808 | tf_op jit(solution)/shard_map/ppermute | solution.py:267
  88.5 12.4 %collective-permute-start.7 = (bf16[72,1152]{1,0:T(8,128)(2,1)S(1)}, bf16[72,1152]{1,0:T(8,128)(2,1)S(1)}, u32[]{:S(2)}, u32[]{:S(2)}) collective-permute-start(bf16[72,1152]{1,0:T(8,128)(2,1)S(1)} %get-tuple-element.46), channel_id=1, source_target_pairs={{0,8},{8,0},{1,9},{9,1},{2,10},{10,2},{3,11},{11,3},{4,12},{12,4},... | collective-permute-start | bytes 497672 | tf_op jit(solution)/shard_map/ppermute | solution.py:269
  100.9 39.0 %collective-permute-done.7.away_ref = bf16[72,1152]{1,0:T(8,128)(2,1)S(1)} collective-permute-done((bf16[72,1152]{1,0:T(8,128)(2,1)S(1)}, bf16[72,1152]{1,0:T(8,128)(2,1)S(1)}, u32[]{:S(2)}, u32[]{:S(2)}) %collective-permute-start.7) | collective-permute-done | bytes 165920 | tf_op jit(solution)/shard_map/ppermute | solution.py:269
  (29 shorter events, 6.4 us)
Async XLA Ops:
  0.0 0.8 copy-start.3
  1.5 41.1 %all-to-all-start = ((bf16[4,16,1152]{2,1,0:T(8,128)(2,1)}), bf16[4,16,1152]{2,1,0:T(8,128)(2,1)S(1)}, u32[]{:S(2)}, u32[]{:S(2)}) async-start(bf16[4,16,1152]{2,1,0:T(8,128)(2,1)} %shard_map.82), calls=%async_computation | async-start | bytes 294912 | tf_op jit(solution)/shard_map/all_to_all | solution.py:32
  23.9 40.7 %copy-start.6 = (bf16[128,1152]{1,0:T(8,128)(2,1)S(1)}, bf16[128,1152]{1,0:T(8,128)(2,1)}, u32[]{:S(2)}) copy-start(bf16[128,1152]{1,0:T(8,128)(2,1)} %get-tuple-element.27.refs_0_) | copy-start | bytes 884740
  23.9 46.0 %copy-start.2 = (f32[16,1152]{1,0:T(8,128)S(1)}, f32[16,1152]{1,0:T(8,128)}, u32[]{:S(2)}) copy-start(f32[16,1152]{1,0:T(8,128)} %get-tuple-element.37.pooled_ref) | copy-start | bytes 221188
  23.9 46.0 %copy-start.5 = (f32[16,128]{1,0:T(8,128)S(1)}, f32[16,128]{1,0:T(8,128)}, u32[]{:S(2)}) copy-start(f32[16,128]{1,0:T(8,128)} %get-tuple-element.38.inverse_ref) | copy-start | bytes 24580
  23.9 18.7 %collective-permute-start = (bf16[128,1152]{1,0:T(8,128)(2,1)}, bf16[128,1152]{1,0:T(8,128)(2,1)S(1)}, u32[]{:S(2)}, u32[]{:S(2)}) collective-permute-start(bf16[128,1152]{1,0:T(8,128)(2,1)} %get-tuple-element.27.refs_0_), channel_id=1, source_target_pairs={{0,6},{2,0},{4,2},{6,4},{1,7},{3,1},{5,3},{7,5},{8,14},{10,8},{12,... | collective-permute-start | bytes 884744 | tf_op jit(solution)/shard_map/ppermute | solution.py:25
  28.7 12.0 %collective-permute-start.3 = (bf16[16,1152]{1,0:T(8,128)(2,1)}, bf16[16,1152]{1,0:T(8,128)(2,1)S(1)}, u32[]{:S(2)}, u32[]{:S(2)}) collective-permute-start(bf16[16,1152]{1,0:T(8,128)(2,1)} %get-tuple-element.30.refs_0_), channel_id=1, source_target_pairs={{0,48},{16,0},{32,16},{48,32},{1,49},{17,1},{33,17},{49,33},{2,50}... | collective-permute-start | bytes 110600 | tf_op jit(solution)/shard_map/ppermute | solution.py:25
  30.7 9.9 %collective-permute-start.2 = (bf16[16,1152]{1,0:T(8,128)(2,1)}, bf16[16,1152]{1,0:T(8,128)(2,1)S(1)}, u32[]{:S(2)}, u32[]{:S(2)}) collective-permute-start(bf16[16,1152]{1,0:T(8,128)(2,1)} %get-tuple-element.30.refs_0_), channel_id=1, source_target_pairs={{0,32},{16,48},{32,0},{48,16},{1,33},{17,49},{33,1},{49,17},{2,34}... | collective-permute-start | bytes 110600 | tf_op jit(solution)/shard_map/ppermute | solution.py:25
  35.9 6.7 %collective-permute-start.1 = (bf16[16,1152]{1,0:T(8,128)(2,1)}, bf16[16,1152]{1,0:T(8,128)(2,1)S(1)}, u32[]{:S(2)}, u32[]{:S(2)}) collective-permute-start(bf16[16,1152]{1,0:T(8,128)(2,1)} %get-tuple-element.30.refs_0_), channel_id=1, source_target_pairs={{0,16},{16,32},{32,48},{48,0},{1,17},{17,33},{33,49},{49,1},{2,18}... | collective-permute-start | bytes 110600 | tf_op jit(solution)/shard_map/ppermute | solution.py:25
  42.6 32.6 %copy-start.7 = (bf16[128,1152]{1,0:T(8,128)(2,1)}, bf16[128,1152]{1,0:T(8,128)(2,1)S(1)}, u32[]{:S(2)}) copy-start(bf16[128,1152]{1,0:T(8,128)(2,1)S(1)} %collective-permute-done.refs_3_) | copy-start | bytes 884740
  43.5 11.9 %all-to-all-start.1 = ((bf16[4,64,1152]{2,1,0:T(8,128)(2,1)}), bf16[4,64,1152]{2,1,0:T(8,128)(2,1)S(1)}, u32[]{:S(2)}, u32[]{:S(2)}) async-start(bf16[4,64,1152]{2,1,0:T(8,128)(2,1)} %shard_map.84), calls=%async_computation.1 | async-start | bytes 1179648 | tf_op jit(solution)/shard_map/all_to_all | solution.py:32
  48.4 10.3 %collective-permute-start.4 = (bf16[128,1152]{1,0:T(8,128)(2,1)}, bf16[128,1152]{1,0:T(8,128)(2,1)S(1)}, u32[]{:S(2)}, u32[]{:S(2)}) collective-permute-start(bf16[128,1152]{1,0:T(8,128)(2,1)} %get-tuple-element.27.refs_0_), channel_id=1, source_target_pairs={{0,4},{2,6},{4,0},{6,2},{1,5},{3,7},{5,1},{7,3},{8,12},{10,14},{12... | collective-permute-start | bytes 884744 | tf_op jit(solution)/shard_map/ppermute | solution.py:25
  55.4 0.8 copy-start.4
  58.8 16.5 %copy-start.8 = (bf16[128,1152]{1,0:T(8,128)(2,1)}, bf16[128,1152]{1,0:T(8,128)(2,1)S(1)}, u32[]{:S(2)}) copy-start(bf16[128,1152]{1,0:T(8,128)(2,1)S(1)} %collective-permute-done.4.refs_2_) | copy-start | bytes 884740
  58.8 11.2 %all-to-all-start.2 = ((bf16[4,16,1152]{2,1,0:T(8,128)(2,1)}), bf16[4,16,1152]{2,1,0:T(8,128)(2,1)S(1)}, u32[]{:S(2)}, u32[]{:S(2)}) async-start(bf16[4,16,1152]{2,1,0:T(8,128)(2,1)} %shard_map.85), calls=%async_computation.2 | async-start | bytes 294912 | tf_op jit(solution)/shard_map/all_to_all | solution.py:32
  64.6 10.6 %collective-permute-start.5 = (bf16[128,1152]{1,0:T(8,128)(2,1)S(1)}, bf16[128,1152]{1,0:T(8,128)(2,1)S(1)}, u32[]{:S(2)}, u32[]{:S(2)}) collective-permute-start(bf16[128,1152]{1,0:T(8,128)(2,1)S(1)} %copy-done.6), channel_id=1, source_target_pairs={{0,2},{2,4},{4,6},{6,0},{1,3},{3,5},{5,7},{7,1},{8,10},{10,12},{12... | collective-permute-start | bytes 884744 | tf_op jit(solution)/shard_map/ppermute | solution.py:25
  70.8 11.1 %all-to-all-start.3 = ((bf16[4,16,1152]{2,1,0:T(8,128)(2,1)}), bf16[4,16,1152]{2,1,0:T(8,128)(2,1)S(1)}, u32[]{:S(2)}, u32[]{:S(2)}) async-start(bf16[4,16,1152]{2,1,0:T(8,128)(2,1)} %shard_map.86), calls=%async_computation.3 | async-start | bytes 294912 | tf_op jit(solution)/shard_map/all_to_all | solution.py:32
  75.2 0.7 copy-start.9
  81.9 1.3 copy-start
  83.2 1.0 copy-start.1
  84.8 3.5 %collective-permute-start.6 = (bf16[144,1152]{1,0:T(8,128)(2,1)S(1)}, bf16[144,1152]{1,0:T(8,128)(2,1)S(1)}, u32[]{:S(2)}, u32[]{:S(2)}) collective-permute-start(bf16[144,1152]{1,0:T(8,128)(2,1)S(1)} %get-tuple-element.44), channel_id=1, source_target_pairs={{0,1},{1,0},{2,3},{3,2},{4,5},{5,4},{6,7},{7,6},{8,9},{9,8},{10,11... | collective-permute-start | bytes 995336 | tf_op jit(solution)/shard_map/ppermute | solution.py:267
  88.5 51.4 %collective-permute-start.7 = (bf16[72,1152]{1,0:T(8,128)(2,1)S(1)}, bf16[72,1152]{1,0:T(8,128)(2,1)S(1)}, u32[]{:S(2)}, u32[]{:S(2)}) collective-permute-start(bf16[72,1152]{1,0:T(8,128)(2,1)S(1)} %get-tuple-element.46), channel_id=1, source_target_pairs={{0,8},{8,0},{1,9},{9,1},{2,10},{10,2},{3,11},{11,3},{4,12},{12,4},... | collective-permute-start | bytes 497672 | tf_op jit(solution)/shard_map/ppermute | solution.py:269
